TPU v7x, 32 devices: a whole 2x2x4 slice. The times are simulated.
32 devices in a mesh: grp: 2 (over x), row: 16 (over z, y, core).
Axes of the slice: x: 2, y: 2, z: 4, core: 2. Of those that a mesh axis runs over, the one named last changes fastest.
Arguments:
- tokens: bfloat16 [4096, 3072], P(('grp', 'row')), parts along dimension 0, may hold values from -6 to 6
- cotangent: bfloat16 [4096, 3072], P(('grp', 'row')), parts along dimension 0, may hold values from -6 to 6
- w1_blocks: bfloat16 [16, 128, 128], P('row'), may hold values from -0.5 to 0.5
- w1_rows: int32 [16], replicated, may hold values from 0 to 23
- w1_cols: int32 [16], replicated, may hold values from 0 to 95
- w2_blocks: bfloat16 [16, 128, 128], P('row'), may hold values from -0.5 to 0.5
- w2_rows: int32 [16], replicated, may hold values from 0 to 95
- w2_cols: int32 [16], replicated, may hold values from 0 to 23
Outputs:
- output: bfloat16 [4096, 3072], P(('grp', 'row')), parts along dimension 0
- input_grad: bfloat16 [4096, 3072], P(('grp', 'row')), parts along dimension 0
- w1_grad: float32 [32, 128, 128], P(('grp', 'row')), parts along dimension 0
- w2_grad: float32 [32, 128, 128], P(('grp', 'row')), parts along dimension 0
There are 2 independent parts, one for each index of `grp`. A program takes and returns all parts, laid end to end along the dimension named above; an argument that names none is the same for every part. Nothing has to cross between parts.
All inputs are finite; a program needn't handle non-finite values.
Results may differ from a plain program's by a relative error of at most 0.005.
Values may be sent and summed in bfloat16 or wider, within the bound.
No kernel may reach another device: no remote copies, remote signals or barrier semaphores. Data moves between devices by JAX's collectives and lax.ppermute only.
A program may use at most 128 MiB of HBM per device.

v0:
```python
import math

import jax
import jax.numpy as jnp
from jax import lax
from jax.sharding import PartitionSpec as P

D = 3072
BS = 128
DB = 24
FB = 96


def gelu_tanh(value):
    return jax.nn.gelu(value, approximate=True)


def body(tokens, cotangent, w1_blocks, w1_rows, w1_cols, w2_blocks, w2_rows, w2_cols):
    width = tokens.shape[0]
    token_rows = tokens.reshape(width, DB, BS)
    cot_rows = cotangent.reshape(width, DB, BS)
    empty_hidden = jnp.zeros((FB, width, BS), jnp.float32)
    empty_model = jnp.zeros((width, DB, BS), jnp.float32)
    rows_here = w1_rows
    cols_here = w1_cols
    product = jnp.einsum(
        "tnk,nkj->ntj",
        token_rows[:, rows_here],
        lax.all_gather(w1_blocks, "row", axis=0, tiled=True),
        preferred_element_type=jnp.float32,
    )
    hidden = empty_hidden.at[cols_here].add(product)
    act = gelu_tanh(hidden).astype(jnp.bfloat16)
    piece = lax.all_gather(w2_blocks, "row", axis=0, tiled=True)
    rows_here = w2_rows
    cols_here = w2_cols
    forward = jnp.einsum("ntk,nkj->tnj", act[rows_here], piece, preferred_element_type=jnp.float32)
    backward = jnp.einsum(
        "tnj,nkj->ntk", cot_rows[:, cols_here], piece, preferred_element_type=jnp.float32
    )
    output_acc = empty_model.at[:, cols_here].add(forward)
    act_grad = empty_hidden.at[rows_here].add(backward)
    output = output_acc.reshape(width, D).astype(jnp.bfloat16)
    hidden_grad = jax.vjp(gelu_tanh, hidden)[1](act_grad)[0].astype(jnp.bfloat16)
    rows_here = w1_rows
    cols_here = w1_cols
    product = jnp.einsum(
        "ntj,nkj->tnk",
        hidden_grad[cols_here],
        lax.all_gather(w1_blocks, "row", axis=0, tiled=True),
        preferred_element_type=jnp.float32,
    )
    input_acc = empty_model.at[:, rows_here].add(product)
    input_grad = input_acc.reshape(width, D).astype(jnp.bfloat16)
    scale = 1.0 / math.sqrt(width * lax.axis_size("row"))
    rows_here = w2_rows
    cols_here = w2_cols
    second_grad = (
        lax.psum_scatter(
            jnp.einsum(
                "ntk,tnj->nkj",
                act[rows_here],
                cot_rows[:, cols_here],
                preferred_element_type=jnp.float32,
            ),
            "row",
            scatter_dimension=0,
            tiled=True,
        )
        * scale
    )
    rows_here = w1_rows
    cols_here = w1_cols
    first_grad = (
        lax.psum_scatter(
            jnp.einsum(
                "tnk,ntj->nkj",
                token_rows[:, rows_here],
                hidden_grad[cols_here],
                preferred_element_type=jnp.float32,
            ),
            "row",
            scatter_dimension=0,
            tiled=True,
        )
        * scale
    )
    return (output, input_grad, first_grad, second_grad)


def solution(mesh):
    return jax.shard_map(
        body,
        mesh=mesh,
        in_specs=(
            P(("grp", "row"), None),
            P(("grp", "row"), None),
            P("row", None, None),
            P(),
            P(),
            P("row", None, None),
            P(),
            P(),
        ),
        out_specs=(
            P(("grp", "row"), None),
            P(("grp", "row"), None),
            P(("grp", "row"), None, None),
            P(("grp", "row"), None, None),
        ),
        check_vma=False,
    )
```

profile of v0, /device:TPU:1, one launch (start us, length us, event | category | flops | bytes accessed | tf_op | source)
XLA Modules:
  0.0 212.8 jit_solution(18387387838932313264)
XLA Ops:
  7.2 0.0 copy-start
  7.2 0.0 copy-start.1
  7.2 0.0 reduce-scatter.5.cloned.1.call-start
  7.2 0.7 compare_select_fusion.1
  7.9 1.5 copy.30
  9.4 0.4 copy.31
  9.8 24.7 %all_gather.7 = bf16[16,128,128]{2,1,0:T(8,128)(2,1)S(1)} all-gather(bf16[1,128,128]{2,1,0:T(8,128)(2,1)} %param.10), channel_id=1, replica_groups=mesh['grp'=2,'row'=16] {'row'}, dimensions={0}, use_global_device_ids=true | all-gather | bytes 557056 | tf_op jit(solution)/shard_map/all_gather | solution.py:29
  34.5 0.7 compare_select_fusion.2
  35.1 0.7 compare_select_fusion.3
  35.8 1.5 copy.33
  37.3 1.2 copy.34
  38.5 0.0 copy-done
  38.5 18.9 %all_gather.8 = bf16[16,128,128]{2,1,0:T(8,128)(2,1)S(1)} all-gather(bf16[1,128,128]{2,1,0:T(8,128)(2,1)S(1)} %copy-done), channel_id=1, replica_groups=mesh['grp'=2,'row'=16] {'row'}, dimensions={0}, use_global_device_ids=true | all-gather | bytes 557056 | tf_op jit(solution)/shard_map/all_gather | solution.py:34
  57.4 0.0 copy-done.1
  57.4 0.6 gather_fusion
  58.0 1.3 fusion.11
  59.4 1.8 gather_fusion.2
  61.2 1.5 fusion.7
  62.6 3.4 %broadcast_in_dim.28.clone.1 = f32[96,128,128]{2,1,0:T(8,128)} broadcast(f32[]{:T(128)} %constant.1.clone.1), dimensions={} | broadcast | bytes 6291460 | tf_op jit(solution)/shard_map/broadcast_in_dim | solution.py:22
  66.1 3.8 %scatter_fusion.2 = f32[96,128,128]{2,1,0:T(8,128)} fusion(f32[96,128,128]{2,1,0:T(8,128)} %broadcast_in_dim.28.clone.1, s32[16]{0:T(128)S(1)} %compare_select_fusion, f32[16,128,128]{2,1,0:T(8,128)} %fusion.7), kind=kCustom, calls=%fused_computation.6 | custom fusion | flops 262144 | bytes 3145792 | tf_op jit(solution)/shard_map/scatter-add | solution.py:42
  69.9 3.4 %broadcast_in_dim.28.clone = f32[96,128,128]{2,1,0:T(8,128)} broadcast(f32[]{:T(128)} %constant.1.clone.1), dimensions={} | broadcast | bytes 6291460 | tf_op jit(solution)/shard_map/broadcast_in_dim | solution.py:22
  73.3 3.8 %scatter_fusion = f32[96,128,128]{2,1,0:T(8,128)} fusion(f32[96,128,128]{2,1,0:T(8,128)} %broadcast_in_dim.28.clone, s32[16]{0:T(128)S(1)} %compare_select_fusion.2, f32[16,128,128]{2,1,0:T(8,128)} %fusion.11), kind=kCustom, calls=%fused_computation.4 | custom fusion | flops 262144 | bytes 3145792 | tf_op jit(solution)/shard_map/scatter-add | solution.py:32
  77.2 9.2 %fusion.6 = (bf16[96,128,128]{2,1,0:T(8,128)(2,1)}, bf16[96,128,128]{2,1,0:T(8,128)(2,1)}) fusion(f32[96,128,128]{2,1,0:T(8,128)} %scatter_fusion, f32[96,128,128]{2,1,0:T(8,128)} %scatter_fusion.2), kind=kLoop, calls=%fused_computation.16 | loop fusion | flops 34603008 | bytes 18874368 | tf_op jit(solution)/shard_map/convert_element_type | solution.py:44
  86.4 2.5 %gather_fusion.1 = bf16[16,128,128]{2,1,0:T(8,128)(2,1)S(1)} fusion(bf16[96,128,128]{2,1,0:T(8,128)(2,1)} %get-tuple-element.17, s32[1024]{0:T(1024)S(1)} %pad_clamp_fusion.2), kind=kCustom, calls=%fused_computation.1 | custom fusion | bytes 1048640 | tf_op jit(solution)/shard_map/gather | solution.py:37
  88.9 1.3 fusion.9
  90.3 0.0 reduce-scatter.5.cloned.1.call-update
  90.3 0.2 reduce-scatter.3.cloned.1.call-start
  90.6 2.5 %gather_fusion.3 = bf16[16,128,128]{2,1,0:T(8,128)(2,1)S(1)} fusion(bf16[96,128,128]{2,1,0:T(8,128)(2,1)} %get-tuple-element.16, s32[1024]{0:T(1024)S(1)} %pad_clamp_fusion), kind=kCustom, calls=%fused_computation.3 | custom fusion | bytes 1048640 | tf_op jit(solution)/shard_map/gather | solution.py:49
  93.1 1.4 fusion.13
  94.5 0.0 reduce-scatter.3.cloned.1.call-update
  94.5 1.5 fusion.16
  96.0 0.2 broadcast_in_dim.12.clone.1
  96.2 2.6 %scatter_fusion.3 = f32[128,24,128]{2,0,1:T(8,128)S(1)} fusion(f32[128,24,128]{2,0,1:T(8,128)S(1)} %broadcast_in_dim.12.clone.1, s32[16]{0:T(128)S(1)} %compare_select_fusion.1, f32[16,128,128]{2,1,0:T(8,128)} %fusion.16), kind=kCustom, calls=%fused_computation.7 | custom fusion | flops 262144 | bytes 3145792 | tf_op jit(solution)/shard_map/scatter-add | solution.py:53
  98.8 1.0 convert_element_type.22
  99.8 1.5 copy.35
  101.3 1.2 copy.39
  102.5 1.3 fusion.15
  103.8 0.2 broadcast_in_dim.12.clone
  103.9 2.6 %scatter_fusion.1 = f32[128,24,128]{2,0,1:T(8,128)S(1)} fusion(f32[128,24,128]{2,0,1:T(8,128)S(1)} %broadcast_in_dim.12.clone, s32[16]{0:T(128)S(1)} %compare_select_fusion.3, f32[16,128,128]{2,1,0:T(8,128)} %fusion.15), kind=kCustom, calls=%fused_computation.5 | custom fusion | flops 262144 | bytes 3145792 | tf_op jit(solution)/shard_map/scatter-add | solution.py:41
  106.6 0.1 convert_element_type.19
  106.7 0.4 copy.32
  107.1 1.2 copy.38
  108.3 35.7 %reduce-scatter.5.cloned.1.call-done = f32[1,128,128]{2,1,0:T(8,128)} async-done(((f32[16,128,128]{2,1,0:T(8,128)}), f32[1,128,128]{2,1,0:T(8,128)}) %reduce-scatter.5.cloned.1.call-update) | async-done | bytes 65552 | tf_op jit(solution)/shard_map/reduce_scatter | solution.py:59
  143.9 1.5 broadcast_multiply_fusion
  145.4 59.0 %reduce-scatter.3.cloned.1.call-done = f32[1,128,128]{2,1,0:T(8,128)} async-done(((f32[16,128,128]{2,1,0:T(8,128)}), f32[1,128,128]{2,1,0:T(8,128)}) %reduce-scatter.3.cloned.1.call-update) | async-done | bytes 65552 | tf_op jit(solution)/shard_map/reduce_scatter | solution.py:75
  204.4 1.5 broadcast_multiply_fusion.1
  (5 shorter events, 0.0 us)
Async XLA Ops:
  7.2 31.3 %copy-start = (bf16[1,128,128]{2,1,0:T(8,128)(2,1)S(1)}, bf16[1,128,128]{2,1,0:T(8,128)(2,1)}, u32[]{:S(2)}) copy-start(bf16[1,128,128]{2,1,0:T(8,128)(2,1)} %param.13) | copy-start | bytes 98308
  7.2 50.2 %copy-start.1 = (s32[16]{0:T(128)S(1)}, s32[16]{0:T(128)}, u32[]{:S(2)}) copy-start(s32[16]{0:T(128)} %param.14) | copy-start | bytes 196
  7.2 136.7 %reduce-scatter.5.cloned.1.call-start = ((), (), s32[]{:S(2)}) async-start(), calls=%async_computation.3 | async-start | bytes 1114112 | tf_op jit(solution)/shard_map/reduce_scatter | solution.py:59
  90.3 114.1 %reduce-scatter.3.cloned.1.call-start = ((), (), s32[]{:S(2)}) async-start(), calls=%async_computation.2 | async-start | bytes 1114112 | tf_op jit(solution)/shard_map/reduce_scatter | solution.py:75
Sparse Core Ops, SparseCore 0:
  90.4 53.4 reduce-scatter.4
  148.0 56.4 reduce-scatter.2
where the time goes:
time: 216 us; the launch traced here: 213 us
  waiting for transfers between devices  94.7 us (44%)
  blocking collectives  43.5 us (20%)
  other arithmetic  28.2 us (13%)
  local copies, waits for them, and re-layouts  23.5 us (11%)
  between operations  14.2 us (7%)
  matrix products  8.3 us (4%)
    reduce_scatter x1, waiting for transfers between devices, body(): lax.psum_scatter(jnp.einsum('tnk,ntj->nkj', token_rows[:, rows_here], hid...  59 us
    reduce_scatter x1, waiting for transfers between devices, body(): lax.psum_scatter(jnp.einsum('ntk,tnj->nkj', act[rows_here], cot_rows[:, c...  35.7 us
    all_gather x1, blocking collectives, body(): lax.all_gather(w1_blocks, 'row', axis=0, tiled=True)  24.7 us
    all_gather x1, blocking collectives, body(): piece = lax.all_gather(w2_blocks, 'row', axis=0, tiled=True)  18.9 us
    convert_element_type x1, other arithmetic, body(): jax.vjp(gelu_tanh, hidden)[1](act_grad)[0].astype(jnp.bfloat16)  9.23 us
    broadcast_in_dim x2, local copies, waits for them, and re-layouts, body(): empty_hidden = jnp.zeros((FB, width, BS), jnp.float32)  6.88 us
    unnamed x8, local copies, waits for them, and re-layouts  5.34 us
  transfers between devices with their start and end apart: 2, of which 2 were waited for; matrix products, arithmetic and copies ran while one was open for 9% of the time, Pallas kernels for 0%

commit v1 on v0

v1 whole, which is shorter than its diff:
```python
import functools
import math

import jax
import jax.numpy as jnp
from jax import lax
from jax.experimental import pallas as pl
from jax.experimental.pallas import tpu as pltpu
from jax.sharding import PartitionSpec as P

FB = 96
ROOT = math.sqrt(2.0 / math.pi)
CUBE = 0.044715
F32 = jnp.float32
BF16 = jnp.bfloat16
VMEM = pl.BlockSpec(memory_space=pltpu.VMEM)
SMEM = pl.BlockSpec(memory_space=pltpu.SMEM)


def stages(n):
    bits = [1 << i for i in range(1, n.bit_length() - 1)]
    rounds = []
    if len(bits) % 2:
        rounds.append([bits.pop(0) | 1])
    while bits:
        low, high = bits.pop(0), bits.pop(0)
        rounds.append([low | 1, high | 1, low | high | 1])
    return rounds[::-1] + [[1]]


def slots(n):
    order = [0]
    for masks in stages(n):
        order = order + [o ^ m for m in masks for o in order]
    return order


def swap(value, mask, n):
    return lax.ppermute(value, "row", [(i, i ^ mask) for i in range(n)])


def panel(ref, index, size):
    return ref[:, pl.ds(pl.multiple_of(index * size, size), size)]


def dot(a, b, dims):
    return lax.dot_general(a, b, (dims, ((), ())), preferred_element_type=F32)


def tanh_of(v):
    return jnp.tanh(ROOT * (v + CUBE * (v * v * v)))


def gelu(v):
    return 0.5 * v * (1.0 + tanh_of(v))


def gelu_slope(v):
    t = tanh_of(v)
    return 0.5 * (1.0 + t) + 0.5 * v * (1.0 - t * t) * (ROOT * (1.0 + 3.0 * CUBE * (v * v)))


def each(count, run):
    if count <= 16:
        for s in range(count):
            run(s)
    else:
        def step(s, _):
            run(s)
            return 0
        lax.fori_loop(0, count, step, 0)


class Lists:
    def __init__(self, me, order, r1, c1, r2, c2):
        self.block = lambda s: me[0] ^ order[s]
        self.r1 = lambda s: r1[self.block(s)]
        self.c1 = lambda s: c1[self.block(s)]
        self.r2 = lambda s: r2[self.block(s)]
        self.c2 = lambda s: c2[self.block(s)]


def middle(nb, nw, me, order, r1, c1, r2, c2, tokens, cot, *refs):
    weights, (act, hgrad, send, keep, hidden, agrad) = refs[:nw], refs[nw:]
    at = Lists(me, order, r1, c1, r2, c2)
    size = act.shape[-1]
    half = nb // 2

    def w(s, which):
        return weights[s][which] if nw > 1 else weights[0][s, which]

    def clear(s):
        zero = jnp.zeros(hidden.shape[1:], F32)
        for index in (at.c1(s), at.r2(s)):
            hidden[index] = zero
            agrad[index] = zero

    each(nb, clear)

    def first(s):
        hidden[at.c1(s)] += dot(panel(tokens, at.r1(s), size), w(s, 0), ((1,), (0,)))

    each(nb, first)

    def second(s):
        agrad[at.r2(s)] += dot(panel(cot, at.c2(s), size), w(s, 1), ((1,), (1,)))

    each(nb, second)

    def slope(s):
        c = at.c1(s)
        hgrad[s] = (agrad[c] * gelu_slope(hidden[c])).astype(BF16)

    def activate(s):
        act[s] = gelu(hidden[at.r2(s)]).astype(BF16)

    def put(s, which, value):
        if isinstance(s, int):
            if s >= half:
                send[s - half, which] = value.astype(BF16)
            else:
                keep[s, which] = value
        else:
            @pl.when(s >= half)
            def _():
                send[s - half, which] = value.astype(BF16)

            @pl.when(s < half)
            def _():
                keep[s, which] = value

    def grads(s):
        activate(s)
        slope(s)
        put(s, 0, dot(panel(tokens, at.r1(s), size), hgrad[s], ((0,), (0,))))
        put(s, 1, dot(act[s], panel(cot, at.c2(s), size), ((0,), (0,))))

    each(nb, grads)


def last(nb, nw, me, order, r1, c1, r2, c2, act, hgrad, *refs):
    weights, (out, igrad, oacc, iacc) = refs[:nw], refs[nw:]
    at = Lists(me, order, r1, c1, r2, c2)
    size = act.shape[-1]

    def w(s, which):
        return weights[s][which] if nw > 1 else weights[0][s, which]

    oacc[...] = jnp.zeros_like(oacc)
    iacc[...] = jnp.zeros_like(iacc)

    def one(s):
        oacc[at.c2(s)] += dot(act[s], w(s, 1), ((1,), (0,)))
        iacc[at.r1(s)] += dot(hgrad[s], w(s, 0), ((1,), (1,)))

    each(nb, one)
    for d in range(oacc.shape[0]):
        out[:, d * size:(d + 1) * size] = oacc[d].astype(BF16)
        igrad[:, d * size:(d + 1) * size] = iacc[d].astype(BF16)


def fold(parts, scale, held, *refs):
    arrived, kept, sends = refs[:-parts], refs[-parts], refs[len(refs) - parts + 1:]
    count = kept.shape[0]

    def total(s):
        value = held[s]
        for a in arrived:
            value = value + a[s].astype(F32)
        return value

    def keep(s):
        kept[s] = total(s) * scale

    each(count, keep)
    for i, out in enumerate(sends):
        def leave(s, i=i, out=out):
            out[s] = total(count * (i + 1) + s).astype(BF16)

        each(count, leave)


def call(kernel, outs, smem, args, scratch=(), flops=0, name=None):
    size = sum(math.prod(a.shape) * a.dtype.itemsize for a in (*args, *outs))
    size += sum(math.prod(s.shape) * 4 for s in scratch)
    return pl.pallas_call(
        kernel,
        out_shape=outs,
        in_specs=[SMEM] * len(smem) + [VMEM] * len(args),
        out_specs=[VMEM] * len(outs),
        scratch_shapes=list(scratch),
        compiler_params=pltpu.CompilerParams(vmem_limit_bytes=min(size + (8 << 20), 60 << 20)),
        cost_estimate=pl.CostEstimate(flops=flops, bytes_accessed=size, transcendentals=0),
        name=name,
    )(*smem, *args)


def body(tokens, cotangent, w1_blocks, w1_rows, w1_cols, w2_blocks, w2_rows, w2_cols):
    n = lax.axis_size("row")
    nb = w1_rows.shape[0]
    width, depth = tokens.shape
    size = w1_blocks.shape[-1]
    order = slots(n)
    rounds = stages(n)
    half = nb // 2
    me = lax.axis_index("row").astype(jnp.int32).reshape(1)

    pieces = [jnp.concatenate([w1_blocks, w2_blocks], 0)]
    for masks in rounds:
        pieces = pieces + [swap(p, m, n) for m in masks for p in pieces]
    weights = pieces if n <= 16 else [jnp.stack(pieces)]
    nw = len(weights)
    if n <= 16:
        lists = (me, w1_rows, w1_cols, w2_rows, w2_cols)

        def bind(kernel):
            return lambda me, r1, c1, r2, c2, *refs: kernel(nb, nw, me, order, r1, c1, r2, c2, *refs)
    else:
        lists = (me, jnp.asarray(order, jnp.int32), w1_rows, w1_cols, w2_rows, w2_cols)

        def bind(kernel):
            return functools.partial(kernel, nb, nw)

    panels = jax.ShapeDtypeStruct((nb, width, size), BF16)
    work = 2 * nb * width * size * size
    act, hgrad, send, keep = call(
        bind(middle),
        [
            panels,
            panels,
            jax.ShapeDtypeStruct((half, 2, size, size), BF16),
            jax.ShapeDtypeStruct((half, 2, size, size), F32),
        ],
        lists,
        [tokens, cotangent, *weights],
        [pltpu.VMEM((FB, width, size), F32), pltpu.VMEM((FB, width, size), F32)],
        4 * work,
        "middle",
    )
    model = jax.ShapeDtypeStruct((width, depth), BF16)
    total = pltpu.VMEM((depth // size, width, size), F32)
    output, input_grad = call(bind(last), [model, model], lists, [act, hgrad, *weights], [total, total], 2 * work, "last")

    scale = 1.0 / math.sqrt(width * n)
    sends = [send]
    for now, later in zip(rounds[::-1], [*rounds[-2::-1], []]):
        arrived = [swap(s, m, n) for s, m in zip(sends, now)]
        parts = len(later) + 1
        count = keep.shape[0] // parts
        shape = (count, 2, size, size)
        keep, *sends = call(
            functools.partial(fold, parts, 1.0 if later else scale),
            [jax.ShapeDtypeStruct(shape, F32)] + [jax.ShapeDtypeStruct(shape, BF16)] * len(later),
            (),
            [keep, *arrived],
            (),
            0,
            "fold",
        )
    return (output, input_grad, keep[:, 0], keep[:, 1])


def solution(mesh):
    rows, blocks = P(("grp", "row"), None), P(("grp", "row"), None, None)
    return jax.shard_map(
        body,
        mesh=mesh,
        in_specs=(rows, rows, P("row", None, None), P(), P(), P("row", None, None), P(), P()),
        out_specs=(rows, rows, blocks, blocks),
        check_vma=False,
    )
```

time: 216 us -> 45 us (0.21); the launches traced: 213 us -> 44.4 us
  waiting for transfers between devices: 94.7 us -> 17.5 us
  blocking collectives: 43.5 us -> 0 us
  other arithmetic: 28.2 us -> 0 us
  local copies, waits for them, and re-layouts: 23.5 us -> 3.71 us
  starting transfers between devices: 0.26 us -> 17 us
  between operations: 14.2 us -> 0.71 us
  matrix products: 8.3 us -> 0 us
  Pallas kernels: 0 us -> 5.5 us
    reduce_scatter x2 -> x0, waiting for transfers between devices: 94.7 us -> none  [the longest x1 59 us: body(): lax.psum_scatter(jnp.einsum('tnk,ntj->nkj', token_rows[:, rows_here], hid...]
    all_gather x2 -> x0, blocking collectives: 43.5 us -> none  [the longest x1 24.7 us: body(): lax.all_gather(w1_blocks, 'row', axis=0, tiled=True)]
    ppermute x0 -> x20, waiting for transfers between devices: none -> 17.5 us  [swap(): return lax.ppermute(value, 'row', [(i, i ^ mask) for i in range(n)])]
    ppermute x0 -> x20, starting transfers between devices: none -> 17 us  [swap(): return lax.ppermute(value, 'row', [(i, i ^ mask) for i in range(n)])]
    scatter-add x4 -> x0, other arithmetic: 12.9 us -> none  [the longest x1 3.84 us: body(): hidden = empty_hidden.at[cols_here].add(product)]
    convert_element_type x3 -> x0, other arithmetic: 10.4 us -> none  [the longest x1 9.23 us: body(): jax.vjp(gelu_tanh, hidden)[1](act_grad)[0].astype(jnp.bfloat16)]
    dot_general x6 -> x0, matrix products: 8.3 us -> none  [the longest x1 1.48 us: body(): jnp.einsum('ntj,nkj->tnk', hidden_grad[cols_here], lax.all_gather(w1_bloc...]
    gather x4 -> x0, local copies, waits for them, and re-layouts: 7.5 us -> none  [the longest x1 2.54 us: body(): hidden_grad[cols_here]]
  transfers between devices with their start and end apart: 2 -> 20, of which waited for: 2 -> 10; matrix products, arithmetic and copies ran while one was open for 9% -> 0% of each run, Pallas kernels for 0% -> 6%
where the time goes in v1:
time: 45 us; the launch traced here: 44.4 us
  waiting for transfers between devices  17.5 us (39%)
  starting transfers between devices  17 us (38%)
  Pallas kernels  5.5 us (12%)
  local copies, waits for them, and re-layouts  3.71 us (8%)
  between operations  0.71 us (2%)
    ppermute x20, waiting for transfers between devices, swap(): return lax.ppermute(value, 'row', [(i, i ^ mask) for i in range(n)])  17.5 us
    ppermute x20, starting transfers between devices, swap(): return lax.ppermute(value, 'row', [(i, i ^ mask) for i in range(n)])  17 us
    pallas_call x5, Pallas kernels, call(): pl.pallas_call(kernel, out_shape=outs, in_specs=[SMEM] * len(smem) + [VME...  5.5 us
    unnamed x15, local copies, waits for them, and re-layouts  3.05 us
  transfers between devices with their start and end apart: 20, of which 10 were waited for; matrix products, arithmetic and copies ran while one was open for 0% of the time, Pallas kernels for 6%

profile of v1, /device:TPU:1, one launch (start us, length us, event | category | flops | bytes accessed | tf_op | source)
XLA Modules:
  0.0 44.4 jit_solution(12687259529618941366)
XLA Ops:
  0.6 0.8 %constant_dynamic-update-slice_fusion.1 = bf16[2,128,128]{2,1,0:T(8,128)(2,1)S(1)} fusion(bf16[1,128,128]{2,1,0:T(8,128)(2,1)} %param.10), kind=kLoop, calls=%fused_computation.3 | loop fusion | bytes 65536
  1.4 2.8 %collective-permute-start = (bf16[2,128,128]{2,1,0:T(8,128)(2,1)S(1)}, bf16[2,128,128]{2,1,0:T(8,128)(2,1)S(1)}, u32[]{:S(2)}, u32[]{:S(2)}) collective-permute-start(bf16[2,128,128]{2,1,0:T(8,128)(2,1)S(1)} %constant_dynamic-update-slice_fusion.refs_2_), channel_id=1, source_target_pairs={{0,5},{1,4},{2,7},{3,6},{4,1},{5,0},{6,3},{7,2},{8,13},{9,12},{10,... | collective-permute-start | bytes 196616 | tf_op jit(solution)/shard_map/ppermute | solution.py:39
  4.2 2.0 %collective-permute-start.1 = (bf16[2,128,128]{2,1,0:T(8,128)(2,1)S(1)}, bf16[2,128,128]{2,1,0:T(8,128)(2,1)S(1)}, u32[]{:S(2)}, u32[]{:S(2)}) collective-permute-start(bf16[2,128,128]{2,1,0:T(8,128)(2,1)S(1)} %constant_dynamic-update-slice_fusion.refs_2_), channel_id=1, source_target_pairs={{0,9},{1,8},{2,11},{3,10},{4,13},{5,12},{6,15},{7,14},{8,1},{9,0},... | collective-permute-start | bytes 196616 | tf_op jit(solution)/shard_map/ppermute | solution.py:39
  6.2 0.2 collective-permute-start.2
  6.4 1.6 %collective-permute-start.3 = (bf16[2,128,128]{2,1,0:T(8,128)(2,1)S(1)}, bf16[2,128,128]{2,1,0:T(8,128)(2,1)S(1)}, u32[]{:S(2)}, u32[]{:S(2)}) collective-permute-start(bf16[2,128,128]{2,1,0:T(8,128)(2,1)S(1)} %constant_dynamic-update-slice_fusion.refs_2_), channel_id=1, source_target_pairs={{0,3},{1,2},{2,1},{3,0},{4,7},{5,6},{6,5},{7,4},{8,11},{9,10},{10,... | collective-permute-start | bytes 196616 | tf_op jit(solution)/shard_map/ppermute | solution.py:39
  8.0 0.3 collective-permute-start.7
  8.3 0.0 collective-permute-done.refs_3_
  8.3 0.3 collective-permute-start.4
  8.6 1.6 %collective-permute-done.1.refs_4_ = bf16[2,128,128]{2,1,0:T(8,128)(2,1)S(1)} collective-permute-done((bf16[2,128,128]{2,1,0:T(8,128)(2,1)S(1)}, bf16[2,128,128]{2,1,0:T(8,128)(2,1)S(1)}, u32[]{:S(2)}, u32[]{:S(2)}) %collective-permute-start.1) | collective-permute-done | bytes 65568 | tf_op jit(solution)/shard_map/ppermute | solution.py:39
  10.3 0.1 collective-permute-start.5
  10.4 2.3 %collective-permute-done.2.refs_5_ = bf16[2,128,128]{2,1,0:T(8,128)(2,1)S(1)} collective-permute-done((bf16[2,128,128]{2,1,0:T(8,128)(2,1)S(1)}, bf16[2,128,128]{2,1,0:T(8,128)(2,1)S(1)}, u32[]{:S(2)}, u32[]{:S(2)}) %collective-permute-start.2) | collective-permute-done | bytes 65568 | tf_op jit(solution)/shard_map/ppermute | solution.py:39
  12.7 1.6 %collective-permute-start.6 = (bf16[2,128,128]{2,1,0:T(8,128)(2,1)S(1)}, bf16[2,128,128]{2,1,0:T(8,128)(2,1)S(1)}, u32[]{:S(2)}, u32[]{:S(2)}) collective-permute-start(bf16[2,128,128]{2,1,0:T(8,128)(2,1)S(1)} %collective-permute-done.2.refs_5_), channel_id=1, source_target_pairs={{0,3},{1,2},{2,1},{3,0},{4,7},{5,6},{6,5},{7,4},{8,11},{9,10},{10,... | collective-permute-start | bytes 196616 | tf_op jit(solution)/shard_map/ppermute | solution.py:39
  14.3 0.0 collective-permute-done.3.refs_6_
  14.3 0.1 collective-permute-start.10
  14.3 0.0 collective-permute-done.7.refs_10_
  14.3 0.5 %collective-permute-start.8 = (bf16[2,128,128]{2,1,0:T(8,128)(2,1)S(1)}, bf16[2,128,128]{2,1,0:T(8,128)(2,1)S(1)}, u32[]{:S(2)}, u32[]{:S(2)}) collective-permute-start(bf16[2,128,128]{2,1,0:T(8,128)(2,1)S(1)} %collective-permute-done.refs_3_), channel_id=1, source_target_pairs={{0,1},{1,0},{2,3},{3,2},{4,5},{5,4},{6,7},{7,6},{8,9},{9,8},{10,11... | collective-permute-start | bytes 196616 | tf_op jit(solution)/shard_map/ppermute | solution.py:39
  14.8 0.0 collective-permute-done.4.refs_7_
  14.8 0.1 collective-permute-start.9
  14.9 0.0 collective-permute-done.5.refs_8_
  14.9 0.4 collective-permute-start.11
  15.3 1.6 %collective-permute-done.6.refs_9_ = bf16[2,128,128]{2,1,0:T(8,128)(2,1)S(1)} collective-permute-done((bf16[2,128,128]{2,1,0:T(8,128)(2,1)S(1)}, bf16[2,128,128]{2,1,0:T(8,128)(2,1)S(1)}, u32[]{:S(2)}, u32[]{:S(2)}) %collective-permute-start.6) | collective-permute-done | bytes 65568 | tf_op jit(solution)/shard_map/ppermute | solution.py:39
  16.9 0.4 collective-permute-start.12
  17.3 0.0 collective-permute-done.10.refs_13_
  17.3 0.1 collective-permute-start.13
  17.4 0.0 collective-permute-done.8.refs_11_
  17.4 0.4 collective-permute-start.14
  17.8 0.0 collective-permute-done.9.refs_12_
  17.8 0.0 collective-permute-done.11.refs_14_
  17.9 0.4 collective-permute-done.12.refs_15_
  18.2 0.4 collective-permute-done.13.refs_16_
  18.6 0.2 collective-permute-done.14.refs_17_
  18.7 0.0 copy-start
  18.8 1.1 %copy-done = bf16[128,3072]{1,0:T(8,128)(2,1)S(1)} copy-done((bf16[128,3072]{1,0:T(8,128)(2,1)S(1)}, bf16[128,3072]{1,0:T(8,128)(2,1)}, u32[]{:S(2)}) %copy-start) | copy-done | bytes 786456
  19.9 1.1 %copy-done.1 = bf16[128,3072]{1,0:T(8,128)(2,1)S(1)} copy-done((bf16[128,3072]{1,0:T(8,128)(2,1)S(1)}, bf16[128,3072]{1,0:T(8,128)(2,1)}, u32[]{:S(2)}) %copy-start.1) | copy-done | bytes 786456
  21.0 2.7 %middle.1 = (bf16[16,128,128]{2,1,0:T(8,128)(2,1)S(1)}, bf16[16,128,128]{2,1,0:T(8,128)(2,1)S(1)}, bf16[8,2,128,128]{3,2,1,0:T(8,128)(2,1)S(1)}, f32[8,2,128,128]{3,2,1,0:T(8,128)S(1)}) custom-call(s32[1]{0:T(128)} %bitcast.me, s32[16]{0:T(128)S(1)} %copy-done.2, s32[16]{0:T(128)S(1)} %copy-done.3, s32[16]{0:T(128)S(1)} %copy-done.4, s32[16]{0:T(128)S(1)} %copy-done.5, ...), custom_call_target="tpu_custom_call" | custom-call | flops 268435456 | bytes 17825792 | tf_op jit(solution)/shard_map/middle/pallas_call | solution.py:186
  23.7 0.4 collective-permute-start.15
  24.1 1.5 %collective-permute-done.15.refs_0_ = bf16[8,2,128,128]{3,2,1,0:T(8,128)(2,1)S(1)} collective-permute-done((bf16[8,2,128,128]{3,2,1,0:T(8,128)(2,1)S(1)}, bf16[8,2,128,128]{3,2,1,0:T(8,128)(2,1)S(1)}, u32[]{:S(2)}, u32[]{:S(2)}) %collective-permute-start.15) | collective-permute-done | bytes 524320 | tf_op jit(solution)/shard_map/ppermute | solution.py:39
  25.7 0.1 fold.3
  25.8 1.6 %collective-permute-start.16 = (bf16[4,2,128,128]{3,2,1,0:T(8,128)(2,1)S(1)}, bf16[4,2,128,128]{3,2,1,0:T(8,128)(2,1)S(1)}, u32[]{:S(2)}, u32[]{:S(2)}) collective-permute-start(bf16[4,2,128,128]{3,2,1,0:T(8,128)(2,1)S(1)} %get-tuple-element.23), channel_id=1, source_target_pairs={{0,3},{1,2},{2,1},{3,0},{4,7},{5,6},{6,5},{7,4},{8,11},{9,10},{10,... | collective-permute-start | bytes 786440 | tf_op jit(solution)/shard_map/ppermute | solution.py:39
  27.4 6.8 %collective-permute-done.16.refs_0_ = bf16[4,2,128,128]{3,2,1,0:T(8,128)(2,1)S(1)} collective-permute-done((bf16[4,2,128,128]{3,2,1,0:T(8,128)(2,1)S(1)}, bf16[4,2,128,128]{3,2,1,0:T(8,128)(2,1)S(1)}, u32[]{:S(2)}, u32[]{:S(2)}) %collective-permute-start.16) | collective-permute-done | bytes 262176 | tf_op jit(solution)/shard_map/ppermute | solution.py:39
  34.2 1.2 %collective-permute-start.17 = (bf16[1,2,128,128]{3,2,1,0:T(8,128)(2,1)S(1)}, bf16[1,2,128,128]{3,2,1,0:T(8,128)(2,1)S(1)}, u32[]{:S(2)}, u32[]{:S(2)}) collective-permute-start(bf16[1,2,128,128]{3,2,1,0:T(8,128)(2,1)S(1)} %get-tuple-element.25), channel_id=1, source_target_pairs={{0,5},{1,4},{2,7},{3,6},{4,1},{5,0},{6,3},{7,2},{8,13},{9,12},{10,... | collective-permute-start | bytes 196616 | tf_op jit(solution)/shard_map/ppermute | solution.py:39
  35.4 2.4 %collective-permute-start.18 = (bf16[1,2,128,128]{3,2,1,0:T(8,128)(2,1)S(1)}, bf16[1,2,128,128]{3,2,1,0:T(8,128)(2,1)S(1)}, u32[]{:S(2)}, u32[]{:S(2)}) collective-permute-start(bf16[1,2,128,128]{3,2,1,0:T(8,128)(2,1)S(1)} %get-tuple-element.26), channel_id=1, source_target_pairs={{0,9},{1,8},{2,11},{3,10},{4,13},{5,12},{6,15},{7,14},{8,1},{9,0},... | collective-permute-start | bytes 196616 | tf_op jit(solution)/shard_map/ppermute | solution.py:39
  37.7 0.6 %collective-permute-start.19 = (bf16[1,2,128,128]{3,2,1,0:T(8,128)(2,1)S(1)}, bf16[1,2,128,128]{3,2,1,0:T(8,128)(2,1)S(1)}, u32[]{:S(2)}, u32[]{:S(2)}) collective-permute-start(bf16[1,2,128,128]{3,2,1,0:T(8,128)(2,1)S(1)} %get-tuple-element.27), channel_id=1, source_target_pairs={{0,13},{1,12},{2,15},{3,14},{4,9},{5,8},{6,11},{7,10},{8,5},{9,4},... | collective-permute-start | bytes 196616 | tf_op jit(solution)/shard_map/ppermute | solution.py:39
  38.3 2.6 %last.1 = (bf16[128,3072]{1,0:T(8,128)(2,1)}, bf16[128,3072]{1,0:T(8,128)(2,1)}) custom-call(s32[1]{0:T(128)} %bitcast.me, s32[16]{0:T(128)S(1)} %copy-done.2, s32[16]{0:T(128)S(1)} %copy-done.3, s32[16]{0:T(128)S(1)} %copy-done.4, s32[16]{0:T(128)S(1)} %copy-done.5, bf16[16,128,128]{2,1,0:T(8,128)(2,1)S(1)} %get-tuple-element.16.refs_0_, ...), custom_call_target="tpu_custom_call" | custom-call | flops 134217728 | bytes 6815744 | tf_op jit(solution)/shard_map/last/pallas_call | solution.py:186
  41.0 0.0 collective-permute-done.17.refs_0_
  41.0 1.0 %collective-permute-done.18.refs_1_ = bf16[1,2,128,128]{3,2,1,0:T(8,128)(2,1)S(1)} collective-permute-done((bf16[1,2,128,128]{3,2,1,0:T(8,128)(2,1)S(1)}, bf16[1,2,128,128]{3,2,1,0:T(8,128)(2,1)S(1)}, u32[]{:S(2)}, u32[]{:S(2)}) %collective-permute-start.18) | collective-permute-done | bytes 65568 | tf_op jit(solution)/shard_map/ppermute | solution.py:39
  41.9 1.8 %collective-permute-done.19.refs_2_ = bf16[1,2,128,128]{3,2,1,0:T(8,128)(2,1)S(1)} collective-permute-done((bf16[1,2,128,128]{3,2,1,0:T(8,128)(2,1)S(1)}, bf16[1,2,128,128]{3,2,1,0:T(8,128)(2,1)S(1)}, u32[]{:S(2)}, u32[]{:S(2)}) %collective-permute-start.19) | collective-permute-done | bytes 65568 | tf_op jit(solution)/shard_map/ppermute | solution.py:39
  43.7 0.7 %slice_bitcast_fusion = (f32[1,128,128]{2,1,0:T(8,128)}, f32[1,128,128]{2,1,0:T(8,128)}) fusion(f32[1,2,128,128]{3,2,1,0:T(8,128)S(1)} %fold.5), kind=kLoop, calls=%fused_computation | loop fusion | bytes 262144 | tf_op jit(solution)/shard_map/squeeze | solution.py:260
  (14 shorter events, 0.1 us)
Async XLA Ops:
  0.6 0.8 %copy-start.6 = (bf16[1,128,128]{2,1,0:T(8,128)(2,1)S(1)}, bf16[1,128,128]{2,1,0:T(8,128)(2,1)}, u32[]{:S(2)}) copy-start(bf16[1,128,128]{2,1,0:T(8,128)(2,1)} %param.13) | copy-start | bytes 98308
  1.4 6.9 %collective-permute-start = (bf16[2,128,128]{2,1,0:T(8,128)(2,1)S(1)}, bf16[2,128,128]{2,1,0:T(8,128)(2,1)S(1)}, u32[]{:S(2)}, u32[]{:S(2)}) collective-permute-start(bf16[2,128,128]{2,1,0:T(8,128)(2,1)S(1)} %constant_dynamic-update-slice_fusion.refs_2_), channel_id=1, source_target_pairs={{0,5},{1,4},{2,7},{3,6},{4,1},{5,0},{6,3},{7,2},{8,13},{9,12},{10,... | collective-permute-start | bytes 196616 | tf_op jit(solution)/shard_map/ppermute | solution.py:39
  4.2 6.1 %collective-permute-start.1 = (bf16[2,128,128]{2,1,0:T(8,128)(2,1)S(1)}, bf16[2,128,128]{2,1,0:T(8,128)(2,1)S(1)}, u32[]{:S(2)}, u32[]{:S(2)}) collective-permute-start(bf16[2,128,128]{2,1,0:T(8,128)(2,1)S(1)} %constant_dynamic-update-slice_fusion.refs_2_), channel_id=1, source_target_pairs={{0,9},{1,8},{2,11},{3,10},{4,13},{5,12},{6,15},{7,14},{8,1},{9,0},... | collective-permute-start | bytes 196616 | tf_op jit(solution)/shard_map/ppermute | solution.py:39
  6.2 6.5 %collective-permute-start.2 = (bf16[2,128,128]{2,1,0:T(8,128)(2,1)S(1)}, bf16[2,128,128]{2,1,0:T(8,128)(2,1)S(1)}, u32[]{:S(2)}, u32[]{:S(2)}) collective-permute-start(bf16[2,128,128]{2,1,0:T(8,128)(2,1)S(1)} %constant_dynamic-update-slice_fusion.refs_2_), channel_id=1, source_target_pairs={{0,13},{1,12},{2,15},{3,14},{4,9},{5,8},{6,11},{7,10},{8,5},{9,4},... | collective-permute-start | bytes 196616 | tf_op jit(solution)/shard_map/ppermute | solution.py:39
  6.4 7.9 %collective-permute-start.3 = (bf16[2,128,128]{2,1,0:T(8,128)(2,1)S(1)}, bf16[2,128,128]{2,1,0:T(8,128)(2,1)S(1)}, u32[]{:S(2)}, u32[]{:S(2)}) collective-permute-start(bf16[2,128,128]{2,1,0:T(8,128)(2,1)S(1)} %constant_dynamic-update-slice_fusion.refs_2_), channel_id=1, source_target_pairs={{0,3},{1,2},{2,1},{3,0},{4,7},{5,6},{6,5},{7,4},{8,11},{9,10},{10,... | collective-permute-start | bytes 196616 | tf_op jit(solution)/shard_map/ppermute | solution.py:39
  8.0 6.3 %collective-permute-start.7 = (bf16[2,128,128]{2,1,0:T(8,128)(2,1)S(1)}, bf16[2,128,128]{2,1,0:T(8,128)(2,1)S(1)}, u32[]{:S(2)}, u32[]{:S(2)}) collective-permute-start(bf16[2,128,128]{2,1,0:T(8,128)(2,1)S(1)} %constant_dynamic-update-slice_fusion.refs_2_), channel_id=1, source_target_pairs={{0,1},{1,0},{2,3},{3,2},{4,5},{5,4},{6,7},{7,6},{8,9},{9,8},{10,11... | collective-permute-start | bytes 196616 | tf_op jit(solution)/shard_map/ppermute | solution.py:39
  8.3 6.5 %collective-permute-start.4 = (bf16[2,128,128]{2,1,0:T(8,128)(2,1)S(1)}, bf16[2,128,128]{2,1,0:T(8,128)(2,1)S(1)}, u32[]{:S(2)}, u32[]{:S(2)}) collective-permute-start(bf16[2,128,128]{2,1,0:T(8,128)(2,1)S(1)} %collective-permute-done.refs_3_), channel_id=1, source_target_pairs={{0,3},{1,2},{2,1},{3,0},{4,7},{5,6},{6,5},{7,4},{8,11},{9,10},{10,... | collective-permute-start | bytes 196616 | tf_op jit(solution)/shard_map/ppermute | solution.py:39
  10.3 4.6 %collective-permute-start.5 = (bf16[2,128,128]{2,1,0:T(8,128)(2,1)S(1)}, bf16[2,128,128]{2,1,0:T(8,128)(2,1)S(1)}, u32[]{:S(2)}, u32[]{:S(2)}) collective-permute-start(bf16[2,128,128]{2,1,0:T(8,128)(2,1)S(1)} %collective-permute-done.1.refs_4_), channel_id=1, source_target_pairs={{0,3},{1,2},{2,1},{3,0},{4,7},{5,6},{6,5},{7,4},{8,11},{9,10},{10,... | collective-permute-start | bytes 196616 | tf_op jit(solution)/shard_map/ppermute | solution.py:39
  12.7 4.2 %collective-permute-start.6 = (bf16[2,128,128]{2,1,0:T(8,128)(2,1)S(1)}, bf16[2,128,128]{2,1,0:T(8,128)(2,1)S(1)}, u32[]{:S(2)}, u32[]{:S(2)}) collective-permute-start(bf16[2,128,128]{2,1,0:T(8,128)(2,1)S(1)} %collective-permute-done.2.refs_5_), channel_id=1, source_target_pairs={{0,3},{1,2},{2,1},{3,0},{4,7},{5,6},{6,5},{7,4},{8,11},{9,10},{10,... | collective-permute-start | bytes 196616 | tf_op jit(solution)/shard_map/ppermute | solution.py:39
  14.3 3.0 %collective-permute-start.10 = (bf16[2,128,128]{2,1,0:T(8,128)(2,1)S(1)}, bf16[2,128,128]{2,1,0:T(8,128)(2,1)S(1)}, u32[]{:S(2)}, u32[]{:S(2)}) collective-permute-start(bf16[2,128,128]{2,1,0:T(8,128)(2,1)S(1)} %collective-permute-done.2.refs_5_), channel_id=1, source_target_pairs={{0,1},{1,0},{2,3},{3,2},{4,5},{5,4},{6,7},{7,6},{8,9},{9,8},{10,11... | collective-permute-start | bytes 196616 | tf_op jit(solution)/shard_map/ppermute | solution.py:39
  14.3 3.1 %collective-permute-start.8 = (bf16[2,128,128]{2,1,0:T(8,128)(2,1)S(1)}, bf16[2,128,128]{2,1,0:T(8,128)(2,1)S(1)}, u32[]{:S(2)}, u32[]{:S(2)}) collective-permute-start(bf16[2,128,128]{2,1,0:T(8,128)(2,1)S(1)} %collective-permute-done.refs_3_), channel_id=1, source_target_pairs={{0,1},{1,0},{2,3},{3,2},{4,5},{5,4},{6,7},{7,6},{8,9},{9,8},{10,11... | collective-permute-start | bytes 196616 | tf_op jit(solution)/shard_map/ppermute | solution.py:39
  14.8 3.0 %collective-permute-start.9 = (bf16[2,128,128]{2,1,0:T(8,128)(2,1)S(1)}, bf16[2,128,128]{2,1,0:T(8,128)(2,1)S(1)}, u32[]{:S(2)}, u32[]{:S(2)}) collective-permute-start(bf16[2,128,128]{2,1,0:T(8,128)(2,1)S(1)} %collective-permute-done.1.refs_4_), channel_id=1, source_target_pairs={{0,1},{1,0},{2,3},{3,2},{4,5},{5,4},{6,7},{7,6},{8,9},{9,8},{10,11... | collective-permute-start | bytes 196616 | tf_op jit(solution)/shard_map/ppermute | solution.py:39
  14.9 3.0 %collective-permute-start.11 = (bf16[2,128,128]{2,1,0:T(8,128)(2,1)S(1)}, bf16[2,128,128]{2,1,0:T(8,128)(2,1)S(1)}, u32[]{:S(2)}, u32[]{:S(2)}) collective-permute-start(bf16[2,128,128]{2,1,0:T(8,128)(2,1)S(1)} %collective-permute-done.3.refs_6_), channel_id=1, source_target_pairs={{0,1},{1,0},{2,3},{3,2},{4,5},{5,4},{6,7},{7,6},{8,9},{9,8},{10,11... | collective-permute-start | bytes 196616 | tf_op jit(solution)/shard_map/ppermute | solution.py:39
  16.9 1.3 %collective-permute-start.12 = (bf16[2,128,128]{2,1,0:T(8,128)(2,1)S(1)}, bf16[2,128,128]{2,1,0:T(8,128)(2,1)S(1)}, u32[]{:S(2)}, u32[]{:S(2)}) collective-permute-start(bf16[2,128,128]{2,1,0:T(8,128)(2,1)S(1)} %collective-permute-done.4.refs_7_), channel_id=1, source_target_pairs={{0,1},{1,0},{2,3},{3,2},{4,5},{5,4},{6,7},{7,6},{8,9},{9,8},{10,11... | collective-permute-start | bytes 196616 | tf_op jit(solution)/shard_map/ppermute | solution.py:39
  17.3 1.3 %collective-permute-start.13 = (bf16[2,128,128]{2,1,0:T(8,128)(2,1)S(1)}, bf16[2,128,128]{2,1,0:T(8,128)(2,1)S(1)}, u32[]{:S(2)}, u32[]{:S(2)}) collective-permute-start(bf16[2,128,128]{2,1,0:T(8,128)(2,1)S(1)} %collective-permute-done.5.refs_8_), channel_id=1, source_target_pairs={{0,1},{1,0},{2,3},{3,2},{4,5},{5,4},{6,7},{7,6},{8,9},{9,8},{10,11... | collective-permute-start | bytes 196616 | tf_op jit(solution)/shard_map/ppermute | solution.py:39
  17.4 1.3 %collective-permute-start.14 = (bf16[2,128,128]{2,1,0:T(8,128)(2,1)S(1)}, bf16[2,128,128]{2,1,0:T(8,128)(2,1)S(1)}, u32[]{:S(2)}, u32[]{:S(2)}) collective-permute-start(bf16[2,128,128]{2,1,0:T(8,128)(2,1)S(1)} %collective-permute-done.6.refs_9_), channel_id=1, source_target_pairs={{0,1},{1,0},{2,3},{3,2},{4,5},{5,4},{6,7},{7,6},{8,9},{9,8},{10,11... | collective-permute-start | bytes 196616 | tf_op jit(solution)/shard_map/ppermute | solution.py:39
  17.8 0.9 %copy-start.5 = (s32[16]{0:T(128)S(1)}, s32[16]{0:T(128)}, u32[]{:S(2)}) copy-start(s32[16]{0:T(128)} %c2.3) | copy-start | bytes 196
  17.8 0.9 %copy-start.2 = (s32[16]{0:T(128)S(1)}, s32[16]{0:T(128)}, u32[]{:S(2)}) copy-start(s32[16]{0:T(128)} %r1.3) | copy-start | bytes 196
  17.8 0.9 %copy-start.3 = (s32[16]{0:T(128)S(1)}, s32[16]{0:T(128)}, u32[]{:S(2)}) copy-start(s32[16]{0:T(128)} %c1.3) | copy-start | bytes 196
  17.8 0.9 %copy-start.4 = (s32[16]{0:T(128)S(1)}, s32[16]{0:T(128)}, u32[]{:S(2)}) copy-start(s32[16]{0:T(128)} %r2.3) | copy-start | bytes 196
  18.7 1.1 %copy-start = (bf16[128,3072]{1,0:T(8,128)(2,1)S(1)}, bf16[128,3072]{1,0:T(8,128)(2,1)}, u32[]{:S(2)}) copy-start(bf16[128,3072]{1,0:T(8,128)(2,1)} %refs_0_.1) | copy-start | bytes 2359300
  19.9 1.1 %copy-start.1 = (bf16[128,3072]{1,0:T(8,128)(2,1)S(1)}, bf16[128,3072]{1,0:T(8,128)(2,1)}, u32[]{:S(2)}) copy-start(bf16[128,3072]{1,0:T(8,128)(2,1)} %refs_1_.1) | copy-start | bytes 2359300
  23.7 2.0 %collective-permute-start.15 = (bf16[8,2,128,128]{3,2,1,0:T(8,128)(2,1)S(1)}, bf16[8,2,128,128]{3,2,1,0:T(8,128)(2,1)S(1)}, u32[]{:S(2)}, u32[]{:S(2)}) collective-permute-start(bf16[8,2,128,128]{3,2,1,0:T(8,128)(2,1)S(1)} %get-tuple-element.21), channel_id=1, source_target_pairs={{0,1},{1,0},{2,3},{3,2},{4,5},{5,4},{6,7},{7,6},{8,9},{9,8},{10,11... | collective-permute-start | bytes 1572872 | tf_op jit(solution)/shard_map/ppermute | solution.py:39
  25.8 8.3 %collective-permute-start.16 = (bf16[4,2,128,128]{3,2,1,0:T(8,128)(2,1)S(1)}, bf16[4,2,128,128]{3,2,1,0:T(8,128)(2,1)S(1)}, u32[]{:S(2)}, u32[]{:S(2)}) collective-permute-start(bf16[4,2,128,128]{3,2,1,0:T(8,128)(2,1)S(1)} %get-tuple-element.23), channel_id=1, source_target_pairs={{0,3},{1,2},{2,1},{3,0},{4,7},{5,6},{6,5},{7,4},{8,11},{9,10},{10,... | collective-permute-start | bytes 786440 | tf_op jit(solution)/shard_map/ppermute | solution.py:39
  34.2 6.8 %collective-permute-start.17 = (bf16[1,2,128,128]{3,2,1,0:T(8,128)(2,1)S(1)}, bf16[1,2,128,128]{3,2,1,0:T(8,128)(2,1)S(1)}, u32[]{:S(2)}, u32[]{:S(2)}) collective-permute-start(bf16[1,2,128,128]{3,2,1,0:T(8,128)(2,1)S(1)} %get-tuple-element.25), channel_id=1, source_target_pairs={{0,5},{1,4},{2,7},{3,6},{4,1},{5,0},{6,3},{7,2},{8,13},{9,12},{10,... | collective-permute-start | bytes 196616 | tf_op jit(solution)/shard_map/ppermute | solution.py:39
  35.4 6.5 %collective-permute-start.18 = (bf16[1,2,128,128]{3,2,1,0:T(8,128)(2,1)S(1)}, bf16[1,2,128,128]{3,2,1,0:T(8,128)(2,1)S(1)}, u32[]{:S(2)}, u32[]{:S(2)}) collective-permute-start(bf16[1,2,128,128]{3,2,1,0:T(8,128)(2,1)S(1)} %get-tuple-element.26), channel_id=1, source_target_pairs={{0,9},{1,8},{2,11},{3,10},{4,13},{5,12},{6,15},{7,14},{8,1},{9,0},... | collective-permute-start | bytes 196616 | tf_op jit(solution)/shard_map/ppermute | solution.py:39
  37.7 6.0 %collective-permute-start.19 = (bf16[1,2,128,128]{3,2,1,0:T(8,128)(2,1)S(1)}, bf16[1,2,128,128]{3,2,1,0:T(8,128)(2,1)S(1)}, u32[]{:S(2)}, u32[]{:S(2)}) collective-permute-start(bf16[1,2,128,128]{3,2,1,0:T(8,128)(2,1)S(1)} %get-tuple-element.27), channel_id=1, source_target_pairs={{0,13},{1,12},{2,15},{3,14},{4,9},{5,8},{6,11},{7,10},{8,5},{9,4},... | collective-permute-start | bytes 196616 | tf_op jit(solution)/shard_map/ppermute | solution.py:39

commit v2 on v1

v2 whole, which is shorter than its diff:
```python
import functools
import math

import jax
import jax.numpy as jnp
from jax import lax
from jax.experimental import pallas as pl
from jax.experimental.pallas import tpu as pltpu
from jax.sharding import PartitionSpec as P

FB = 96
ROOT = math.sqrt(2.0 / math.pi)
CUBE = 0.044715
F32 = jnp.float32
BF16 = jnp.bfloat16
VMEM = pl.BlockSpec(memory_space=pltpu.VMEM)
ANY = pl.BlockSpec(memory_space=pl.ANY)
SMEM = pl.BlockSpec(memory_space=pltpu.SMEM)


def stages(n):
    bits = [1 << i for i in range(1, n.bit_length() - 1)]
    rounds = []
    if len(bits) % 2:
        rounds.append([bits.pop(0) | 1])
    while bits:
        low, high = bits.pop(0), bits.pop(0)
        rounds.append([low | 1, high | 1, low | high | 1])
    return rounds[::-1] + [[1]]


def slots(n):
    order = [0]
    for masks in stages(n):
        order = order + [o ^ m for m in masks for o in order]
    return order


def swap(value, mask, n):
    return lax.ppermute(value, "row", [(i, i ^ mask) for i in range(n)])


def panel(ref, index, size):
    return ref[:, pl.ds(pl.multiple_of(index * size, size), size)]


def dot(a, b, dims):
    return lax.dot_general(a, b, (dims, ((), ())), preferred_element_type=F32)


def tanh_of(v):
    return jnp.tanh(ROOT * (v + CUBE * (v * v * v)))


def gelu(v):
    return 0.5 * v * (1.0 + tanh_of(v))


def gelu_slope(v):
    t = tanh_of(v)
    return 0.5 * (1.0 + t) + 0.5 * v * (1.0 - t * t) * (ROOT * (1.0 + 3.0 * CUBE * (v * v)))


def each(count, run):
    if count <= 16:
        for s in range(count):
            run(s)
    else:
        def step(s, _):
            run(s)
            return 0
        lax.fori_loop(0, count, step, 0)


class Lists:
    def __init__(self, me, order, r1, c1, r2, c2):
        self.block = lambda s: me[0] ^ order[s]
        self.r1 = lambda s: r1[self.block(s)]
        self.c1 = lambda s: c1[self.block(s)]
        self.r2 = lambda s: r2[self.block(s)]
        self.c2 = lambda s: c2[self.block(s)]


def middle(nb, nw, parts, me, order, r1, c1, r2, c2, tokens, cot, *refs):
    weights, (act, hgrad, *out), (hidden, agrad, tok, ct, sems) = refs[:nw], refs[nw:-5], refs[-5:]
    sends, keeps = out[:parts], out[parts:]
    at = Lists(me, order, r1, c1, r2, c2)
    size = act.shape[-1]
    rest = nb // parts
    half = rest // 2

    def w(s, which):
        return weights[s][which] if nw > 1 else weights[0][s, which]

    def begin(s):
        pltpu.make_async_copy(panel(tokens.at, at.r1(s), size), tok.at[s], sems.at[0]).start()
        pltpu.make_async_copy(panel(cot.at, at.c2(s), size), ct.at[s], sems.at[1]).start()

    each(nb, begin)

    def clear(s):
        zero = jnp.zeros(hidden.shape[1:], F32)
        for index in (at.c1(s), at.r2(s)):
            hidden[index] = zero
            agrad[index] = zero

    each(nb, clear)

    pltpu.make_async_copy(tok, tok, sems.at[0]).wait()

    def first(s):
        hidden[at.c1(s)] += dot(tok[s], w(s, 0), ((1,), (0,)))

    each(nb, first)
    pltpu.make_async_copy(ct, ct, sems.at[1]).wait()

    def second(s):
        agrad[at.r2(s)] += dot(ct[s], w(s, 1), ((1,), (1,)))

    each(nb, second)

    def slope(s):
        c = at.c1(s)
        hgrad[s] = (agrad[c] * gelu_slope(hidden[c])).astype(BF16)

    def activate(s):
        act[s] = gelu(hidden[at.r2(s)]).astype(BF16)

    def put(i, q, which, value):
        def leave():
            sends[i][q - half, which] = value.astype(BF16)

        def stay():
            keeps[i][q, which] = value

        if isinstance(q, int):
            leave() if q >= half else stay()
        else:
            pl.when(q >= half)(leave)
            pl.when(q < half)(stay)

    def grads(i, q):
        s = i + parts * q
        activate(s)
        slope(s)
        put(i, q, 0, dot(tok[s], hgrad[s], ((0,), (0,))))
        put(i, q, 1, dot(act[s], ct[s], ((0,), (0,))))

    for i in range(parts):
        each(rest, functools.partial(grads, i))


def last(nb, nw, me, order, r1, c1, r2, c2, act, hgrad, *refs):
    weights, (out, igrad, oacc, iacc) = refs[:nw], refs[nw:]
    at = Lists(me, order, r1, c1, r2, c2)
    size = act.shape[-1]

    def w(s, which):
        return weights[s][which] if nw > 1 else weights[0][s, which]

    oacc[...] = jnp.zeros_like(oacc)
    iacc[...] = jnp.zeros_like(iacc)

    def one(s):
        oacc[at.c2(s)] += dot(act[s], w(s, 1), ((1,), (0,)))
        iacc[at.r1(s)] += dot(hgrad[s], w(s, 0), ((1,), (1,)))

    each(nb, one)
    for d in range(oacc.shape[0]):
        out[:, d * size:(d + 1) * size] = oacc[d].astype(BF16)
        igrad[:, d * size:(d + 1) * size] = iacc[d].astype(BF16)


def fold(parts, held, *refs):
    arrived, outs = refs[:-parts], refs[-parts:]
    count = outs[0].shape[0]
    for i, out in enumerate(outs):
        def one(q, i=i, out=out):
            value = held[count * i + q]
            for a in arrived:
                value = value + a[count * i + q].astype(F32)
            out[q] = value.astype(out.dtype)

        each(count, one)


def close(scale, held, *refs):
    arrived, outs = refs[:-2], refs[-2:]
    for which, out in enumerate(outs):
        value = held[0, which]
        for a in arrived:
            value = value + a[0, which].astype(F32)
        out[0] = value * scale


def call(kernel, outs, smem, args, scratch=(), flops=0, name=None, any_args=()):
    size = sum(math.prod(a.shape) * a.dtype.itemsize for a in (*args, *outs))
    size += sum(math.prod(s.shape) * 4 for s in scratch[:4])
    return pl.pallas_call(
        kernel,
        out_shape=outs,
        in_specs=[SMEM] * len(smem) + [ANY] * len(any_args) + [VMEM] * len(args),
        out_specs=[VMEM] * len(outs),
        scratch_shapes=list(scratch),
        compiler_params=pltpu.CompilerParams(vmem_limit_bytes=min(size + (4 << 20), 60 << 20)),
        cost_estimate=pl.CostEstimate(flops=flops, bytes_accessed=size, transcendentals=0),
        name=name,
    )(*smem, *[pltpu.with_memory_space_constraint(a, pltpu.HBM) for a in any_args], *args)


def body(tokens, cotangent, w1_blocks, w1_rows, w1_cols, w2_blocks, w2_rows, w2_cols):
    n = lax.axis_size("row")
    nb = w1_rows.shape[0]
    width, depth = tokens.shape
    size = w1_blocks.shape[-1]
    order = slots(n)
    rounds = stages(n)
    me = lax.axis_index("row").astype(jnp.int32).reshape(1)

    pieces = [jnp.concatenate([w1_blocks, w2_blocks], 0)]
    for masks in rounds:
        pieces = pieces + [swap(p, m, n) for m in masks for p in pieces]
    weights = pieces if n <= 16 else [jnp.stack(pieces)]
    nw = len(weights)
    if n <= 16:
        lists = (me, w1_rows, w1_cols, w2_rows, w2_cols)

        def bind(kernel, *given):
            return lambda me, r1, c1, r2, c2, *refs: kernel(*given, me, order, r1, c1, r2, c2, *refs)
    else:
        lists = (me, jnp.asarray(order, jnp.int32), w1_rows, w1_cols, w2_rows, w2_cols)

        def bind(kernel, *given):
            return functools.partial(kernel, *given)

    def blocks(count, dtype):
        return jax.ShapeDtypeStruct((count, 2, size, size), dtype)

    parts = len(rounds[0]) + 1
    half = nb // parts // 2
    panels = jax.ShapeDtypeStruct((nb, width, size), BF16)
    work = 2 * nb * width * size * size
    act, hgrad, *out = call(
        bind(middle, nb, nw, parts),
        [panels, panels] + [blocks(half, BF16)] * parts + [blocks(half, F32)] * parts,
        lists,
        weights,
        [
            pltpu.VMEM((FB, width, size), F32),
            pltpu.VMEM((FB, width, size), F32),
            pltpu.VMEM((nb, width, size), BF16),
            pltpu.VMEM((nb, width, size), BF16),
            pltpu.SemaphoreType.DMA((2,)),
        ],
        4 * work,
        "middle",
        (tokens, cotangent),
    )
    model = jax.ShapeDtypeStruct((width, depth), BF16)
    total = pltpu.VMEM((depth // size, width, size), F32)
    output, input_grad = call(bind(last, nb, nw), [model, model], lists, [act, hgrad, *weights], [total, total], 2 * work, "last")

    sends, keeps = out[:parts], out[parts:]
    near = rounds[1:][::-1]
    landed = []
    for i in range(parts):
        leaving, held = [sends[i]], keeps[i]
        for now, later in zip(near, [*near[1:], []]):
            arrived = [swap(v, m, n) for v, m in zip(leaving, now)]
            if later or i:
                count = held.shape[0] // (len(later) + 1)
                kept = blocks(count, F32 if later else BF16)
                held, *leaving = call(
                    functools.partial(fold, len(later) + 1),
                    [kept] + [blocks(count, BF16)] * len(later),
                    (),
                    [held, *arrived],
                    name="fold",
                )
        landed += [held, *arrived] if i == 0 else [swap(held, rounds[0][i - 1], n)]
    grad = jax.ShapeDtypeStruct((1, size, size), F32)
    first_grad, second_grad = call(
        functools.partial(close, 1.0 / math.sqrt(width * n)), [grad, grad], (), landed, name="close"
    )
    return (output, input_grad, first_grad, second_grad)


def solution(mesh):
    rows, blocks = P(("grp", "row"), None), P(("grp", "row"), None, None)
    return jax.shard_map(
        body,
        mesh=mesh,
        in_specs=(rows, rows, P("row", None, None), P(), P(), P("row", None, None), P(), P()),
        out_specs=(rows, rows, blocks, blocks),
        check_vma=False,
    )
```

time: 45 us -> 38.8 us (0.86)
  waiting for transfers between devices: 17.5 us -> 8.6 us
  starting transfers between devices: 17 us -> 20.7 us
  local copies, waits for them, and re-layouts: 3.71 us -> 0.79 us
  Pallas kernels: 5.5 us -> 7.38 us
    ppermute x20 -> x26, waiting for transfers between devices: 17.5 us -> 8.6 us  [swap(): return lax.ppermute(value, 'row', [(i, i ^ mask) for i in range(n)])]
    ppermute x20 -> x26, starting transfers between devices: 17 us -> 20.7 us  [swap(): return lax.ppermute(value, 'row', [(i, i ^ mask) for i in range(n)])]
    unnamed x15 -> x11, local copies, waits for them, and re-layouts: 3.05 us -> 0.79 us
    pallas_call x5 -> x10, Pallas kernels: 5.5 us -> 7.38 us  [call(): pl.pallas_call(kernel, out_shape=outs, in_specs=[SMEM] * len(smem) + [ANY...]
    squeeze x1 -> x0, local copies, waits for them, and re-layouts: 0.66 us -> none  [body(): return (output, input_grad, keep[:, 0], keep[:, 1])]
  transfers between devices with their start and end apart: 20 -> 26, of which waited for: 10 -> 11; matrix products, arithmetic and copies ran while one was open for 0% -> 0% of each run, Pallas kernels for 6% -> 7%
where the time goes in v2:
time: 38.8 us; the launch traced here: 38.2 us
  starting transfers between devices  20.7 us (53%)
  waiting for transfers between devices  8.6 us (22%)
  Pallas kernels  7.38 us (19%)
  local copies, waits for them, and re-layouts  0.79 us (2%)
  between operations  0.74 us (2%)
    ppermute x26, starting transfers between devices, swap(): return lax.ppermute(value, 'row', [(i, i ^ mask) for i in range(n)])  20.7 us
    ppermute x26, waiting for transfers between devices, swap(): return lax.ppermute(value, 'row', [(i, i ^ mask) for i in range(n)])  8.6 us
    pallas_call x10, Pallas kernels, call(): pl.pallas_call(kernel, out_shape=outs, in_specs=[SMEM] * len(smem) + [ANY...  7.38 us
    unnamed x11, local copies, waits for them, and re-layouts  0.79 us
  transfers between devices with their start and end apart: 26, of which 11 were waited for; matrix products, arithmetic and copies ran while one was open for 0% of the time, Pallas kernels for 7%

profile of v2, /device:TPU:1, one launch (start us, length us, event | category | flops | bytes accessed | tf_op | source)
XLA Modules:
  0.0 38.2 jit_solution(10781089512365248687)
XLA Ops:
  0.6 0.8 %constant_dynamic-update-slice_fusion.1 = bf16[2,128,128]{2,1,0:T(8,128)(2,1)S(1)} fusion(bf16[1,128,128]{2,1,0:T(8,128)(2,1)} %param.10), kind=kLoop, calls=%fused_computation.1 | loop fusion | bytes 65536
  1.4 2.8 %collective-permute-start = (bf16[2,128,128]{2,1,0:T(8,128)(2,1)S(1)}, bf16[2,128,128]{2,1,0:T(8,128)(2,1)S(1)}, u32[]{:S(2)}, u32[]{:S(2)}) collective-permute-start(bf16[2,128,128]{2,1,0:T(8,128)(2,1)S(1)} %constant_dynamic-update-slice_fusion.refs_2_), channel_id=1, source_target_pairs={{0,5},{1,4},{2,7},{3,6},{4,1},{5,0},{6,3},{7,2},{8,13},{9,12},{10,... | collective-permute-start | bytes 196616 | tf_op jit(solution)/shard_map/ppermute | solution.py:40
  4.2 2.0 %collective-permute-start.1 = (bf16[2,128,128]{2,1,0:T(8,128)(2,1)S(1)}, bf16[2,128,128]{2,1,0:T(8,128)(2,1)S(1)}, u32[]{:S(2)}, u32[]{:S(2)}) collective-permute-start(bf16[2,128,128]{2,1,0:T(8,128)(2,1)S(1)} %constant_dynamic-update-slice_fusion.refs_2_), channel_id=1, source_target_pairs={{0,9},{1,8},{2,11},{3,10},{4,13},{5,12},{6,15},{7,14},{8,1},{9,0},... | collective-permute-start | bytes 196616 | tf_op jit(solution)/shard_map/ppermute | solution.py:40
  6.2 0.2 collective-permute-start.2
  6.4 1.6 %collective-permute-start.3 = (bf16[2,128,128]{2,1,0:T(8,128)(2,1)S(1)}, bf16[2,128,128]{2,1,0:T(8,128)(2,1)S(1)}, u32[]{:S(2)}, u32[]{:S(2)}) collective-permute-start(bf16[2,128,128]{2,1,0:T(8,128)(2,1)S(1)} %constant_dynamic-update-slice_fusion.refs_2_), channel_id=1, source_target_pairs={{0,3},{1,2},{2,1},{3,0},{4,7},{5,6},{6,5},{7,4},{8,11},{9,10},{10,... | collective-permute-start | bytes 196616 | tf_op jit(solution)/shard_map/ppermute | solution.py:40
  8.0 0.3 collective-permute-start.7
  8.3 0.3 collective-permute-start.4
  8.6 1.6 %collective-permute-done.1.refs_4_ = bf16[2,128,128]{2,1,0:T(8,128)(2,1)S(1)} collective-permute-done((bf16[2,128,128]{2,1,0:T(8,128)(2,1)S(1)}, bf16[2,128,128]{2,1,0:T(8,128)(2,1)S(1)}, u32[]{:S(2)}, u32[]{:S(2)}) %collective-permute-start.1) | collective-permute-done | bytes 65568 | tf_op jit(solution)/shard_map/ppermute | solution.py:40
  10.3 0.1 collective-permute-start.5
  10.4 2.3 %collective-permute-done.2.refs_5_ = bf16[2,128,128]{2,1,0:T(8,128)(2,1)S(1)} collective-permute-done((bf16[2,128,128]{2,1,0:T(8,128)(2,1)S(1)}, bf16[2,128,128]{2,1,0:T(8,128)(2,1)S(1)}, u32[]{:S(2)}, u32[]{:S(2)}) %collective-permute-start.2) | collective-permute-done | bytes 65568 | tf_op jit(solution)/shard_map/ppermute | solution.py:40
  12.7 1.6 %collective-permute-start.6 = (bf16[2,128,128]{2,1,0:T(8,128)(2,1)S(1)}, bf16[2,128,128]{2,1,0:T(8,128)(2,1)S(1)}, u32[]{:S(2)}, u32[]{:S(2)}) collective-permute-start(bf16[2,128,128]{2,1,0:T(8,128)(2,1)S(1)} %collective-permute-done.2.refs_5_), channel_id=1, source_target_pairs={{0,3},{1,2},{2,1},{3,0},{4,7},{5,6},{6,5},{7,4},{8,11},{9,10},{10,... | collective-permute-start | bytes 196616 | tf_op jit(solution)/shard_map/ppermute | solution.py:40
  14.3 0.0 collective-permute-done.3.refs_6_
  14.3 0.1 collective-permute-start.10
  14.3 0.5 %collective-permute-start.8 = (bf16[2,128,128]{2,1,0:T(8,128)(2,1)S(1)}, bf16[2,128,128]{2,1,0:T(8,128)(2,1)S(1)}, u32[]{:S(2)}, u32[]{:S(2)}) collective-permute-start(bf16[2,128,128]{2,1,0:T(8,128)(2,1)S(1)} %collective-permute-done.refs_3_), channel_id=1, source_target_pairs={{0,1},{1,0},{2,3},{3,2},{4,5},{5,4},{6,7},{7,6},{8,9},{9,8},{10,11... | collective-permute-start | bytes 196616 | tf_op jit(solution)/shard_map/ppermute | solution.py:40
  14.8 0.0 collective-permute-done.4.refs_7_
  14.8 0.1 collective-permute-start.9
  14.9 0.0 collective-permute-done.5.refs_8_
  14.9 0.4 %collective-permute-start.11 = (bf16[2,128,128]{2,1,0:T(8,128)(2,1)S(1)}, bf16[2,128,128]{2,1,0:T(8,128)(2,1)S(1)}, u32[]{:S(2)}, u32[]{:S(2)}) collective-permute-start(bf16[2,128,128]{2,1,0:T(8,128)(2,1)S(1)} %collective-permute-done.3.refs_6_), channel_id=1, source_target_pairs={{0,1},{1,0},{2,3},{3,2},{4,5},{5,4},{6,7},{7,6},{8,9},{9,8},{10,11... | collective-permute-start | bytes 196616 | tf_op jit(solution)/shard_map/ppermute | solution.py:40
  15.3 1.6 %collective-permute-done.6.refs_9_ = bf16[2,128,128]{2,1,0:T(8,128)(2,1)S(1)} collective-permute-done((bf16[2,128,128]{2,1,0:T(8,128)(2,1)S(1)}, bf16[2,128,128]{2,1,0:T(8,128)(2,1)S(1)}, u32[]{:S(2)}, u32[]{:S(2)}) %collective-permute-start.6) | collective-permute-done | bytes 65568 | tf_op jit(solution)/shard_map/ppermute | solution.py:40
  16.9 0.4 %collective-permute-start.12 = (bf16[2,128,128]{2,1,0:T(8,128)(2,1)S(1)}, bf16[2,128,128]{2,1,0:T(8,128)(2,1)S(1)}, u32[]{:S(2)}, u32[]{:S(2)}) collective-permute-start(bf16[2,128,128]{2,1,0:T(8,128)(2,1)S(1)} %collective-permute-done.4.refs_7_), channel_id=1, source_target_pairs={{0,1},{1,0},{2,3},{3,2},{4,5},{5,4},{6,7},{7,6},{8,9},{9,8},{10,11... | collective-permute-start | bytes 196616 | tf_op jit(solution)/shard_map/ppermute | solution.py:40
  17.3 0.0 collective-permute-done.10.refs_13_
  17.3 0.1 collective-permute-start.13
  17.4 0.0 collective-permute-done.8.refs_11_
  17.4 0.4 %collective-permute-start.14 = (bf16[2,128,128]{2,1,0:T(8,128)(2,1)S(1)}, bf16[2,128,128]{2,1,0:T(8,128)(2,1)S(1)}, u32[]{:S(2)}, u32[]{:S(2)}) collective-permute-start(bf16[2,128,128]{2,1,0:T(8,128)(2,1)S(1)} %collective-permute-done.6.refs_9_), channel_id=1, source_target_pairs={{0,1},{1,0},{2,3},{3,2},{4,5},{5,4},{6,7},{7,6},{8,9},{9,8},{10,11... | collective-permute-start | bytes 196616 | tf_op jit(solution)/shard_map/ppermute | solution.py:40
  17.8 0.0 collective-permute-done.9.refs_12_
  17.8 0.0 collective-permute-done.11.refs_14_
  17.9 0.4 collective-permute-done.12.refs_15_
  18.2 0.4 collective-permute-done.13.refs_16_
  18.6 0.2 collective-permute-done.14.refs_17_
  18.7 3.9 %middle.1 = (bf16[16,128,128]{2,1,0:T(8,128)(2,1)S(1)}, bf16[16,128,128]{2,1,0:T(8,128)(2,1)S(1)}, bf16[2,2,128,128]{3,2,1,0:T(8,128)(2,1)S(1)}, bf16[2,2,128,12...) custom-call(s32[1]{0:T(128)} %bitcast.me, ...), custom_call_target="tpu_custom_call" | custom-call | flops 268435456 | bytes 18350080 | tf_op jit(solution)/shard_map/middle/pallas_call | solution.py:199
  22.7 0.4 %collective-permute-start.23 = (bf16[2,2,128,128]{3,2,1,0:T(8,128)(2,1)S(1)}, bf16[2,2,128,128]{3,2,1,0:T(8,128)(2,1)S(1)}, u32[]{:S(2)}, u32[]{:S(2)}) collective-permute-start(bf16[2,2,128,128]{3,2,1,0:T(8,128)(2,1)S(1)} %get-tuple-element.43), channel_id=1, source_target_pairs={{0,1},{1,0},{2,3},{3,2},{4,5},{5,4},{6,7},{7,6},{8,9},{9,8},{10,11... | collective-permute-start | bytes 393224 | tf_op jit(solution)/shard_map/ppermute | solution.py:40
  23.1 0.1 collective-permute-start.20
  23.3 0.4 collective-permute-start.17
  23.6 0.1 collective-permute-start.15
  23.8 0.3 collective-permute-done.23.refs_0_
  24.1 1.6 %collective-permute-start.24 = (bf16[1,2,128,128]{3,2,1,0:T(8,128)(2,1)S(1)}, bf16[1,2,128,128]{3,2,1,0:T(8,128)(2,1)S(1)}, u32[]{:S(2)}, u32[]{:S(2)}) collective-permute-start(bf16[1,2,128,128]{3,2,1,0:T(8,128)(2,1)S(1)} %get-tuple-element.45), channel_id=1, source_target_pairs={{0,3},{1,2},{2,1},{3,0},{4,7},{5,6},{6,5},{7,4},{8,11},{9,10},{10,... | collective-permute-start | bytes 196616 | tf_op jit(solution)/shard_map/ppermute | solution.py:40
  25.7 0.3 collective-permute-start.21
  26.1 1.5 %collective-permute-start.18 = (bf16[1,2,128,128]{3,2,1,0:T(8,128)(2,1)S(1)}, bf16[1,2,128,128]{3,2,1,0:T(8,128)(2,1)S(1)}, u32[]{:S(2)}, u32[]{:S(2)}) collective-permute-start(bf16[1,2,128,128]{3,2,1,0:T(8,128)(2,1)S(1)} %get-tuple-element.37), channel_id=1, source_target_pairs={{0,3},{1,2},{2,1},{3,0},{4,7},{5,6},{6,5},{7,4},{8,11},{9,10},{10,... | collective-permute-start | bytes 196616 | tf_op jit(solution)/shard_map/ppermute | solution.py:40
  27.7 0.3 collective-permute-start.16
  28.0 0.6 %collective-permute-done.24.refs_0_ = bf16[1,2,128,128]{3,2,1,0:T(8,128)(2,1)S(1)} collective-permute-done((bf16[1,2,128,128]{3,2,1,0:T(8,128)(2,1)S(1)}, bf16[1,2,128,128]{3,2,1,0:T(8,128)(2,1)S(1)}, u32[]{:S(2)}, u32[]{:S(2)}) %collective-permute-start.24) | collective-permute-done | bytes 65568 | tf_op jit(solution)/shard_map/ppermute | solution.py:40
  28.6 2.9 %collective-permute-start.25 = (bf16[1,2,128,128]{3,2,1,0:T(8,128)(2,1)S(1)}, bf16[1,2,128,128]{3,2,1,0:T(8,128)(2,1)S(1)}, u32[]{:S(2)}, u32[]{:S(2)}) collective-permute-start(bf16[1,2,128,128]{3,2,1,0:T(8,128)(2,1)S(1)} %fold.13), channel_id=1, source_target_pairs={{0,13},{1,12},{2,15},{3,14},{4,9},{5,8},{6,11},{7,10},{8,5},{9,4},... | collective-permute-start | bytes 196616 | tf_op jit(solution)/shard_map/ppermute | solution.py:40
  31.5 0.1 collective-permute-start.22
  31.6 0.2 collective-permute-done.18.refs_0_
  31.8 2.1 %collective-permute-start.19 = (bf16[1,2,128,128]{3,2,1,0:T(8,128)(2,1)S(1)}, bf16[1,2,128,128]{3,2,1,0:T(8,128)(2,1)S(1)}, u32[]{:S(2)}, u32[]{:S(2)}) collective-permute-start(bf16[1,2,128,128]{3,2,1,0:T(8,128)(2,1)S(1)} %fold.9), channel_id=1, source_target_pairs={{0,5},{1,4},{2,7},{3,6},{4,1},{5,0},{6,3},{7,2},{8,13},{9,12},{10,... | collective-permute-start | bytes 196616 | tf_op jit(solution)/shard_map/ppermute | solution.py:40
  33.9 2.6 %last.1 = (bf16[128,3072]{1,0:T(8,128)(2,1)}, bf16[128,3072]{1,0:T(8,128)(2,1)}) custom-call(s32[1]{0:T(128)} %bitcast.me, s32[16]{0:T(128)S(1)} %copy-done, s32[16]{0:T(128)S(1)} %copy-done.1, s32[16]{0:T(128)S(1)} %copy-done.2, s32[16]{0:T(128)S(1)} %copy-done.3, bf16[16,128,128]{2,1,0:T(8,128)(2,1)S(1)} %get-tuple-element.26.refs_0_, ...), custom_call_target="tpu_custom_call" | custom-call | flops 134217728 | bytes 6815744 | tf_op jit(solution)/shard_map/last/pallas_call | solution.py:199
  36.5 0.9 %collective-permute-done.22.refs_2_ = bf16[1,2,128,128]{3,2,1,0:T(8,128)(2,1)S(1)} collective-permute-done((bf16[1,2,128,128]{3,2,1,0:T(8,128)(2,1)S(1)}, bf16[1,2,128,128]{3,2,1,0:T(8,128)(2,1)S(1)}, u32[]{:S(2)}, u32[]{:S(2)}) %collective-permute-start.22) | collective-permute-done | bytes 65568 | tf_op jit(solution)/shard_map/ppermute | solution.py:40
  37.4 0.1 collective-permute-done.19.refs_1_
  37.6 0.7 %close.1 = (f32[1,128,128]{2,1,0:T(8,128)}, f32[1,128,128]{2,1,0:T(8,128)}) custom-call(f32[1,2,128,128]{3,2,1,0:T(8,128)S(1)} %get-tuple-element.32.held, bf16[1,2,128,128]{3,2,1,0:T(8,128)(2,1)S(1)} %collective-permute-done.16.refs_0_, bf16[1,2,128,128]{3,2,1,0:T(8,128)(2,1)S(1)} %collective-permute-done.19.refs_1_, ...), custom_call_target="tpu_custom_call" | custom-call | bytes 524288 | tf_op jit(solution)/shard_map/close/pallas_call | solution.py:199
  (26 shorter events, 0.2 us)
Async XLA Ops:
  0.6 0.8 %copy-start.4 = (bf16[1,128,128]{2,1,0:T(8,128)(2,1)S(1)}, bf16[1,128,128]{2,1,0:T(8,128)(2,1)}, u32[]{:S(2)}) copy-start(bf16[1,128,128]{2,1,0:T(8,128)(2,1)} %param.13) | copy-start | bytes 98308
  1.4 6.9 %collective-permute-start = (bf16[2,128,128]{2,1,0:T(8,128)(2,1)S(1)}, bf16[2,128,128]{2,1,0:T(8,128)(2,1)S(1)}, u32[]{:S(2)}, u32[]{:S(2)}) collective-permute-start(bf16[2,128,128]{2,1,0:T(8,128)(2,1)S(1)} %constant_dynamic-update-slice_fusion.refs_2_), channel_id=1, source_target_pairs={{0,5},{1,4},{2,7},{3,6},{4,1},{5,0},{6,3},{7,2},{8,13},{9,12},{10,... | collective-permute-start | bytes 196616 | tf_op jit(solution)/shard_map/ppermute | solution.py:40
  4.2 6.1 %collective-permute-start.1 = (bf16[2,128,128]{2,1,0:T(8,128)(2,1)S(1)}, bf16[2,128,128]{2,1,0:T(8,128)(2,1)S(1)}, u32[]{:S(2)}, u32[]{:S(2)}) collective-permute-start(bf16[2,128,128]{2,1,0:T(8,128)(2,1)S(1)} %constant_dynamic-update-slice_fusion.refs_2_), channel_id=1, source_target_pairs={{0,9},{1,8},{2,11},{3,10},{4,13},{5,12},{6,15},{7,14},{8,1},{9,0},... | collective-permute-start | bytes 196616 | tf_op jit(solution)/shard_map/ppermute | solution.py:40
  6.2 6.5 %collective-permute-start.2 = (bf16[2,128,128]{2,1,0:T(8,128)(2,1)S(1)}, bf16[2,128,128]{2,1,0:T(8,128)(2,1)S(1)}, u32[]{:S(2)}, u32[]{:S(2)}) collective-permute-start(bf16[2,128,128]{2,1,0:T(8,128)(2,1)S(1)} %constant_dynamic-update-slice_fusion.refs_2_), channel_id=1, source_target_pairs={{0,13},{1,12},{2,15},{3,14},{4,9},{5,8},{6,11},{7,10},{8,5},{9,4},... | collective-permute-start | bytes 196616 | tf_op jit(solution)/shard_map/ppermute | solution.py:40
  6.4 7.9 %collective-permute-start.3 = (bf16[2,128,128]{2,1,0:T(8,128)(2,1)S(1)}, bf16[2,128,128]{2,1,0:T(8,128)(2,1)S(1)}, u32[]{:S(2)}, u32[]{:S(2)}) collective-permute-start(bf16[2,128,128]{2,1,0:T(8,128)(2,1)S(1)} %constant_dynamic-update-slice_fusion.refs_2_), channel_id=1, source_target_pairs={{0,3},{1,2},{2,1},{3,0},{4,7},{5,6},{6,5},{7,4},{8,11},{9,10},{10,... | collective-permute-start | bytes 196616 | tf_op jit(solution)/shard_map/ppermute | solution.py:40
  8.0 6.3 %collective-permute-start.7 = (bf16[2,128,128]{2,1,0:T(8,128)(2,1)S(1)}, bf16[2,128,128]{2,1,0:T(8,128)(2,1)S(1)}, u32[]{:S(2)}, u32[]{:S(2)}) collective-permute-start(bf16[2,128,128]{2,1,0:T(8,128)(2,1)S(1)} %constant_dynamic-update-slice_fusion.refs_2_), channel_id=1, source_target_pairs={{0,1},{1,0},{2,3},{3,2},{4,5},{5,4},{6,7},{7,6},{8,9},{9,8},{10,11... | collective-permute-start | bytes 196616 | tf_op jit(solution)/shard_map/ppermute | solution.py:40
  8.3 6.5 %collective-permute-start.4 = (bf16[2,128,128]{2,1,0:T(8,128)(2,1)S(1)}, bf16[2,128,128]{2,1,0:T(8,128)(2,1)S(1)}, u32[]{:S(2)}, u32[]{:S(2)}) collective-permute-start(bf16[2,128,128]{2,1,0:T(8,128)(2,1)S(1)} %collective-permute-done.refs_3_), channel_id=1, source_target_pairs={{0,3},{1,2},{2,1},{3,0},{4,7},{5,6},{6,5},{7,4},{8,11},{9,10},{10,... | collective-permute-start | bytes 196616 | tf_op jit(solution)/shard_map/ppermute | solution.py:40
  10.3 4.6 %collective-permute-start.5 = (bf16[2,128,128]{2,1,0:T(8,128)(2,1)S(1)}, bf16[2,128,128]{2,1,0:T(8,128)(2,1)S(1)}, u32[]{:S(2)}, u32[]{:S(2)}) collective-permute-start(bf16[2,128,128]{2,1,0:T(8,128)(2,1)S(1)} %collective-permute-done.1.refs_4_), channel_id=1, source_target_pairs={{0,3},{1,2},{2,1},{3,0},{4,7},{5,6},{6,5},{7,4},{8,11},{9,10},{10,... | collective-permute-start | bytes 196616 | tf_op jit(solution)/shard_map/ppermute | solution.py:40
  12.7 4.2 %collective-permute-start.6 = (bf16[2,128,128]{2,1,0:T(8,128)(2,1)S(1)}, bf16[2,128,128]{2,1,0:T(8,128)(2,1)S(1)}, u32[]{:S(2)}, u32[]{:S(2)}) collective-permute-start(bf16[2,128,128]{2,1,0:T(8,128)(2,1)S(1)} %collective-permute-done.2.refs_5_), channel_id=1, source_target_pairs={{0,3},{1,2},{2,1},{3,0},{4,7},{5,6},{6,5},{7,4},{8,11},{9,10},{10,... | collective-permute-start | bytes 196616 | tf_op jit(solution)/shard_map/ppermute | solution.py:40
  14.3 3.0 %collective-permute-start.10 = (bf16[2,128,128]{2,1,0:T(8,128)(2,1)S(1)}, bf16[2,128,128]{2,1,0:T(8,128)(2,1)S(1)}, u32[]{:S(2)}, u32[]{:S(2)}) collective-permute-start(bf16[2,128,128]{2,1,0:T(8,128)(2,1)S(1)} %collective-permute-done.2.refs_5_), channel_id=1, source_target_pairs={{0,1},{1,0},{2,3},{3,2},{4,5},{5,4},{6,7},{7,6},{8,9},{9,8},{10,11... | collective-permute-start | bytes 196616 | tf_op jit(solution)/shard_map/ppermute | solution.py:40
  14.3 3.1 %collective-permute-start.8 = (bf16[2,128,128]{2,1,0:T(8,128)(2,1)S(1)}, bf16[2,128,128]{2,1,0:T(8,128)(2,1)S(1)}, u32[]{:S(2)}, u32[]{:S(2)}) collective-permute-start(bf16[2,128,128]{2,1,0:T(8,128)(2,1)S(1)} %collective-permute-done.refs_3_), channel_id=1, source_target_pairs={{0,1},{1,0},{2,3},{3,2},{4,5},{5,4},{6,7},{7,6},{8,9},{9,8},{10,11... | collective-permute-start | bytes 196616 | tf_op jit(solution)/shard_map/ppermute | solution.py:40
  14.8 3.0 %collective-permute-start.9 = (bf16[2,128,128]{2,1,0:T(8,128)(2,1)S(1)}, bf16[2,128,128]{2,1,0:T(8,128)(2,1)S(1)}, u32[]{:S(2)}, u32[]{:S(2)}) collective-permute-start(bf16[2,128,128]{2,1,0:T(8,128)(2,1)S(1)} %collective-permute-done.1.refs_4_), channel_id=1, source_target_pairs={{0,1},{1,0},{2,3},{3,2},{4,5},{5,4},{6,7},{7,6},{8,9},{9,8},{10,11... | collective-permute-start | bytes 196616 | tf_op jit(solution)/shard_map/ppermute | solution.py:40
  14.9 3.0 %collective-permute-start.11 = (bf16[2,128,128]{2,1,0:T(8,128)(2,1)S(1)}, bf16[2,128,128]{2,1,0:T(8,128)(2,1)S(1)}, u32[]{:S(2)}, u32[]{:S(2)}) collective-permute-start(bf16[2,128,128]{2,1,0:T(8,128)(2,1)S(1)} %collective-permute-done.3.refs_6_), channel_id=1, source_target_pairs={{0,1},{1,0},{2,3},{3,2},{4,5},{5,4},{6,7},{7,6},{8,9},{9,8},{10,11... | collective-permute-start | bytes 196616 | tf_op jit(solution)/shard_map/ppermute | solution.py:40
  16.9 1.3 %collective-permute-start.12 = (bf16[2,128,128]{2,1,0:T(8,128)(2,1)S(1)}, bf16[2,128,128]{2,1,0:T(8,128)(2,1)S(1)}, u32[]{:S(2)}, u32[]{:S(2)}) collective-permute-start(bf16[2,128,128]{2,1,0:T(8,128)(2,1)S(1)} %collective-permute-done.4.refs_7_), channel_id=1, source_target_pairs={{0,1},{1,0},{2,3},{3,2},{4,5},{5,4},{6,7},{7,6},{8,9},{9,8},{10,11... | collective-permute-start | bytes 196616 | tf_op jit(solution)/shard_map/ppermute | solution.py:40
  17.3 1.3 %collective-permute-start.13 = (bf16[2,128,128]{2,1,0:T(8,128)(2,1)S(1)}, bf16[2,128,128]{2,1,0:T(8,128)(2,1)S(1)}, u32[]{:S(2)}, u32[]{:S(2)}) collective-permute-start(bf16[2,128,128]{2,1,0:T(8,128)(2,1)S(1)} %collective-permute-done.5.refs_8_), channel_id=1, source_target_pairs={{0,1},{1,0},{2,3},{3,2},{4,5},{5,4},{6,7},{7,6},{8,9},{9,8},{10,11... | collective-permute-start | bytes 196616 | tf_op jit(solution)/shard_map/ppermute | solution.py:40
  17.4 1.3 %collective-permute-start.14 = (bf16[2,128,128]{2,1,0:T(8,128)(2,1)S(1)}, bf16[2,128,128]{2,1,0:T(8,128)(2,1)S(1)}, u32[]{:S(2)}, u32[]{:S(2)}) collective-permute-start(bf16[2,128,128]{2,1,0:T(8,128)(2,1)S(1)} %collective-permute-done.6.refs_9_), channel_id=1, source_target_pairs={{0,1},{1,0},{2,3},{3,2},{4,5},{5,4},{6,7},{7,6},{8,9},{9,8},{10,11... | collective-permute-start | bytes 196616 | tf_op jit(solution)/shard_map/ppermute | solution.py:40
  17.8 0.9 %copy-start.3 = (s32[16]{0:T(128)S(1)}, s32[16]{0:T(128)}, u32[]{:S(2)}) copy-start(s32[16]{0:T(128)} %c2.3) | copy-start | bytes 196
  17.8 0.9 %copy-start = (s32[16]{0:T(128)S(1)}, s32[16]{0:T(128)}, u32[]{:S(2)}) copy-start(s32[16]{0:T(128)} %r1.3) | copy-start | bytes 196
  17.8 0.9 %copy-start.1 = (s32[16]{0:T(128)S(1)}, s32[16]{0:T(128)}, u32[]{:S(2)}) copy-start(s32[16]{0:T(128)} %c1.3) | copy-start | bytes 196
  17.8 0.9 %copy-start.2 = (s32[16]{0:T(128)S(1)}, s32[16]{0:T(128)}, u32[]{:S(2)}) copy-start(s32[16]{0:T(128)} %r2.3) | copy-start | bytes 196
  22.7 1.4 %collective-permute-start.23 = (bf16[2,2,128,128]{3,2,1,0:T(8,128)(2,1)S(1)}, bf16[2,2,128,128]{3,2,1,0:T(8,128)(2,1)S(1)}, u32[]{:S(2)}, u32[]{:S(2)}) collective-permute-start(bf16[2,2,128,128]{3,2,1,0:T(8,128)(2,1)S(1)} %get-tuple-element.43), channel_id=1, source_target_pairs={{0,1},{1,0},{2,3},{3,2},{4,5},{5,4},{6,7},{7,6},{8,9},{9,8},{10,11... | collective-permute-start | bytes 393224 | tf_op jit(solution)/shard_map/ppermute | solution.py:40
  23.1 2.6 %collective-permute-start.20 = (bf16[2,2,128,128]{3,2,1,0:T(8,128)(2,1)S(1)}, bf16[2,2,128,128]{3,2,1,0:T(8,128)(2,1)S(1)}, u32[]{:S(2)}, u32[]{:S(2)}) collective-permute-start(bf16[2,2,128,128]{3,2,1,0:T(8,128)(2,1)S(1)} %get-tuple-element.39), channel_id=1, source_target_pairs={{0,1},{1,0},{2,3},{3,2},{4,5},{5,4},{6,7},{7,6},{8,9},{9,8},{10,11... | collective-permute-start | bytes 393224 | tf_op jit(solution)/shard_map/ppermute | solution.py:40
  23.3 2.8 %collective-permute-start.17 = (bf16[2,2,128,128]{3,2,1,0:T(8,128)(2,1)S(1)}, bf16[2,2,128,128]{3,2,1,0:T(8,128)(2,1)S(1)}, u32[]{:S(2)}, u32[]{:S(2)}) collective-permute-start(bf16[2,2,128,128]{3,2,1,0:T(8,128)(2,1)S(1)} %get-tuple-element.35), channel_id=1, source_target_pairs={{0,1},{1,0},{2,3},{3,2},{4,5},{5,4},{6,7},{7,6},{8,9},{9,8},{10,11... | collective-permute-start | bytes 393224 | tf_op jit(solution)/shard_map/ppermute | solution.py:40
  23.6 4.0 %collective-permute-start.15 = (bf16[2,2,128,128]{3,2,1,0:T(8,128)(2,1)S(1)}, bf16[2,2,128,128]{3,2,1,0:T(8,128)(2,1)S(1)}, u32[]{:S(2)}, u32[]{:S(2)}) collective-permute-start(bf16[2,2,128,128]{3,2,1,0:T(8,128)(2,1)S(1)} %get-tuple-element.31), channel_id=1, source_target_pairs={{0,1},{1,0},{2,3},{3,2},{4,5},{5,4},{6,7},{7,6},{8,9},{9,8},{10,11... | collective-permute-start | bytes 393224 | tf_op jit(solution)/shard_map/ppermute | solution.py:40
  24.1 4.4 %collective-permute-start.24 = (bf16[1,2,128,128]{3,2,1,0:T(8,128)(2,1)S(1)}, bf16[1,2,128,128]{3,2,1,0:T(8,128)(2,1)S(1)}, u32[]{:S(2)}, u32[]{:S(2)}) collective-permute-start(bf16[1,2,128,128]{3,2,1,0:T(8,128)(2,1)S(1)} %get-tuple-element.45), channel_id=1, source_target_pairs={{0,3},{1,2},{2,1},{3,0},{4,7},{5,6},{6,5},{7,4},{8,11},{9,10},{10,... | collective-permute-start | bytes 196616 | tf_op jit(solution)/shard_map/ppermute | solution.py:40
  25.7 5.8 %collective-permute-start.21 = (bf16[1,2,128,128]{3,2,1,0:T(8,128)(2,1)S(1)}, bf16[1,2,128,128]{3,2,1,0:T(8,128)(2,1)S(1)}, u32[]{:S(2)}, u32[]{:S(2)}) collective-permute-start(bf16[1,2,128,128]{3,2,1,0:T(8,128)(2,1)S(1)} %get-tuple-element.41), channel_id=1, source_target_pairs={{0,3},{1,2},{2,1},{3,0},{4,7},{5,6},{6,5},{7,4},{8,11},{9,10},{10,... | collective-permute-start | bytes 196616 | tf_op jit(solution)/shard_map/ppermute | solution.py:40
  26.1 5.7 %collective-permute-start.18 = (bf16[1,2,128,128]{3,2,1,0:T(8,128)(2,1)S(1)}, bf16[1,2,128,128]{3,2,1,0:T(8,128)(2,1)S(1)}, u32[]{:S(2)}, u32[]{:S(2)}) collective-permute-start(bf16[1,2,128,128]{3,2,1,0:T(8,128)(2,1)S(1)} %get-tuple-element.37), channel_id=1, source_target_pairs={{0,3},{1,2},{2,1},{3,0},{4,7},{5,6},{6,5},{7,4},{8,11},{9,10},{10,... | collective-permute-start | bytes 196616 | tf_op jit(solution)/shard_map/ppermute | solution.py:40
  27.7 8.9 %collective-permute-start.16 = (bf16[1,2,128,128]{3,2,1,0:T(8,128)(2,1)S(1)}, bf16[1,2,128,128]{3,2,1,0:T(8,128)(2,1)S(1)}, u32[]{:S(2)}, u32[]{:S(2)}) collective-permute-start(bf16[1,2,128,128]{3,2,1,0:T(8,128)(2,1)S(1)} %get-tuple-element.33), channel_id=1, source_target_pairs={{0,3},{1,2},{2,1},{3,0},{4,7},{5,6},{6,5},{7,4},{8,11},{9,10},{10,... | collective-permute-start | bytes 196616 | tf_op jit(solution)/shard_map/ppermute | solution.py:40
  28.6 8.0 %collective-permute-start.25 = (bf16[1,2,128,128]{3,2,1,0:T(8,128)(2,1)S(1)}, bf16[1,2,128,128]{3,2,1,0:T(8,128)(2,1)S(1)}, u32[]{:S(2)}, u32[]{:S(2)}) collective-permute-start(bf16[1,2,128,128]{3,2,1,0:T(8,128)(2,1)S(1)} %fold.13), channel_id=1, source_target_pairs={{0,13},{1,12},{2,15},{3,14},{4,9},{5,8},{6,11},{7,10},{8,5},{9,4},... | collective-permute-start | bytes 196616 | tf_op jit(solution)/shard_map/ppermute | solution.py:40
  31.5 6.0 %collective-permute-start.22 = (bf16[1,2,128,128]{3,2,1,0:T(8,128)(2,1)S(1)}, bf16[1,2,128,128]{3,2,1,0:T(8,128)(2,1)S(1)}, u32[]{:S(2)}, u32[]{:S(2)}) collective-permute-start(bf16[1,2,128,128]{3,2,1,0:T(8,128)(2,1)S(1)} %fold.11), channel_id=1, source_target_pairs={{0,9},{1,8},{2,11},{3,10},{4,13},{5,12},{6,15},{7,14},{8,1},{9,0},... | collective-permute-start | bytes 196616 | tf_op jit(solution)/shard_map/ppermute | solution.py:40
  31.8 5.8 %collective-permute-start.19 = (bf16[1,2,128,128]{3,2,1,0:T(8,128)(2,1)S(1)}, bf16[1,2,128,128]{3,2,1,0:T(8,128)(2,1)S(1)}, u32[]{:S(2)}, u32[]{:S(2)}) collective-permute-start(bf16[1,2,128,128]{3,2,1,0:T(8,128)(2,1)S(1)} %fold.9), channel_id=1, source_target_pairs={{0,5},{1,4},{2,7},{3,6},{4,1},{5,0},{6,3},{7,2},{8,13},{9,12},{10,... | collective-permute-start | bytes 196616 | tf_op jit(solution)/shard_map/ppermute | solution.py:40

commit v3 on v2

--- a/solution.py
+++ b/solution.py
@@ -9,6 +9,11 @@
 from jax.sharding import PartitionSpec as P
 
 FB = 96
+BEGIN_FLOPS = 10**10
+CHUNK = 6
+PRE_SLOT = 3
+TIE = 1
+EARLY = 4
 ROOT = math.sqrt(2.0 / math.pi)
 CUBE = 0.044715
 F32 = jnp.float32
@@ -18,20 +23,37 @@
 SMEM = pl.BlockSpec(memory_space=pltpu.SMEM)
 
 
-def stages(n):
-    bits = [1 << i for i in range(1, n.bit_length() - 1)]
-    rounds = []
-    if len(bits) % 2:
-        rounds.append([bits.pop(0) | 1])
-    while bits:
-        low, high = bits.pop(0), bits.pop(0)
-        rounds.append([low | 1, high | 1, low | high | 1])
-    return rounds[::-1] + [[1]]
-
-
-def slots(n):
+GATHER = [[9, 5, 13], [3], [1]]
+EXCHANGE = [[9, 5, 13], [3], [1]]
+
+
+def bits(n):
+    return [(1 << i) | 1 for i in range(n.bit_length() - 2, 0, -1)]
+
+
+def gather_rounds(n):
+    if GATHER and n == 16:
+        return GATHER
+    return [[b] for b in bits(n)] + [[1]]
+
+
+def exchange_rounds(n):
+    if EXCHANGE and n == 16:
+        return EXCHANGE
+    far, rounds = bits(n), []
+    while far:
+        a, far = far[0], far[1:]
+        masks = [a]
+        if far:
+            b, far = far[0], far[1:]
+            masks = [a, b, a ^ b]
+        rounds.append(masks)
+    return rounds + [[1]]
+
+
+def slots(rounds):
     order = [0]
-    for masks in stages(n):
+    for masks in rounds:
         order = order + [o ^ m for m in masks for o in order]
     return order
 
@@ -48,17 +70,20 @@
     return lax.dot_general(a, b, (dims, ((), ())), preferred_element_type=F32)
 
 
-def tanh_of(v):
-    return jnp.tanh(ROOT * (v + CUBE * (v * v * v)))
+def tanh_of(v, u):
+    return jnp.tanh(v * (ROOT + ROOT * CUBE * u))
 
 
 def gelu(v):
-    return 0.5 * v * (1.0 + tanh_of(v))
+    h = 0.5 * v
+    return h + h * tanh_of(v, v * v)
 
 
 def gelu_slope(v):
-    t = tanh_of(v)
-    return 0.5 * (1.0 + t) + 0.5 * v * (1.0 - t * t) * (ROOT * (1.0 + 3.0 * CUBE * (v * v)))
+    u = v * v
+    t = tanh_of(v, u)
+    g = 0.5 + 0.5 * t
+    return g + (g * (1.0 - t)) * (v * (ROOT + 3.0 * ROOT * CUBE * u))
 
 
 def each(count, run):
@@ -81,8 +106,19 @@
         self.c2 = lambda s: c2[self.block(s)]
 
 
-def middle(nb, nw, parts, me, order, r1, c1, r2, c2, tokens, cot, *refs):
-    weights, (act, hgrad, *out), (hidden, agrad, tok, ct, sems) = refs[:nw], refs[nw:-5], refs[-5:]
+def begin(w1, w2, weights, sems):
+    copies = [
+        pltpu.make_async_copy(w1, weights.at[pl.ds(0, 1)], sems.at[0]),
+        pltpu.make_async_copy(w2, weights.at[pl.ds(1, 1)], sems.at[1]),
+    ]
+    for copy in copies:
+        copy.start()
+    for copy in copies:
+        copy.wait()
+
+
+def middle(nb, nw, parts, place, me, order, r1, c1, r2, c2, tokens, cot, *refs):
+    weights, (act, hgrad, *out), (hidden, agrad) = refs[:nw], refs[nw:-2], refs[-2:]
     sends, keeps = out[:parts], out[parts:]
     at = Lists(me, order, r1, c1, r2, c2)
     size = act.shape[-1]
@@ -92,12 +128,6 @@
     def w(s, which):
         return weights[s][which] if nw > 1 else weights[0][s, which]
 
-    def begin(s):
-        pltpu.make_async_copy(panel(tokens.at, at.r1(s), size), tok.at[s], sems.at[0]).start()
-        pltpu.make_async_copy(panel(cot.at, at.c2(s), size), ct.at[s], sems.at[1]).start()
-
-    each(nb, begin)
-
     def clear(s):
         zero = jnp.zeros(hidden.shape[1:], F32)
         for index in (at.c1(s), at.r2(s)):
@@ -106,16 +136,14 @@
 
     each(nb, clear)
 
-    pltpu.make_async_copy(tok, tok, sems.at[0]).wait()
 
     def first(s):
-        hidden[at.c1(s)] += dot(tok[s], w(s, 0), ((1,), (0,)))
+        hidden[at.c1(s)] += dot(panel(tokens, at.r1(s), size), w(s, 0), ((1,), (0,)))
 
     each(nb, first)
-    pltpu.make_async_copy(ct, ct, sems.at[1]).wait()
 
     def second(s):
-        agrad[at.r2(s)] += dot(ct[s], w(s, 1), ((1,), (1,)))
+        agrad[at.r2(s)] += dot(panel(cot, at.c2(s), size), w(s, 1), ((1,), (1,)))
 
     each(nb, second)
 
@@ -141,13 +169,96 @@
 
     def grads(i, q):
         s = i + parts * q
+        s = place[s] if isinstance(q, int) else s
         activate(s)
         slope(s)
-        put(i, q, 0, dot(tok[s], hgrad[s], ((0,), (0,))))
-        put(i, q, 1, dot(act[s], ct[s], ((0,), (0,))))
+        put(i, q, 0, dot(panel(tokens, at.r1(s), size), hgrad[s], ((0,), (0,))))
+        put(i, q, 1, dot(act[s], panel(cot, at.c2(s), size), ((0,), (0,))))
 
     for i in range(parts):
         each(rest, functools.partial(grads, i))
+
+
+def finish(nb, table, act, hgrad, *refs):
+    weights, (out, igrad, oacc, iacc, ostage, istage, sems) = refs[:nb], refs[nb:]
+    size = act.shape[-1]
+    count = oacc.shape[0]
+    oacc[...] = jnp.zeros_like(oacc)
+    iacc[...] = jnp.zeros_like(iacc)
+    for s in range(nb):
+        oacc[table[3, s]] += dot(act[s], weights[s][1], ((1,), (0,)))
+        iacc[table[2, s]] += dot(hgrad[s], weights[s][0], ((1,), (1,)))
+    copies = []
+    for acc, stage, target in ((oacc, ostage, out), (iacc, istage, igrad)):
+        for d in range(0, count, CHUNK):
+            for e in range(d, d + CHUNK):
+                stage[:, e * size:(e + 1) * size] = acc[e].astype(BF16)
+            at = (slice(None), pl.ds(d * size, CHUNK * size))
+            copies.append(pltpu.make_async_copy(stage.at[at], target.at[at], sems.at[len(copies)]))
+            copies[-1].start()
+    for copy in copies:
+        copy.wait()
+
+
+def ready(nb, order, me, r1, c1, r2, c2, tokens, cot, piece, *refs):
+    weights, (passed, hidden, agrad, tok, tok_t, ct, ct_t, table) = refs[:-8], refs[-8:]
+    del piece, passed
+    at = Lists(me, order, r1, c1, r2, c2)
+    size = tok.shape[-1]
+    zero = jnp.zeros(hidden.shape[1:], F32)
+    for s in range(nb):
+        hidden[at.c1(s)] = zero
+        hidden[at.r2(s)] = zero
+        agrad[at.c1(s)] = zero
+        agrad[at.r2(s)] = zero
+    lane = lax.broadcasted_iota(jnp.int32, table.shape, 1)
+    row = lax.broadcasted_iota(jnp.int32, table.shape, 0)
+    entries = jnp.zeros(table.shape, jnp.int32)
+    for s in range(nb):
+        value = jnp.where(row < 2, jnp.where(row == 0, at.c1(s), at.r2(s)), jnp.where(row == 2, at.r1(s), at.c2(s)))
+        entries = jnp.where(lane == s, value, entries)
+    table[...] = entries
+    for s in range(nb):
+        value = panel(tokens, at.r1(s), size)
+        tok[s] = value
+        tok_t[s] = value.T
+        value = panel(cot, at.c2(s), size)
+        ct[s] = value
+        ct_t[s] = value.T
+    for s, w in enumerate(weights):
+        hidden[at.c1(s)] += dot(tok[s], w[0], ((1,), (0,)))
+        agrad[at.r2(s)] += dot(ct[s], w[1], ((1,), (1,)))
+
+
+def core(nb, parts, place, table, hidden_in, agrad_in, tok, tok_t, ct, ct_t, *refs):
+    late, (hidden, agrad, act, hgrad, *out, prod, prod_t) = refs[:-6 - 2 * parts], refs[-6 - 2 * parts:]
+    del hidden_in, agrad_in
+    sends, keeps = out[:parts], out[parts:]
+    ne = nb - len(late)
+    for i, w in enumerate(late):
+        prod[i] = dot(tok[ne + i], w[0], ((1,), (0,)))
+        prod_t[i] = dot(ct[ne + i], w[1], ((1,), (1,)))
+    c1 = [table[0, s] for s in range(nb)]
+    r2 = [table[1, s] for s in range(nb)]
+    for i in range(len(late)):
+        hidden[c1[ne + i]] += prod[i]
+    for i in range(len(late)):
+        agrad[r2[ne + i]] += prod_t[i]
+    half = nb // parts // 2
+
+    def put(e, which, value):
+        i, q = e % parts, e // parts
+        if q < half:
+            keeps[i][q, which] = value
+        else:
+            sends[i][q - half, which] = value.astype(BF16)
+
+    for s in range(nb):
+        act[s] = gelu(hidden[r2[s]]).astype(BF16)
+        hgrad[s] = (agrad[c1[s]] * gelu_slope(hidden[c1[s]])).astype(BF16)
+    for e, s in enumerate(place):
+        put(e, 0, dot(tok_t[s], hgrad[s], ((1,), (0,))))
+        put(e, 1, dot(ct_t[s], act[s], ((1,), (0,))))
 
 
 def last(nb, nw, me, order, r1, c1, r2, c2, act, hgrad, *refs):
@@ -184,28 +295,40 @@
         each(count, one)
 
 
-def close(scale, held, *refs):
+def close(scale, turned, held, *refs):
     arrived, outs = refs[:-2], refs[-2:]
     for which, out in enumerate(outs):
         value = held[0, which]
         for a in arrived:
             value = value + a[0, which].astype(F32)
-        out[0] = value * scale
-
-
-def call(kernel, outs, smem, args, scratch=(), flops=0, name=None, any_args=()):
+        value = value * scale
+        out[0] = value.T if which == turned else value
+
+
+def copy_after(value, other, out):
+    del other
+    out[...] = value[...]
+
+
+def after(value, other):
+    return call(copy_after, [jax.ShapeDtypeStruct(value.shape, value.dtype)], (), [value, other], (), BEGIN_FLOPS, "after")[0]
+
+
+def call(kernel, outs, smem, args, scratch=(), flops=0, name=None, hbm_args=(), any_args=(), aliases=(), hbm_outs=False):
     size = sum(math.prod(a.shape) * a.dtype.itemsize for a in (*args, *outs))
-    size += sum(math.prod(s.shape) * 4 for s in scratch[:4])
+    size += sum(math.prod(s.shape) * 4 for s in scratch)
+    first = len(smem) + len(hbm_args) + len(any_args)
     return pl.pallas_call(
         kernel,
         out_shape=outs,
-        in_specs=[SMEM] * len(smem) + [ANY] * len(any_args) + [VMEM] * len(args),
-        out_specs=[VMEM] * len(outs),
+        in_specs=[SMEM] * len(smem) + [ANY] * (len(hbm_args) + len(any_args)) + [VMEM] * len(args),
+        out_specs=[ANY if hbm_outs else VMEM] * len(outs),
         scratch_shapes=list(scratch),
+        input_output_aliases={first + i: o for i, o in aliases},
         compiler_params=pltpu.CompilerParams(vmem_limit_bytes=min(size + (4 << 20), 60 << 20)),
         cost_estimate=pl.CostEstimate(flops=flops, bytes_accessed=size, transcendentals=0),
         name=name,
-    )(*smem, *[pltpu.with_memory_space_constraint(a, pltpu.HBM) for a in any_args], *args)
+    )(*smem, *[pltpu.with_memory_space_constraint(a, pltpu.HBM) for a in hbm_args], *any_args, *args)
 
 
 def body(tokens, cotangent, w1_blocks, w1_rows, w1_cols, w2_blocks, w2_rows, w2_cols):
@@ -213,13 +336,41 @@
     nb = w1_rows.shape[0]
     width, depth = tokens.shape
     size = w1_blocks.shape[-1]
-    order = slots(n)
-    rounds = stages(n)
+    order = slots(gather_rounds(n))
+    rounds = exchange_rounds(n)
+    place = [order.index(o) for o in slots(rounds)]
     me = lax.axis_index("row").astype(jnp.int32).reshape(1)
 
-    pieces = [jnp.concatenate([w1_blocks, w2_blocks], 0)]
-    for masks in rounds:
-        pieces = pieces + [swap(p, m, n) for m in masks for p in pieces]
+    (own,) = call(
+        begin,
+        [jax.ShapeDtypeStruct((2, size, size), BF16)],
+        (),
+        (),
+        [pltpu.SemaphoreType.DMA((2,))],
+        0,
+        "begin",
+        (w1_blocks, w2_blocks),
+    )
+    fast = n <= 16
+    panels = jax.ShapeDtypeStruct((nb, width, size), BF16)
+    units = jax.ShapeDtypeStruct((FB, width, size), F32)
+    pieces = [own]
+    for masks in gather_rounds(n)[:-1]:
+        moving = list(pieces)
+        if fast and TIE and len(pieces) > 1:
+            moving[0] = after(pieces[0], pieces[TIE])
+        pieces = pieces + [swap(p, m, n) for m in masks for p in moving]
+    moved = list(pieces)
+    if fast:
+        moved[PRE_SLOT], hidden, agrad, tok, tok_t, ct, ct_t, table = call(
+            functools.partial(ready, nb, order),
+            [jax.ShapeDtypeStruct(own.shape, BF16), units, units, panels, panels, panels, panels, jax.ShapeDtypeStruct((8, 128), jnp.int32)],
+            (me, w1_rows, w1_cols, w2_rows, w2_cols),
+            [tokens, cotangent, pieces[PRE_SLOT], *pieces[:EARLY]],
+            name="ready",
+            aliases=((2, 0),),
+        )
+    pieces = pieces + [swap(p, 1, n) for p in moved]
     weights = pieces if n <= 16 else [jnp.stack(pieces)]
     nw = len(weights)
     if n <= 16:
@@ -228,6 +379,7 @@
         def bind(kernel, *given):
             return lambda me, r1, c1, r2, c2, *refs: kernel(*given, me, order, r1, c1, r2, c2, *refs)
     else:
+        assert place == list(range(nb))
         lists = (me, jnp.asarray(order, jnp.int32), w1_rows, w1_cols, w2_rows, w2_cols)
 
         def bind(kernel, *given):
@@ -238,27 +390,49 @@
 
     parts = len(rounds[0]) + 1
     half = nb // parts // 2
-    panels = jax.ShapeDtypeStruct((nb, width, size), BF16)
     work = 2 * nb * width * size * size
-    act, hgrad, *out = call(
-        bind(middle, nb, nw, parts),
-        [panels, panels] + [blocks(half, BF16)] * parts + [blocks(half, F32)] * parts,
-        lists,
-        weights,
-        [
-            pltpu.VMEM((FB, width, size), F32),
-            pltpu.VMEM((FB, width, size), F32),
-            pltpu.VMEM((nb, width, size), BF16),
-            pltpu.VMEM((nb, width, size), BF16),
-            pltpu.SemaphoreType.DMA((2,)),
-        ],
-        4 * work,
-        "middle",
-        (tokens, cotangent),
-    )
+    outs = [panels, panels] + [blocks(half, BF16)] * parts + [blocks(half, F32)] * parts
+    if fast:
+        late = nb - EARLY
+        _, _, act, hgrad, *out = call(
+            functools.partial(core, nb, parts, place),
+            [units, units, *outs],
+            (),
+            [table, hidden, agrad, tok, tok_t, ct, ct_t, *pieces[EARLY:]],
+            [
+                pltpu.VMEM((late, width, size), F32),
+                pltpu.VMEM((late, width, size), F32),
+            ],
+            4 * work,
+            "middle",
+            aliases=((1, 0), (2, 1)),
+        )
+    else:
+        act, hgrad, *out = call(
+            bind(middle, nb, nw, parts, place),
+            outs,
+            lists,
+            [tokens, cotangent, *weights],
+            [pltpu.VMEM((FB, width, size), F32), pltpu.VMEM((FB, width, size), F32)],
+            4 * work,
+            "middle",
+        )
     model = jax.ShapeDtypeStruct((width, depth), BF16)
     total = pltpu.VMEM((depth // size, width, size), F32)
-    output, input_grad = call(bind(last, nb, nw), [model, model], lists, [act, hgrad, *weights], [total, total], 2 * work, "last")
+    if fast:
+        stage = pltpu.VMEM((width, depth), BF16)
+        output, input_grad = call(
+            functools.partial(finish, nb),
+            [model, model],
+            (),
+            [table, act, hgrad, *weights],
+            [total, total, stage, stage, pltpu.SemaphoreType.DMA((2 * (depth // size // CHUNK),))],
+            2 * work,
+            "last",
+            hbm_outs=True,
+        )
+    else:
+        output, input_grad = call(bind(last, nb, nw), [model, model], lists, [act, hgrad, *weights], [total, total], 2 * work, "last")
 
     sends, keeps = out[:parts], out[parts:]
     near = rounds[1:][::-1]
@@ -280,7 +454,7 @@
         landed += [held, *arrived] if i == 0 else [swap(held, rounds[0][i - 1], n)]
     grad = jax.ShapeDtypeStruct((1, size, size), F32)
     first_grad, second_grad = call(
-        functools.partial(close, 1.0 / math.sqrt(width * n)), [grad, grad], (), landed, name="close"
+        functools.partial(close, 1.0 / math.sqrt(width * n), 1 if fast else -1), [grad, grad], (), landed, name="close"
     )
     return (output, input_grad, first_grad, second_grad)
 

time: 38.8 us -> 37.5 us (0.966)
  starting transfers between devices: 20.7 us -> 22.4 us
  waiting for transfers between devices: 8.6 us -> 7.15 us
  local copies, waits for them, and re-layouts: 0.79 us -> 0.04 us
  Pallas kernels: 7.38 us -> 6.89 us
    ppermute x26, starting transfers between devices: 20.7 us -> 22.4 us  [swap(): return lax.ppermute(value, 'row', [(i, i ^ mask) for i in range(n)])]
    ppermute x26, waiting for transfers between devices: 8.6 us -> 7.15 us  [swap(): return lax.ppermute(value, 'row', [(i, i ^ mask) for i in range(n)])]
    unnamed x11 -> x13, local copies, waits for them, and re-layouts: 0.79 us -> 0.04 us
    pallas_call x10 -> x13, Pallas kernels: 7.38 us -> 6.89 us  [call(): pl.pallas_call(kernel, out_shape=outs, in_specs=[SMEM] * len(smem) + [ANY...]
  transfers between devices with their start and end apart: 26 -> 26, of which waited for: 11 -> 7; matrix products, arithmetic and copies ran while one was open for 0% -> 0% of each run, Pallas kernels for 7% -> 10%
where the time goes in v3:
time: 37.5 us; the launch traced here: 37.3 us
  starting transfers between devices  22.4 us (60%)
  waiting for transfers between devices  7.15 us (19%)
  Pallas kernels  6.89 us (18%)
  between operations  0.84 us (2%)
    ppermute x26, starting transfers between devices, swap(): return lax.ppermute(value, 'row', [(i, i ^ mask) for i in range(n)])  22.4 us
    ppermute x26, waiting for transfers between devices, swap(): return lax.ppermute(value, 'row', [(i, i ^ mask) for i in range(n)])  7.15 us
    pallas_call x13, Pallas kernels, call(): pl.pallas_call(kernel, out_shape=outs, in_specs=[SMEM] * len(smem) + [ANY...  6.89 us
  transfers between devices with their start and end apart: 26, of which 7 were waited for; matrix products, arithmetic and copies ran while one was open for 0% of the time, Pallas kernels for 10%

profile of v3, /device:TPU:1, one launch (start us, length us, event | category | flops | bytes accessed | tf_op | source)
XLA Modules:
  0.0 37.3 jit_solution(9720342953063015355)
XLA Ops:
  0.6 0.8 %begin.1.refs_0_.value = bf16[2,128,128]{2,1,0:T(8,128)(2,1)S(1)} custom-call(bf16[1,128,128]{2,1,0:T(8,128)(2,1)} %w1.1, bf16[1,128,128]{2,1,0:T(8,128)(2,1)} %w2.1), custom_call_target="tpu_custom_call" | custom-call | bytes 65544 | tf_op jit(solution)/shard_map/begin/pallas_call | solution.py:321
  1.4 0.0 copy-start
  1.4 0.0 copy-start.1
  1.5 0.0 copy-start.2
  1.5 0.0 copy-start.3
  1.5 0.0 copy-start.4
  1.5 0.0 copy-start.5
  1.5 2.8 %collective-permute-start.2 = (bf16[2,128,128]{2,1,0:T(8,128)(2,1)S(1)}, bf16[2,128,128]{2,1,0:T(8,128)(2,1)S(1)}, u32[]{:S(2)}, u32[]{:S(2)}) collective-permute-start(bf16[2,128,128]{2,1,0:T(8,128)(2,1)S(1)} %begin.1.refs_0_.value), channel_id=1, source_target_pairs={{0,5},{1,4},{2,7},{3,6},{4,1},{5,0},{6,3},{7,2},{8,13},{9,12},{10,... | collective-permute-start | bytes 196616 | tf_op jit(solution)/shard_map/ppermute | solution.py:62
  4.3 2.0 %collective-permute-start.1 = (bf16[2,128,128]{2,1,0:T(8,128)(2,1)S(1)}, bf16[2,128,128]{2,1,0:T(8,128)(2,1)S(1)}, u32[]{:S(2)}, u32[]{:S(2)}) collective-permute-start(bf16[2,128,128]{2,1,0:T(8,128)(2,1)S(1)} %begin.1.refs_0_.value), channel_id=1, source_target_pairs={{0,9},{1,8},{2,11},{3,10},{4,13},{5,12},{6,15},{7,14},{8,1},{9,0},... | collective-permute-start | bytes 196616 | tf_op jit(solution)/shard_map/ppermute | solution.py:62
  6.3 0.7 %collective-permute-start.7 = (bf16[2,128,128]{2,1,0:T(8,128)(2,1)S(1)}, bf16[2,128,128]{2,1,0:T(8,128)(2,1)S(1)}, u32[]{:S(2)}, u32[]{:S(2)}) collective-permute-start(bf16[2,128,128]{2,1,0:T(8,128)(2,1)S(1)} %begin.1.refs_0_.value), channel_id=1, source_target_pairs={{0,1},{1,0},{2,3},{3,2},{4,5},{5,4},{6,7},{7,6},{8,9},{9,8},{10,11... | collective-permute-start | bytes 196616 | tf_op jit(solution)/shard_map/ppermute | solution.py:62
  7.0 0.1 collective-permute-start.9
  7.0 1.6 %collective-permute-start.5 = (bf16[2,128,128]{2,1,0:T(8,128)(2,1)S(1)}, bf16[2,128,128]{2,1,0:T(8,128)(2,1)S(1)}, u32[]{:S(2)}, u32[]{:S(2)}) collective-permute-start(bf16[2,128,128]{2,1,0:T(8,128)(2,1)S(1)} %collective-permute-done.2.refs_2_), channel_id=1, source_target_pairs={{0,3},{1,2},{2,1},{3,0},{4,7},{5,6},{6,5},{7,4},{8,11},{9,10},{10,... | collective-permute-start | bytes 196616 | tf_op jit(solution)/shard_map/ppermute | solution.py:62
  8.6 1.7 %collective-permute-done.1.refs_1_.other = bf16[2,128,128]{2,1,0:T(8,128)(2,1)S(1)} collective-permute-done((bf16[2,128,128]{2,1,0:T(8,128)(2,1)S(1)}, bf16[2,128,128]{2,1,0:T(8,128)(2,1)S(1)}, u32[]{:S(2)}, u32[]{:S(2)}) %collective-permute-start.1) | collective-permute-done | bytes 65568 | tf_op jit(solution)/shard_map/ppermute | solution.py:62
  10.3 0.1 collective-permute-start.3
  10.5 0.0 collective-permute-done.7.refs_4_.refs_8_
  10.5 1.5 %collective-permute-start.8 = (bf16[2,128,128]{2,1,0:T(8,128)(2,1)S(1)}, bf16[2,128,128]{2,1,0:T(8,128)(2,1)S(1)}, u32[]{:S(2)}, u32[]{:S(2)}) collective-permute-start(bf16[2,128,128]{2,1,0:T(8,128)(2,1)S(1)} %collective-permute-done.1.refs_1_.other), channel_id=1, source_target_pairs={{0,1},{1,0},{2,3},{3,2},{4,5},{5,4},{6,7},{7,6},{8,9},{9,8},{10,11... | collective-permute-start | bytes 196616 | tf_op jit(solution)/shard_map/ppermute | solution.py:62
  12.0 0.6 %collective-permute-done.refs_3_ = bf16[2,128,128]{2,1,0:T(8,128)(2,1)S(1)} collective-permute-done((bf16[2,128,128]{2,1,0:T(8,128)(2,1)S(1)}, bf16[2,128,128]{2,1,0:T(8,128)(2,1)S(1)}, u32[]{:S(2)}, u32[]{:S(2)}) %collective-permute-start) | collective-permute-done | bytes 65568 | tf_op jit(solution)/shard_map/ppermute | solution.py:62
  12.6 1.2 %collective-permute-start.4 = (bf16[2,128,128]{2,1,0:T(8,128)(2,1)S(1)}, bf16[2,128,128]{2,1,0:T(8,128)(2,1)S(1)}, u32[]{:S(2)}, u32[]{:S(2)}) collective-permute-start(bf16[2,128,128]{2,1,0:T(8,128)(2,1)S(1)} %collective-permute-done.1.refs_1_.other), channel_id=1, source_target_pairs={{0,3},{1,2},{2,1},{3,0},{4,7},{5,6},{6,5},{7,4},{8,11},{9,10},{10,... | collective-permute-start | bytes 196616 | tf_op jit(solution)/shard_map/ppermute | solution.py:62
  13.7 0.0 collective-permute-done.9.refs_6_.refs_10_
  13.7 0.6 %collective-permute-start.6 = (bf16[2,128,128]{2,1,0:T(8,128)(2,1)S(1)}, bf16[2,128,128]{2,1,0:T(8,128)(2,1)S(1)}, u32[]{:S(2)}, u32[]{:S(2)}) collective-permute-start(bf16[2,128,128]{2,1,0:T(8,128)(2,1)S(1)} %collective-permute-done.refs_3_), channel_id=1, source_target_pairs={{0,3},{1,2},{2,1},{3,0},{4,7},{5,6},{6,5},{7,4},{8,11},{9,10},{10,... | collective-permute-start | bytes 196616 | tf_op jit(solution)/shard_map/ppermute | solution.py:62
  14.4 1.4 %ready.1 = (bf16[2,128,128]{2,1,0:T(8,128)(2,1)S(1)}, f32[96,128,128]{2,1,0:T(8,128)S(1)}, f32[96,128,128]{2,1,0:T(8,128)S(1)}, bf16[16,128,128]{2,1,0:T(8,128)(...) custom-call(s32[1]{0:T(128)} %bitcast.me, ...), custom_call_target="tpu_custom_call", output_to_operand_aliasing={{0}: (7, {})} | custom-call | bytes 16650240 | tf_op jit(solution)/shard_map/ready/pallas_call | solution.py:321
  15.7 0.0 collective-permute-done.5.refs_2_.refs_6_
  15.8 0.1 collective-permute-start.10
  15.9 0.0 collective-permute-done.3.refs_0_.refs_4_
  15.9 0.5 %collective-permute-start.13 = (bf16[2,128,128]{2,1,0:T(8,128)(2,1)S(1)}, bf16[2,128,128]{2,1,0:T(8,128)(2,1)S(1)}, u32[]{:S(2)}, u32[]{:S(2)}) collective-permute-start(bf16[2,128,128]{2,1,0:T(8,128)(2,1)S(1)} %collective-permute-done.5.refs_2_.refs_6_), channel_id=1, source_target_pairs={{0,1},{1,0},{2,3},{3,2},{4,5},{5,4},{6,7},{7,6},{8,9},{9,8},{10,11... | collective-permute-start | bytes 196616 | tf_op jit(solution)/shard_map/ppermute | solution.py:62
  16.3 0.0 collective-permute-done.8.refs_5_.refs_9_
  16.3 0.1 collective-permute-start.11
  16.4 0.4 %collective-permute-start.12 = (bf16[2,128,128]{2,1,0:T(8,128)(2,1)S(1)}, bf16[2,128,128]{2,1,0:T(8,128)(2,1)S(1)}, u32[]{:S(2)}, u32[]{:S(2)}) collective-permute-start(bf16[2,128,128]{2,1,0:T(8,128)(2,1)S(1)} %collective-permute-done.4.refs_1_.refs_5_), channel_id=1, source_target_pairs={{0,1},{1,0},{2,3},{3,2},{4,5},{5,4},{6,7},{7,6},{8,9},{9,8},{10,11... | collective-permute-start | bytes 196616 | tf_op jit(solution)/shard_map/ppermute | solution.py:62
  16.9 1.1 %collective-permute-done.6.refs_3_.refs_7_ = bf16[2,128,128]{2,1,0:T(8,128)(2,1)S(1)} collective-permute-done((bf16[2,128,128]{2,1,0:T(8,128)(2,1)S(1)}, bf16[2,128,128]{2,1,0:T(8,128)(2,1)S(1)}, u32[]{:S(2)}, u32[]{:S(2)}) %collective-permute-start.6) | collective-permute-done | bytes 65568 | tf_op jit(solution)/shard_map/ppermute | solution.py:62
  18.0 0.4 %collective-permute-start.14 = (bf16[2,128,128]{2,1,0:T(8,128)(2,1)S(1)}, bf16[2,128,128]{2,1,0:T(8,128)(2,1)S(1)}, u32[]{:S(2)}, u32[]{:S(2)}) collective-permute-start(bf16[2,128,128]{2,1,0:T(8,128)(2,1)S(1)} %collective-permute-done.6.refs_3_.refs_7_), channel_id=1, source_target_pairs={{0,1},{1,0},{2,3},{3,2},{4,5},{5,4},{6,7},{7,6},{8,9},{9,8},{10,11... | collective-permute-start | bytes 196616 | tf_op jit(solution)/shard_map/ppermute | solution.py:62
  18.4 0.9 %collective-permute-done.14.refs_11_.refs_15_ = bf16[2,128,128]{2,1,0:T(8,128)(2,1)S(1)} collective-permute-done((bf16[2,128,128]{2,1,0:T(8,128)(2,1)S(1)}, bf16[2,128,128]{2,1,0:T(8,128)(2,1)S(1)}, u32[]{:S(2)}, u32[]{:S(2)}) %collective-permute-start.14) | collective-permute-done | bytes 65568 | tf_op jit(solution)/shard_map/ppermute | solution.py:62
  19.3 1.8 %middle.1 = (f32[96,128,128]{2,1,0:T(8,128)S(1)}, f32[96,128,128]{2,1,0:T(8,128)S(1)}, bf16[16,128,128]{2,1,0:T(8,128)(2,1)S(1)}, bf16[16,128,128]{2,1,0:T(8,128...) custom-call(s32[8,128]{1,0:T(8,128)S(1)} %get-tuple-element.34.table, ...), custom_call_target="tpu_custom_call", output_to_operand_aliasing={{0}: (1, {}), {1}: (2, {})} | custom-call | flops 268435456 | bytes 32247808 | tf_op jit(solution)/shard_map/middle/pallas_call | solution.py:321
  21.1 0.4 %collective-permute-start.17 = (bf16[2,2,128,128]{3,2,1,0:T(8,128)(2,1)S(1)}, bf16[2,2,128,128]{3,2,1,0:T(8,128)(2,1)S(1)}, u32[]{:S(2)}, u32[]{:S(2)}) collective-permute-start(bf16[2,2,128,128]{3,2,1,0:T(8,128)(2,1)S(1)} %get-tuple-element.51), channel_id=1, source_target_pairs={{0,1},{1,0},{2,3},{3,2},{4,5},{5,4},{6,7},{7,6},{8,9},{9,8},{10,11... | collective-permute-start | bytes 393224 | tf_op jit(solution)/shard_map/ppermute | solution.py:62
  21.5 0.2 collective-permute-start.20
  21.7 0.4 collective-permute-start.23
  22.0 0.2 collective-permute-start.15
  22.2 0.3 collective-permute-done.17.refs_0_
  22.6 1.0 %collective-permute-start.18 = (bf16[1,2,128,128]{3,2,1,0:T(8,128)(2,1)S(1)}, bf16[1,2,128,128]{3,2,1,0:T(8,128)(2,1)S(1)}, u32[]{:S(2)}, u32[]{:S(2)}) collective-permute-start(bf16[1,2,128,128]{3,2,1,0:T(8,128)(2,1)S(1)} %get-tuple-element.53), channel_id=1, source_target_pairs={{0,3},{1,2},{2,1},{3,0},{4,7},{5,6},{6,5},{7,4},{8,11},{9,10},{10,... | collective-permute-start | bytes 196616 | tf_op jit(solution)/shard_map/ppermute | solution.py:62
  23.6 0.8 %collective-permute-start.21 = (bf16[1,2,128,128]{3,2,1,0:T(8,128)(2,1)S(1)}, bf16[1,2,128,128]{3,2,1,0:T(8,128)(2,1)S(1)}, u32[]{:S(2)}, u32[]{:S(2)}) collective-permute-start(bf16[1,2,128,128]{3,2,1,0:T(8,128)(2,1)S(1)} %get-tuple-element.57), channel_id=1, source_target_pairs={{0,3},{1,2},{2,1},{3,0},{4,7},{5,6},{6,5},{7,4},{8,11},{9,10},{10,... | collective-permute-start | bytes 196616 | tf_op jit(solution)/shard_map/ppermute | solution.py:62
  24.5 1.0 %collective-permute-start.24 = (bf16[1,2,128,128]{3,2,1,0:T(8,128)(2,1)S(1)}, bf16[1,2,128,128]{3,2,1,0:T(8,128)(2,1)S(1)}, u32[]{:S(2)}, u32[]{:S(2)}) collective-permute-start(bf16[1,2,128,128]{3,2,1,0:T(8,128)(2,1)S(1)} %get-tuple-element.61), channel_id=1, source_target_pairs={{0,3},{1,2},{2,1},{3,0},{4,7},{5,6},{6,5},{7,4},{8,11},{9,10},{10,... | collective-permute-start | bytes 196616 | tf_op jit(solution)/shard_map/ppermute | solution.py:62
  25.6 0.8 %collective-permute-start.16 = (bf16[1,2,128,128]{3,2,1,0:T(8,128)(2,1)S(1)}, bf16[1,2,128,128]{3,2,1,0:T(8,128)(2,1)S(1)}, u32[]{:S(2)}, u32[]{:S(2)}) collective-permute-start(bf16[1,2,128,128]{3,2,1,0:T(8,128)(2,1)S(1)} %get-tuple-element.49), channel_id=1, source_target_pairs={{0,3},{1,2},{2,1},{3,0},{4,7},{5,6},{6,5},{7,4},{8,11},{9,10},{10,... | collective-permute-start | bytes 196616 | tf_op jit(solution)/shard_map/ppermute | solution.py:62
  26.4 0.9 %collective-permute-done.18.refs_0_ = bf16[1,2,128,128]{3,2,1,0:T(8,128)(2,1)S(1)} collective-permute-done((bf16[1,2,128,128]{3,2,1,0:T(8,128)(2,1)S(1)}, bf16[1,2,128,128]{3,2,1,0:T(8,128)(2,1)S(1)}, u32[]{:S(2)}, u32[]{:S(2)}) %collective-permute-start.18) | collective-permute-done | bytes 65568 | tf_op jit(solution)/shard_map/ppermute | solution.py:62
  27.4 1.6 %collective-permute-start.19 = (bf16[1,2,128,128]{3,2,1,0:T(8,128)(2,1)S(1)}, bf16[1,2,128,128]{3,2,1,0:T(8,128)(2,1)S(1)}, u32[]{:S(2)}, u32[]{:S(2)}) collective-permute-start(bf16[1,2,128,128]{3,2,1,0:T(8,128)(2,1)S(1)} %fold.9), channel_id=1, source_target_pairs={{0,9},{1,8},{2,11},{3,10},{4,13},{5,12},{6,15},{7,14},{8,1},{9,0},... | collective-permute-start | bytes 196616 | tf_op jit(solution)/shard_map/ppermute | solution.py:62
  28.9 2.0 %collective-permute-start.22 = (bf16[1,2,128,128]{3,2,1,0:T(8,128)(2,1)S(1)}, bf16[1,2,128,128]{3,2,1,0:T(8,128)(2,1)S(1)}, u32[]{:S(2)}, u32[]{:S(2)}) collective-permute-start(bf16[1,2,128,128]{3,2,1,0:T(8,128)(2,1)S(1)} %fold.11), channel_id=1, source_target_pairs={{0,5},{1,4},{2,7},{3,6},{4,1},{5,0},{6,3},{7,2},{8,13},{9,12},{10,... | collective-permute-start | bytes 196616 | tf_op jit(solution)/shard_map/ppermute | solution.py:62
  31.0 2.0 %collective-permute-start.25 = (bf16[1,2,128,128]{3,2,1,0:T(8,128)(2,1)S(1)}, bf16[1,2,128,128]{3,2,1,0:T(8,128)(2,1)S(1)}, u32[]{:S(2)}, u32[]{:S(2)}) collective-permute-start(bf16[1,2,128,128]{3,2,1,0:T(8,128)(2,1)S(1)} %fold.13), channel_id=1, source_target_pairs={{0,13},{1,12},{2,15},{3,14},{4,9},{5,8},{6,11},{7,10},{8,5},{9,4},... | collective-permute-start | bytes 196616 | tf_op jit(solution)/shard_map/ppermute | solution.py:62
  33.0 2.0 %last.1 = (bf16[128,3072]{1,0:T(8,128)(2,1)}, bf16[128,3072]{1,0:T(8,128)(2,1)}) custom-call(s32[8,128]{1,0:T(8,128)S(1)} %get-tuple-element.34.table, bf16[16,128,128]{2,1,0:T(8,128)(2,1)S(1)} %get-tuple-element.42.act, bf16[16,128,128]{2,1,0:T(8,128)(2,1)S(1)} %get-tuple-element.43.hgrad, bf16[2,128,128]{2,1,0:T(8,128)(2,1)S(1)} %begin.1.refs_0_.value, ...), custom_call_target="tpu_custom_call" | custom-call | flops 134217728 | bytes 9965600 | tf_op jit(solution)/shard_map/last/pallas_call | solution.py:321
  35.0 1.5 %collective-permute-done.25.refs_3_ = bf16[1,2,128,128]{3,2,1,0:T(8,128)(2,1)S(1)} collective-permute-done((bf16[1,2,128,128]{3,2,1,0:T(8,128)(2,1)S(1)}, bf16[1,2,128,128]{3,2,1,0:T(8,128)(2,1)S(1)}, u32[]{:S(2)}, u32[]{:S(2)}) %collective-permute-start.25) | collective-permute-done | bytes 65568 | tf_op jit(solution)/shard_map/ppermute | solution.py:62
  36.6 0.7 %close.1 = (f32[1,128,128]{2,1,0:T(8,128)}, f32[1,128,128]{2,1,0:T(8,128)}) custom-call(f32[1,2,128,128]{3,2,1,0:T(8,128)S(1)} %get-tuple-element.48.held, bf16[1,2,128,128]{3,2,1,0:T(8,128)(2,1)S(1)} %collective-permute-done.16.refs_0_, bf16[1,2,128,128]{3,2,1,0:T(8,128)(2,1)S(1)} %collective-permute-done.19.refs_1_, ...), custom_call_target="tpu_custom_call" | custom-call | bytes 524288 | tf_op jit(solution)/shard_map/close/pallas_call | solution.py:321
  (30 shorter events, 0.2 us)
Async XLA Ops:
  1.4 12.9 %copy-start = (bf16[128,3072]{1,0:T(8,128)(2,1)S(1)}, bf16[128,3072]{1,0:T(8,128)(2,1)}, u32[]{:S(2)}) copy-start(bf16[128,3072]{1,0:T(8,128)(2,1)} %tokens.1) | copy-start | bytes 2359300
  1.4 12.9 %copy-start.1 = (bf16[128,3072]{1,0:T(8,128)(2,1)S(1)}, bf16[128,3072]{1,0:T(8,128)(2,1)}, u32[]{:S(2)}) copy-start(bf16[128,3072]{1,0:T(8,128)(2,1)} %cot.1) | copy-start | bytes 2359300
  1.5 12.9 %copy-start.2 = (s32[16]{0:T(128)S(1)}, s32[16]{0:T(128)}, u32[]{:S(2)}) copy-start(s32[16]{0:T(128)} %r1.1) | copy-start | bytes 196
  1.5 12.9 %copy-start.3 = (s32[16]{0:T(128)S(1)}, s32[16]{0:T(128)}, u32[]{:S(2)}) copy-start(s32[16]{0:T(128)} %c1.1) | copy-start | bytes 196
  1.5 12.9 %copy-start.4 = (s32[16]{0:T(128)S(1)}, s32[16]{0:T(128)}, u32[]{:S(2)}) copy-start(s32[16]{0:T(128)} %r2.1) | copy-start | bytes 196
  1.5 12.9 %copy-start.5 = (s32[16]{0:T(128)S(1)}, s32[16]{0:T(128)}, u32[]{:S(2)}) copy-start(s32[16]{0:T(128)} %c2.1) | copy-start | bytes 196
  1.5 5.5 %collective-permute-start.2 = (bf16[2,128,128]{2,1,0:T(8,128)(2,1)S(1)}, bf16[2,128,128]{2,1,0:T(8,128)(2,1)S(1)}, u32[]{:S(2)}, u32[]{:S(2)}) collective-permute-start(bf16[2,128,128]{2,1,0:T(8,128)(2,1)S(1)} %begin.1.refs_0_.value), channel_id=1, source_target_pairs={{0,5},{1,4},{2,7},{3,6},{4,1},{5,0},{6,3},{7,2},{8,13},{9,12},{10,... | collective-permute-start | bytes 196616 | tf_op jit(solution)/shard_map/ppermute | solution.py:62
  4.3 6.1 %collective-permute-start.1 = (bf16[2,128,128]{2,1,0:T(8,128)(2,1)S(1)}, bf16[2,128,128]{2,1,0:T(8,128)(2,1)S(1)}, u32[]{:S(2)}, u32[]{:S(2)}) collective-permute-start(bf16[2,128,128]{2,1,0:T(8,128)(2,1)S(1)} %begin.1.refs_0_.value), channel_id=1, source_target_pairs={{0,9},{1,8},{2,11},{3,10},{4,13},{5,12},{6,15},{7,14},{8,1},{9,0},... | collective-permute-start | bytes 196616 | tf_op jit(solution)/shard_map/ppermute | solution.py:62
  6.3 4.2 %collective-permute-start.7 = (bf16[2,128,128]{2,1,0:T(8,128)(2,1)S(1)}, bf16[2,128,128]{2,1,0:T(8,128)(2,1)S(1)}, u32[]{:S(2)}, u32[]{:S(2)}) collective-permute-start(bf16[2,128,128]{2,1,0:T(8,128)(2,1)S(1)} %begin.1.refs_0_.value), channel_id=1, source_target_pairs={{0,1},{1,0},{2,3},{3,2},{4,5},{5,4},{6,7},{7,6},{8,9},{9,8},{10,11... | collective-permute-start | bytes 196616 | tf_op jit(solution)/shard_map/ppermute | solution.py:62
  7.0 5.6 %collective-permute-start = (bf16[2,128,128]{2,1,0:T(8,128)(2,1)S(1)}, bf16[2,128,128]{2,1,0:T(8,128)(2,1)S(1)}, u32[]{:S(2)}, u32[]{:S(2)}) collective-permute-start(bf16[2,128,128]{2,1,0:T(8,128)(2,1)S(1)} %begin.1.refs_0_.value), channel_id=1, source_target_pairs={{0,13},{1,12},{2,15},{3,14},{4,9},{5,8},{6,11},{7,10},{8,5},{9,4},... | collective-permute-start | bytes 196616 | tf_op jit(solution)/shard_map/ppermute | solution.py:62
  7.0 6.8 %collective-permute-start.9 = (bf16[2,128,128]{2,1,0:T(8,128)(2,1)S(1)}, bf16[2,128,128]{2,1,0:T(8,128)(2,1)S(1)}, u32[]{:S(2)}, u32[]{:S(2)}) collective-permute-start(bf16[2,128,128]{2,1,0:T(8,128)(2,1)S(1)} %collective-permute-done.2.refs_2_), channel_id=1, source_target_pairs={{0,1},{1,0},{2,3},{3,2},{4,5},{5,4},{6,7},{7,6},{8,9},{9,8},{10,11... | collective-permute-start | bytes 196616 | tf_op jit(solution)/shard_map/ppermute | solution.py:62
  7.0 8.7 %collective-permute-start.5 = (bf16[2,128,128]{2,1,0:T(8,128)(2,1)S(1)}, bf16[2,128,128]{2,1,0:T(8,128)(2,1)S(1)}, u32[]{:S(2)}, u32[]{:S(2)}) collective-permute-start(bf16[2,128,128]{2,1,0:T(8,128)(2,1)S(1)} %collective-permute-done.2.refs_2_), channel_id=1, source_target_pairs={{0,3},{1,2},{2,1},{3,0},{4,7},{5,6},{6,5},{7,4},{8,11},{9,10},{10,... | collective-permute-start | bytes 196616 | tf_op jit(solution)/shard_map/ppermute | solution.py:62
  10.3 5.5 %collective-permute-start.3 = (bf16[2,128,128]{2,1,0:T(8,128)(2,1)S(1)}, bf16[2,128,128]{2,1,0:T(8,128)(2,1)S(1)}, u32[]{:S(2)}, u32[]{:S(2)}) collective-permute-start(bf16[2,128,128]{2,1,0:T(8,128)(2,1)S(1)} %after.1), channel_id=1, source_target_pairs={{0,3},{1,2},{2,1},{3,0},{4,7},{5,6},{6,5},{7,4},{8,11},{9,10},{10,... | collective-permute-start | bytes 196616 | tf_op jit(solution)/shard_map/ppermute | solution.py:62
  10.5 5.9 %collective-permute-start.8 = (bf16[2,128,128]{2,1,0:T(8,128)(2,1)S(1)}, bf16[2,128,128]{2,1,0:T(8,128)(2,1)S(1)}, u32[]{:S(2)}, u32[]{:S(2)}) collective-permute-start(bf16[2,128,128]{2,1,0:T(8,128)(2,1)S(1)} %collective-permute-done.1.refs_1_.other), channel_id=1, source_target_pairs={{0,1},{1,0},{2,3},{3,2},{4,5},{5,4},{6,7},{7,6},{8,9},{9,8},{10,11... | collective-permute-start | bytes 196616 | tf_op jit(solution)/shard_map/ppermute | solution.py:62
  12.6 3.9 %collective-permute-start.4 = (bf16[2,128,128]{2,1,0:T(8,128)(2,1)S(1)}, bf16[2,128,128]{2,1,0:T(8,128)(2,1)S(1)}, u32[]{:S(2)}, u32[]{:S(2)}) collective-permute-start(bf16[2,128,128]{2,1,0:T(8,128)(2,1)S(1)} %collective-permute-done.1.refs_1_.other), channel_id=1, source_target_pairs={{0,3},{1,2},{2,1},{3,0},{4,7},{5,6},{6,5},{7,4},{8,11},{9,10},{10,... | collective-permute-start | bytes 196616 | tf_op jit(solution)/shard_map/ppermute | solution.py:62
  13.7 4.3 %collective-permute-start.6 = (bf16[2,128,128]{2,1,0:T(8,128)(2,1)S(1)}, bf16[2,128,128]{2,1,0:T(8,128)(2,1)S(1)}, u32[]{:S(2)}, u32[]{:S(2)}) collective-permute-start(bf16[2,128,128]{2,1,0:T(8,128)(2,1)S(1)} %collective-permute-done.refs_3_), channel_id=1, source_target_pairs={{0,3},{1,2},{2,1},{3,0},{4,7},{5,6},{6,5},{7,4},{8,11},{9,10},{10,... | collective-permute-start | bytes 196616 | tf_op jit(solution)/shard_map/ppermute | solution.py:62
  15.8 2.6 %collective-permute-start.10 = (bf16[2,128,128]{2,1,0:T(8,128)(2,1)S(1)}, bf16[2,128,128]{2,1,0:T(8,128)(2,1)S(1)}, u32[]{:S(2)}, u32[]{:S(2)}) collective-permute-start(bf16[2,128,128]{2,1,0:T(8,128)(2,1)S(1)} %get-tuple-element.41), channel_id=1, source_target_pairs={{0,1},{1,0},{2,3},{3,2},{4,5},{5,4},{6,7},{7,6},{8,9},{9,8},{10,11... | collective-permute-start | bytes 196616 | tf_op jit(solution)/shard_map/ppermute | solution.py:62
  15.9 2.5 %collective-permute-start.13 = (bf16[2,128,128]{2,1,0:T(8,128)(2,1)S(1)}, bf16[2,128,128]{2,1,0:T(8,128)(2,1)S(1)}, u32[]{:S(2)}, u32[]{:S(2)}) collective-permute-start(bf16[2,128,128]{2,1,0:T(8,128)(2,1)S(1)} %collective-permute-done.5.refs_2_.refs_6_), channel_id=1, source_target_pairs={{0,1},{1,0},{2,3},{3,2},{4,5},{5,4},{6,7},{7,6},{8,9},{9,8},{10,11... | collective-permute-start | bytes 196616 | tf_op jit(solution)/shard_map/ppermute | solution.py:62
  16.3 2.1 %collective-permute-start.11 = (bf16[2,128,128]{2,1,0:T(8,128)(2,1)S(1)}, bf16[2,128,128]{2,1,0:T(8,128)(2,1)S(1)}, u32[]{:S(2)}, u32[]{:S(2)}) collective-permute-start(bf16[2,128,128]{2,1,0:T(8,128)(2,1)S(1)} %collective-permute-done.3.refs_0_.refs_4_), channel_id=1, source_target_pairs={{0,1},{1,0},{2,3},{3,2},{4,5},{5,4},{6,7},{7,6},{8,9},{9,8},{10,11... | collective-permute-start | bytes 196616 | tf_op jit(solution)/shard_map/ppermute | solution.py:62
  16.4 2.0 %collective-permute-start.12 = (bf16[2,128,128]{2,1,0:T(8,128)(2,1)S(1)}, bf16[2,128,128]{2,1,0:T(8,128)(2,1)S(1)}, u32[]{:S(2)}, u32[]{:S(2)}) collective-permute-start(bf16[2,128,128]{2,1,0:T(8,128)(2,1)S(1)} %collective-permute-done.4.refs_1_.refs_5_), channel_id=1, source_target_pairs={{0,1},{1,0},{2,3},{3,2},{4,5},{5,4},{6,7},{7,6},{8,9},{9,8},{10,11... | collective-permute-start | bytes 196616 | tf_op jit(solution)/shard_map/ppermute | solution.py:62
  18.0 1.3 %collective-permute-start.14 = (bf16[2,128,128]{2,1,0:T(8,128)(2,1)S(1)}, bf16[2,128,128]{2,1,0:T(8,128)(2,1)S(1)}, u32[]{:S(2)}, u32[]{:S(2)}) collective-permute-start(bf16[2,128,128]{2,1,0:T(8,128)(2,1)S(1)} %collective-permute-done.6.refs_3_.refs_7_), channel_id=1, source_target_pairs={{0,1},{1,0},{2,3},{3,2},{4,5},{5,4},{6,7},{7,6},{8,9},{9,8},{10,11... | collective-permute-start | bytes 196616 | tf_op jit(solution)/shard_map/ppermute | solution.py:62
  21.1 1.4 %collective-permute-start.17 = (bf16[2,2,128,128]{3,2,1,0:T(8,128)(2,1)S(1)}, bf16[2,2,128,128]{3,2,1,0:T(8,128)(2,1)S(1)}, u32[]{:S(2)}, u32[]{:S(2)}) collective-permute-start(bf16[2,2,128,128]{3,2,1,0:T(8,128)(2,1)S(1)} %get-tuple-element.51), channel_id=1, source_target_pairs={{0,1},{1,0},{2,3},{3,2},{4,5},{5,4},{6,7},{7,6},{8,9},{9,8},{10,11... | collective-permute-start | bytes 393224 | tf_op jit(solution)/shard_map/ppermute | solution.py:62
  21.5 2.1 %collective-permute-start.20 = (bf16[2,2,128,128]{3,2,1,0:T(8,128)(2,1)S(1)}, bf16[2,2,128,128]{3,2,1,0:T(8,128)(2,1)S(1)}, u32[]{:S(2)}, u32[]{:S(2)}) collective-permute-start(bf16[2,2,128,128]{3,2,1,0:T(8,128)(2,1)S(1)} %get-tuple-element.55), channel_id=1, source_target_pairs={{0,1},{1,0},{2,3},{3,2},{4,5},{5,4},{6,7},{7,6},{8,9},{9,8},{10,11... | collective-permute-start | bytes 393224 | tf_op jit(solution)/shard_map/ppermute | solution.py:62
  21.7 2.8 %collective-permute-start.23 = (bf16[2,2,128,128]{3,2,1,0:T(8,128)(2,1)S(1)}, bf16[2,2,128,128]{3,2,1,0:T(8,128)(2,1)S(1)}, u32[]{:S(2)}, u32[]{:S(2)}) collective-permute-start(bf16[2,2,128,128]{3,2,1,0:T(8,128)(2,1)S(1)} %get-tuple-element.59), channel_id=1, source_target_pairs={{0,1},{1,0},{2,3},{3,2},{4,5},{5,4},{6,7},{7,6},{8,9},{9,8},{10,11... | collective-permute-start | bytes 393224 | tf_op jit(solution)/shard_map/ppermute | solution.py:62
  22.0 3.5 %collective-permute-start.15 = (bf16[2,2,128,128]{3,2,1,0:T(8,128)(2,1)S(1)}, bf16[2,2,128,128]{3,2,1,0:T(8,128)(2,1)S(1)}, u32[]{:S(2)}, u32[]{:S(2)}) collective-permute-start(bf16[2,2,128,128]{3,2,1,0:T(8,128)(2,1)S(1)} %get-tuple-element.47), channel_id=1, source_target_pairs={{0,1},{1,0},{2,3},{3,2},{4,5},{5,4},{6,7},{7,6},{8,9},{9,8},{10,11... | collective-permute-start | bytes 393224 | tf_op jit(solution)/shard_map/ppermute | solution.py:62
  22.6 4.8 %collective-permute-start.18 = (bf16[1,2,128,128]{3,2,1,0:T(8,128)(2,1)S(1)}, bf16[1,2,128,128]{3,2,1,0:T(8,128)(2,1)S(1)}, u32[]{:S(2)}, u32[]{:S(2)}) collective-permute-start(bf16[1,2,128,128]{3,2,1,0:T(8,128)(2,1)S(1)} %get-tuple-element.53), channel_id=1, source_target_pairs={{0,3},{1,2},{2,1},{3,0},{4,7},{5,6},{6,5},{7,4},{8,11},{9,10},{10,... | collective-permute-start | bytes 196616 | tf_op jit(solution)/shard_map/ppermute | solution.py:62
  23.6 5.3 %collective-permute-start.21 = (bf16[1,2,128,128]{3,2,1,0:T(8,128)(2,1)S(1)}, bf16[1,2,128,128]{3,2,1,0:T(8,128)(2,1)S(1)}, u32[]{:S(2)}, u32[]{:S(2)}) collective-permute-start(bf16[1,2,128,128]{3,2,1,0:T(8,128)(2,1)S(1)} %get-tuple-element.57), channel_id=1, source_target_pairs={{0,3},{1,2},{2,1},{3,0},{4,7},{5,6},{6,5},{7,4},{8,11},{9,10},{10,... | collective-permute-start | bytes 196616 | tf_op jit(solution)/shard_map/ppermute | solution.py:62
  24.5 6.5 %collective-permute-start.24 = (bf16[1,2,128,128]{3,2,1,0:T(8,128)(2,1)S(1)}, bf16[1,2,128,128]{3,2,1,0:T(8,128)(2,1)S(1)}, u32[]{:S(2)}, u32[]{:S(2)}) collective-permute-start(bf16[1,2,128,128]{3,2,1,0:T(8,128)(2,1)S(1)} %get-tuple-element.61), channel_id=1, source_target_pairs={{0,3},{1,2},{2,1},{3,0},{4,7},{5,6},{6,5},{7,4},{8,11},{9,10},{10,... | collective-permute-start | bytes 196616 | tf_op jit(solution)/shard_map/ppermute | solution.py:62
  25.6 9.4 %collective-permute-start.16 = (bf16[1,2,128,128]{3,2,1,0:T(8,128)(2,1)S(1)}, bf16[1,2,128,128]{3,2,1,0:T(8,128)(2,1)S(1)}, u32[]{:S(2)}, u32[]{:S(2)}) collective-permute-start(bf16[1,2,128,128]{3,2,1,0:T(8,128)(2,1)S(1)} %get-tuple-element.49), channel_id=1, source_target_pairs={{0,3},{1,2},{2,1},{3,0},{4,7},{5,6},{6,5},{7,4},{8,11},{9,10},{10,... | collective-permute-start | bytes 196616 | tf_op jit(solution)/shard_map/ppermute | solution.py:62
  27.4 7.7 %collective-permute-start.19 = (bf16[1,2,128,128]{3,2,1,0:T(8,128)(2,1)S(1)}, bf16[1,2,128,128]{3,2,1,0:T(8,128)(2,1)S(1)}, u32[]{:S(2)}, u32[]{:S(2)}) collective-permute-start(bf16[1,2,128,128]{3,2,1,0:T(8,128)(2,1)S(1)} %fold.9), channel_id=1, source_target_pairs={{0,9},{1,8},{2,11},{3,10},{4,13},{5,12},{6,15},{7,14},{8,1},{9,0},... | collective-permute-start | bytes 196616 | tf_op jit(solution)/shard_map/ppermute | solution.py:62
  28.9 6.1 %collective-permute-start.22 = (bf16[1,2,128,128]{3,2,1,0:T(8,128)(2,1)S(1)}, bf16[1,2,128,128]{3,2,1,0:T(8,128)(2,1)S(1)}, u32[]{:S(2)}, u32[]{:S(2)}) collective-permute-start(bf16[1,2,128,128]{3,2,1,0:T(8,128)(2,1)S(1)} %fold.11), channel_id=1, source_target_pairs={{0,5},{1,4},{2,7},{3,6},{4,1},{5,0},{6,3},{7,2},{8,13},{9,12},{10,... | collective-permute-start | bytes 196616 | tf_op jit(solution)/shard_map/ppermute | solution.py:62
  31.0 5.6 %collective-permute-start.25 = (bf16[1,2,128,128]{3,2,1,0:T(8,128)(2,1)S(1)}, bf16[1,2,128,128]{3,2,1,0:T(8,128)(2,1)S(1)}, u32[]{:S(2)}, u32[]{:S(2)}) collective-permute-start(bf16[1,2,128,128]{3,2,1,0:T(8,128)(2,1)S(1)} %fold.13), channel_id=1, source_target_pairs={{0,13},{1,12},{2,15},{3,14},{4,9},{5,8},{6,11},{7,10},{8,5},{9,4},... | collective-permute-start | bytes 196616 | tf_op jit(solution)/shard_map/ppermute | solution.py:62

commit v4 on v3

--- a/solution.py
+++ b/solution.py
@@ -14,6 +14,9 @@
 PRE_SLOT = 3
 TIE = 1
 EARLY = 4
+TAIL = 1
+GROUPS = ((1,), (2,), (3,), (0,))
+SPLIT = 0
 ROOT = math.sqrt(2.0 / math.pi)
 CUBE = 0.044715
 F32 = jnp.float32
@@ -84,6 +87,17 @@
     t = tanh_of(v, u)
     g = 0.5 + 0.5 * t
     return g + (g * (1.0 - t)) * (v * (ROOT + 3.0 * ROOT * CUBE * u))
+
+
+def twice_gelu(v):
+    return v + v * tanh_of(v, v * v)
+
+
+def twice_gelu_slope(v):
+    u = v * v
+    t = tanh_of(v, u)
+    p = 1.0 + t
+    return p + (p * (1.0 - t)) * (v * (ROOT + 3.0 * ROOT * CUBE * u))
 
 
 def each(count, run):
@@ -192,7 +206,7 @@
     for acc, stage, target in ((oacc, ostage, out), (iacc, istage, igrad)):
         for d in range(0, count, CHUNK):
             for e in range(d, d + CHUNK):
-                stage[:, e * size:(e + 1) * size] = acc[e].astype(BF16)
+                stage[:, e * size:(e + 1) * size] = (0.5 * acc[e]).astype(BF16)
             at = (slice(None), pl.ds(d * size, CHUNK * size))
             copies.append(pltpu.make_async_copy(stage.at[at], target.at[at], sems.at[len(copies)]))
             copies[-1].start()
@@ -230,35 +244,52 @@
         agrad[at.r2(s)] += dot(ct[s], w[1], ((1,), (1,)))
 
 
-def core(nb, parts, place, table, hidden_in, agrad_in, tok, tok_t, ct, ct_t, *refs):
-    late, (hidden, agrad, act, hgrad, *out, prod, prod_t) = refs[:-6 - 2 * parts], refs[-6 - 2 * parts:]
+def add_products(late, table, tok, ct, refs, hidden, agrad, prod, prod_t):
+    for i, (s, w) in enumerate(zip(late, refs)):
+        prod[i] = dot(tok[s], w[0], ((1,), (0,)))
+        prod_t[i] = dot(ct[s], w[1], ((1,), (1,)))
+    for i, s in enumerate(late):
+        hidden[table[0, s]] += prod[i]
+    for i, s in enumerate(late):
+        agrad[table[1, s]] += prod_t[i]
+
+
+def more(late, table, hidden_in, agrad_in, tok, ct, *refs):
+    weights, (hidden, agrad, prod, prod_t) = refs[:-4], refs[-4:]
     del hidden_in, agrad_in
-    sends, keeps = out[:parts], out[parts:]
-    ne = nb - len(late)
-    for i, w in enumerate(late):
-        prod[i] = dot(tok[ne + i], w[0], ((1,), (0,)))
-        prod_t[i] = dot(ct[ne + i], w[1], ((1,), (1,)))
-    c1 = [table[0, s] for s in range(nb)]
-    r2 = [table[1, s] for s in range(nb)]
-    for i in range(len(late)):
-        hidden[c1[ne + i]] += prod[i]
-    for i in range(len(late)):
-        agrad[r2[ne + i]] += prod_t[i]
-    half = nb // parts // 2
-
-    def put(e, which, value):
-        i, q = e % parts, e // parts
-        if q < half:
-            keeps[i][q, which] = value
-        else:
-            sends[i][q - half, which] = value.astype(BF16)
-
+    add_products(late, table, tok, ct, weights, hidden, agrad, prod, prod_t)
+
+
+def grads_of(groups, parts, place, tok_t, ct_t, act, hgrad, out):
+    sends, keeps = out[:len(groups)], out[len(groups):]
+    half = len(place) // parts // 2
+    for group, send, keep in zip(groups, sends, keeps):
+        for q in range(2 * half):
+            for k, i in enumerate(group):
+                s = place[i + parts * q]
+                at = q % half * len(group) + k
+                values = dot(tok_t[s], hgrad[s], ((1,), (0,))), dot(ct_t[s], act[s], ((1,), (0,)))
+                for which, value in enumerate(values):
+                    if q < half:
+                        keep[at, which] = value
+                    else:
+                        send[at, which] = value.astype(BF16)
+
+
+def core(nb, parts, place, late, pieces, table, hidden_in, agrad_in, tok, tok_t, ct, ct_t, *refs):
+    weights, (hidden, agrad, act, hgrad, *out, prod, prod_t) = refs[:len(late)], refs[len(late):]
+    del hidden_in, agrad_in
+    add_products(late, table, tok, ct, weights, hidden, agrad, prod, prod_t)
     for s in range(nb):
-        act[s] = gelu(hidden[r2[s]]).astype(BF16)
-        hgrad[s] = (agrad[c1[s]] * gelu_slope(hidden[c1[s]])).astype(BF16)
-    for e, s in enumerate(place):
-        put(e, 0, dot(tok_t[s], hgrad[s], ((1,), (0,))))
-        put(e, 1, dot(ct_t[s], act[s], ((1,), (0,))))
+        act[s] = twice_gelu(hidden[table[1, s]]).astype(BF16)
+        c = table[0, s]
+        hgrad[s] = (agrad[c] * twice_gelu_slope(hidden[c])).astype(BF16)
+    grads_of(pieces, parts, place, tok_t, ct_t, act, hgrad, out)
+
+
+def rest(parts, place, pieces, arrived, tok_t, ct_t, act, hgrad, *out):
+    del arrived
+    grads_of(pieces, parts, place, tok_t, ct_t, act, hgrad, out)
 
 
 def last(nb, nw, me, order, r1, c1, r2, c2, act, hgrad, *refs):
@@ -298,9 +329,9 @@
 def close(scale, turned, held, *refs):
     arrived, outs = refs[:-2], refs[-2:]
     for which, out in enumerate(outs):
-        value = held[0, which]
+        value = held[held.shape[0] - 1, which]
         for a in arrived:
-            value = value + a[0, which].astype(F32)
+            value = value + a[a.shape[0] - 1, which].astype(F32)
         value = value * scale
         out[0] = value.T if which == turned else value
 
@@ -371,6 +402,18 @@
             aliases=((2, 0),),
         )
     pieces = pieces + [swap(p, 1, n) for p in moved]
+    late = list(range(EARLY, nb))
+    if fast and TAIL:
+        soon, late = late[:-TAIL], late[-TAIL:]
+        hidden, agrad = call(
+            functools.partial(more, soon),
+            [units, units],
+            (),
+            [table, hidden, agrad, tok, ct, *[pieces[s] for s in soon]],
+            [pltpu.VMEM((len(soon), width, size), F32)] * 2,
+            name="more",
+            aliases=((1, 0), (2, 1)),
+        )
     weights = pieces if n <= 16 else [jnp.stack(pieces)]
     nw = len(weights)
     if n <= 16:
@@ -393,16 +436,14 @@
     work = 2 * nb * width * size * size
     outs = [panels, panels] + [blocks(half, BF16)] * parts + [blocks(half, F32)] * parts
     if fast:
-        late = nb - EARLY
+        count = [half * len(g) for g in GROUPS]
+        mine = GROUPS[:SPLIT] if SPLIT else GROUPS
         _, _, act, hgrad, *out = call(
-            functools.partial(core, nb, parts, place),
-            [units, units, *outs],
+            functools.partial(core, nb, parts, place, late, mine),
+            [units, units, panels, panels] + [blocks(c, BF16) for c in count[:len(mine)]] + [blocks(c, F32) for c in count[:len(mine)]],
             (),
-            [table, hidden, agrad, tok, tok_t, ct, ct_t, *pieces[EARLY:]],
-            [
-                pltpu.VMEM((late, width, size), F32),
-                pltpu.VMEM((late, width, size), F32),
-            ],
+            [table, hidden, agrad, tok, tok_t, ct, ct_t, *[pieces[s] for s in late]],
+            [pltpu.VMEM((len(late), width, size), F32)] * 2,
             4 * work,
             "middle",
             aliases=((1, 0), (2, 1)),
@@ -434,27 +475,55 @@
     else:
         output, input_grad = call(bind(last, nb, nw), [model, model], lists, [act, hgrad, *weights], [total, total], 2 * work, "last")
 
-    sends, keeps = out[:parts], out[parts:]
-    near = rounds[1:][::-1]
-    landed = []
-    for i in range(parts):
-        leaving, held = [sends[i]], keeps[i]
-        for now, later in zip(near, [*near[1:], []]):
-            arrived = [swap(v, m, n) for v, m in zip(leaving, now)]
-            if later or i:
-                count = held.shape[0] // (len(later) + 1)
-                kept = blocks(count, F32 if later else BF16)
-                held, *leaving = call(
-                    functools.partial(fold, len(later) + 1),
-                    [kept] + [blocks(count, BF16)] * len(later),
-                    (),
-                    [held, *arrived],
-                    name="fold",
-                )
-        landed += [held, *arrived] if i == 0 else [swap(held, rounds[0][i - 1], n)]
+    if fast:
+        sends, keeps = out[:len(mine)], out[len(mine):]
+        arrived = [swap(v, 1, n) for v in sends]
+        if SPLIT:
+            others = count[SPLIT:]
+            made = call(
+                functools.partial(rest, parts, place, GROUPS[SPLIT:]),
+                [blocks(c, BF16) for c in others] + [blocks(c, F32) for c in others],
+                (),
+                [arrived[0], tok_t, ct_t, act, hgrad],
+                name="rest",
+            )
+            keeps = [*keeps, *made[len(others):]]
+            arrived = [*arrived, *[swap(v, 1, n) for v in made[:len(others)]]]
+
+        def sums(held, arrived, shapes):
+            return call(functools.partial(fold, len(shapes)), shapes, (), [held, *arrived], name="fold")
+
+        landed = []
+        for group, keep, near in zip(GROUPS, keeps, arrived):
+            kept, leaving = sums(keep, [near], [blocks(len(group), F32), blocks(len(group), BF16)])
+            beside = swap(leaving, 3, n)
+            if group[-1] == 0:
+                landed = [kept, beside, *landed]
+            if group[0] != 0:
+                (leaving,) = sums(kept, [beside], [blocks(1, BF16)])
+                landed.append(swap(leaving, rounds[0][group[0] - 1], n))
+    else:
+        sends, keeps = out[:parts], out[parts:]
+        near = rounds[1:][::-1]
+        landed = []
+        for i in range(parts):
+            leaving, held = [sends[i]], keeps[i]
+            for now, later in zip(near, [*near[1:], []]):
+                arrived = [swap(v, m, n) for v, m in zip(leaving, now)]
+                if later or i:
+                    count = held.shape[0] // (len(later) + 1)
+                    kept = blocks(count, F32 if later else BF16)
+                    held, *leaving = call(
+                        functools.partial(fold, len(later) + 1),
+                        [kept] + [blocks(count, BF16)] * len(later),
+                        (),
+                        [held, *arrived],
+                        name="fold",
+                    )
+            landed += [held, *arrived] if i == 0 else [swap(held, rounds[0][i - 1], n)]
     grad = jax.ShapeDtypeStruct((1, size, size), F32)
     first_grad, second_grad = call(
-        functools.partial(close, 1.0 / math.sqrt(width * n), 1 if fast else -1), [grad, grad], (), landed, name="close"
+        functools.partial(close, (0.5 if fast else 1.0) / math.sqrt(width * n), 1 if fast else -1), [grad, grad], (), landed, name="close"
     )
     return (output, input_grad, first_grad, second_grad)
 

time: 37.5 us -> 37.1 us (0.989)
  waiting for transfers between devices: 7.15 us -> 6.68 us
    ppermute x26, waiting for transfers between devices: 7.15 us -> 6.68 us  [swap(): return lax.ppermute(value, 'row', [(i, i ^ mask) for i in range(n)])]
    pallas_call x13 -> x14, Pallas kernels: 6.89 us -> 6.98 us  [call(): pl.pallas_call(kernel, out_shape=outs, in_specs=[SMEM] * len(smem) + [ANY...]
  transfers between devices with their start and end apart: 26 -> 26, of which waited for: 7 -> 7; matrix products, arithmetic and copies ran while one was open for 0% -> 0% of each run, Pallas kernels for 10% -> 11%
where the time goes in v4:
time: 37.1 us; the launch traced here: 36.9 us
  starting transfers between devices  22.4 us (60%)
  Pallas kernels  6.98 us (19%)
  waiting for transfers between devices  6.68 us (18%)
  between operations  0.84 us (2%)
    ppermute x26, starting transfers between devices, swap(): return lax.ppermute(value, 'row', [(i, i ^ mask) for i in range(n)])  22.4 us
    pallas_call x14, Pallas kernels, call(): pl.pallas_call(kernel, out_shape=outs, in_specs=[SMEM] * len(smem) + [ANY...  6.98 us
    ppermute x26, waiting for transfers between devices, swap(): return lax.ppermute(value, 'row', [(i, i ^ mask) for i in range(n)])  6.68 us
  transfers between devices with their start and end apart: 26, of which 7 were waited for; matrix products, arithmetic and copies ran while one was open for 0% of the time, Pallas kernels for 11%

profile of v4, /device:TPU:1, one launch (start us, length us, event | category | flops | bytes accessed | tf_op | source)
XLA Modules:
  0.0 36.9 jit_solution(1926824964079632570)
XLA Ops:
  0.6 0.8 %begin.1.refs_0_.value = bf16[2,128,128]{2,1,0:T(8,128)(2,1)S(1)} custom-call(bf16[1,128,128]{2,1,0:T(8,128)(2,1)} %w1.1, bf16[1,128,128]{2,1,0:T(8,128)(2,1)} %w2.1), custom_call_target="tpu_custom_call" | custom-call | bytes 65544 | tf_op jit(solution)/shard_map/begin/pallas_call | solution.py:352
  1.4 0.0 copy-start
  1.4 0.0 copy-start.1
  1.5 0.0 copy-start.2
  1.5 0.0 copy-start.3
  1.5 0.0 copy-start.4
  1.5 0.0 copy-start.5
  1.5 2.8 %collective-permute-start.2 = (bf16[2,128,128]{2,1,0:T(8,128)(2,1)S(1)}, bf16[2,128,128]{2,1,0:T(8,128)(2,1)S(1)}, u32[]{:S(2)}, u32[]{:S(2)}) collective-permute-start(bf16[2,128,128]{2,1,0:T(8,128)(2,1)S(1)} %begin.1.refs_0_.value), channel_id=1, source_target_pairs={{0,5},{1,4},{2,7},{3,6},{4,1},{5,0},{6,3},{7,2},{8,13},{9,12},{10,... | collective-permute-start | bytes 196616 | tf_op jit(solution)/shard_map/ppermute | solution.py:65
  4.3 2.0 %collective-permute-start.1 = (bf16[2,128,128]{2,1,0:T(8,128)(2,1)S(1)}, bf16[2,128,128]{2,1,0:T(8,128)(2,1)S(1)}, u32[]{:S(2)}, u32[]{:S(2)}) collective-permute-start(bf16[2,128,128]{2,1,0:T(8,128)(2,1)S(1)} %begin.1.refs_0_.value), channel_id=1, source_target_pairs={{0,9},{1,8},{2,11},{3,10},{4,13},{5,12},{6,15},{7,14},{8,1},{9,0},... | collective-permute-start | bytes 196616 | tf_op jit(solution)/shard_map/ppermute | solution.py:65
  6.3 0.7 %collective-permute-start.7 = (bf16[2,128,128]{2,1,0:T(8,128)(2,1)S(1)}, bf16[2,128,128]{2,1,0:T(8,128)(2,1)S(1)}, u32[]{:S(2)}, u32[]{:S(2)}) collective-permute-start(bf16[2,128,128]{2,1,0:T(8,128)(2,1)S(1)} %begin.1.refs_0_.value), channel_id=1, source_target_pairs={{0,1},{1,0},{2,3},{3,2},{4,5},{5,4},{6,7},{7,6},{8,9},{9,8},{10,11... | collective-permute-start | bytes 196616 | tf_op jit(solution)/shard_map/ppermute | solution.py:65
  7.0 0.0 collective-permute-start
  7.0 0.1 collective-permute-start.9
  7.0 1.6 %collective-permute-start.5 = (bf16[2,128,128]{2,1,0:T(8,128)(2,1)S(1)}, bf16[2,128,128]{2,1,0:T(8,128)(2,1)S(1)}, u32[]{:S(2)}, u32[]{:S(2)}) collective-permute-start(bf16[2,128,128]{2,1,0:T(8,128)(2,1)S(1)} %collective-permute-done.2.refs_2_), channel_id=1, source_target_pairs={{0,3},{1,2},{2,1},{3,0},{4,7},{5,6},{6,5},{7,4},{8,11},{9,10},{10,... | collective-permute-start | bytes 196616 | tf_op jit(solution)/shard_map/ppermute | solution.py:65
  8.6 1.7 %collective-permute-done.1.refs_1_.other = bf16[2,128,128]{2,1,0:T(8,128)(2,1)S(1)} collective-permute-done((bf16[2,128,128]{2,1,0:T(8,128)(2,1)S(1)}, bf16[2,128,128]{2,1,0:T(8,128)(2,1)S(1)}, u32[]{:S(2)}, u32[]{:S(2)}) %collective-permute-start.1) | collective-permute-done | bytes 65568 | tf_op jit(solution)/shard_map/ppermute | solution.py:65
  10.3 0.1 collective-permute-start.3
  10.5 0.0 collective-permute-done.7.refs_4_.refs_8_
  10.5 1.5 %collective-permute-start.8 = (bf16[2,128,128]{2,1,0:T(8,128)(2,1)S(1)}, bf16[2,128,128]{2,1,0:T(8,128)(2,1)S(1)}, u32[]{:S(2)}, u32[]{:S(2)}) collective-permute-start(bf16[2,128,128]{2,1,0:T(8,128)(2,1)S(1)} %collective-permute-done.1.refs_1_.other), channel_id=1, source_target_pairs={{0,1},{1,0},{2,3},{3,2},{4,5},{5,4},{6,7},{7,6},{8,9},{9,8},{10,11... | collective-permute-start | bytes 196616 | tf_op jit(solution)/shard_map/ppermute | solution.py:65
  12.0 0.6 %collective-permute-done.refs_3_ = bf16[2,128,128]{2,1,0:T(8,128)(2,1)S(1)} collective-permute-done((bf16[2,128,128]{2,1,0:T(8,128)(2,1)S(1)}, bf16[2,128,128]{2,1,0:T(8,128)(2,1)S(1)}, u32[]{:S(2)}, u32[]{:S(2)}) %collective-permute-start) | collective-permute-done | bytes 65568 | tf_op jit(solution)/shard_map/ppermute | solution.py:65
  12.6 1.2 %collective-permute-start.4 = (bf16[2,128,128]{2,1,0:T(8,128)(2,1)S(1)}, bf16[2,128,128]{2,1,0:T(8,128)(2,1)S(1)}, u32[]{:S(2)}, u32[]{:S(2)}) collective-permute-start(bf16[2,128,128]{2,1,0:T(8,128)(2,1)S(1)} %collective-permute-done.1.refs_1_.other), channel_id=1, source_target_pairs={{0,3},{1,2},{2,1},{3,0},{4,7},{5,6},{6,5},{7,4},{8,11},{9,10},{10,... | collective-permute-start | bytes 196616 | tf_op jit(solution)/shard_map/ppermute | solution.py:65
  13.7 0.0 collective-permute-done.9.refs_6_.refs_10_
  13.7 0.6 %collective-permute-start.6 = (bf16[2,128,128]{2,1,0:T(8,128)(2,1)S(1)}, bf16[2,128,128]{2,1,0:T(8,128)(2,1)S(1)}, u32[]{:S(2)}, u32[]{:S(2)}) collective-permute-start(bf16[2,128,128]{2,1,0:T(8,128)(2,1)S(1)} %collective-permute-done.refs_3_), channel_id=1, source_target_pairs={{0,3},{1,2},{2,1},{3,0},{4,7},{5,6},{6,5},{7,4},{8,11},{9,10},{10,... | collective-permute-start | bytes 196616 | tf_op jit(solution)/shard_map/ppermute | solution.py:65
  14.4 1.4 %ready.1 = (bf16[2,128,128]{2,1,0:T(8,128)(2,1)S(1)}, f32[96,128,128]{2,1,0:T(8,128)S(1)}, f32[96,128,128]{2,1,0:T(8,128)S(1)}, bf16[16,128,128]{2,1,0:T(8,128)(...) custom-call(s32[1]{0:T(128)} %bitcast.me, ...), custom_call_target="tpu_custom_call", output_to_operand_aliasing={{0}: (7, {})} | custom-call | bytes 16650240 | tf_op jit(solution)/shard_map/ready/pallas_call | solution.py:352
  15.7 0.0 collective-permute-done.5.refs_2_.refs_6_
  15.8 0.1 collective-permute-start.10
  15.9 0.5 %collective-permute-start.13 = (bf16[2,128,128]{2,1,0:T(8,128)(2,1)S(1)}, bf16[2,128,128]{2,1,0:T(8,128)(2,1)S(1)}, u32[]{:S(2)}, u32[]{:S(2)}) collective-permute-start(bf16[2,128,128]{2,1,0:T(8,128)(2,1)S(1)} %collective-permute-done.5.refs_2_.refs_6_), channel_id=1, source_target_pairs={{0,1},{1,0},{2,3},{3,2},{4,5},{5,4},{6,7},{7,6},{8,9},{9,8},{10,11... | collective-permute-start | bytes 196616 | tf_op jit(solution)/shard_map/ppermute | solution.py:65
  16.3 0.1 collective-permute-start.11
  16.4 0.4 %collective-permute-start.12 = (bf16[2,128,128]{2,1,0:T(8,128)(2,1)S(1)}, bf16[2,128,128]{2,1,0:T(8,128)(2,1)S(1)}, u32[]{:S(2)}, u32[]{:S(2)}) collective-permute-start(bf16[2,128,128]{2,1,0:T(8,128)(2,1)S(1)} %collective-permute-done.4.refs_1_.refs_5_), channel_id=1, source_target_pairs={{0,1},{1,0},{2,3},{3,2},{4,5},{5,4},{6,7},{7,6},{8,9},{9,8},{10,11... | collective-permute-start | bytes 196616 | tf_op jit(solution)/shard_map/ppermute | solution.py:65
  16.9 1.1 %collective-permute-done.6.refs_3_.refs_7_ = bf16[2,128,128]{2,1,0:T(8,128)(2,1)S(1)} collective-permute-done((bf16[2,128,128]{2,1,0:T(8,128)(2,1)S(1)}, bf16[2,128,128]{2,1,0:T(8,128)(2,1)S(1)}, u32[]{:S(2)}, u32[]{:S(2)}) %collective-permute-start.6) | collective-permute-done | bytes 65568 | tf_op jit(solution)/shard_map/ppermute | solution.py:65
  18.0 0.4 %collective-permute-start.14 = (bf16[2,128,128]{2,1,0:T(8,128)(2,1)S(1)}, bf16[2,128,128]{2,1,0:T(8,128)(2,1)S(1)}, u32[]{:S(2)}, u32[]{:S(2)}) collective-permute-start(bf16[2,128,128]{2,1,0:T(8,128)(2,1)S(1)} %collective-permute-done.6.refs_3_.refs_7_), channel_id=1, source_target_pairs={{0,1},{1,0},{2,3},{3,2},{4,5},{5,4},{6,7},{7,6},{8,9},{9,8},{10,11... | collective-permute-start | bytes 196616 | tf_op jit(solution)/shard_map/ppermute | solution.py:65
  18.4 0.5 %more.1 = (f32[96,128,128]{2,1,0:T(8,128)S(1)}, f32[96,128,128]{2,1,0:T(8,128)S(1)}) custom-call(s32[8,128]{1,0:T(8,128)S(1)} %get-tuple-element.36.table, f32[96,128,128]{2,1,0:T(8,128)S(1)} %get-tuple-element.37.hidden_in, f32[96,128,128]{2,1,0:T(8,128)S(1)} %get-tuple-element.38.agrad_in, ...), custom_call_target="tpu_custom_call", output_to_operand_aliasing={{0}: (1, {}), {1}: (2, {})} | custom-call | bytes 28381184 | tf_op jit(solution)/shard_map/more/pallas_call | solution.py:352
  18.9 0.4 %collective-permute-done.14.refs_0_.refs_15_ = bf16[2,128,128]{2,1,0:T(8,128)(2,1)S(1)} collective-permute-done((bf16[2,128,128]{2,1,0:T(8,128)(2,1)S(1)}, bf16[2,128,128]{2,1,0:T(8,128)(2,1)S(1)}, u32[]{:S(2)}, u32[]{:S(2)}) %collective-permute-start.14) | collective-permute-done | bytes 65568 | tf_op jit(solution)/shard_map/ppermute | solution.py:65
  19.3 1.4 %middle.1 = (f32[96,128,128]{2,1,0:T(8,128)S(1)}, f32[96,128,128]{2,1,0:T(8,128)S(1)}, bf16[16,128,128]{2,1,0:T(8,128)(2,1)S(1)}, bf16[16,128,128]{2,1,0:T(8,128...) custom-call(s32[8,128]{1,0:T(8,128)S(1)} %get-tuple-element.36.table, ...), custom_call_target="tpu_custom_call", output_to_operand_aliasing={{0}: (1, {}), {1}: (2, {})} | custom-call | flops 268435456 | bytes 30085120 | tf_op jit(solution)/shard_map/middle/pallas_call | solution.py:352
  20.7 0.4 %collective-permute-start.17 = (bf16[2,2,128,128]{3,2,1,0:T(8,128)(2,1)S(1)}, bf16[2,2,128,128]{3,2,1,0:T(8,128)(2,1)S(1)}, u32[]{:S(2)}, u32[]{:S(2)}) collective-permute-start(bf16[2,2,128,128]{3,2,1,0:T(8,128)(2,1)S(1)} %get-tuple-element.55), channel_id=1, source_target_pairs={{0,1},{1,0},{2,3},{3,2},{4,5},{5,4},{6,7},{7,6},{8,9},{9,8},{10,11... | collective-permute-start | bytes 393224 | tf_op jit(solution)/shard_map/ppermute | solution.py:65
  21.1 0.2 collective-permute-start.20
  21.3 0.4 collective-permute-start.23
  21.7 0.2 collective-permute-start.15
  21.8 0.3 collective-permute-done.17.refs_0_
  22.2 1.0 %collective-permute-start.18 = (bf16[1,2,128,128]{3,2,1,0:T(8,128)(2,1)S(1)}, bf16[1,2,128,128]{3,2,1,0:T(8,128)(2,1)S(1)}, u32[]{:S(2)}, u32[]{:S(2)}) collective-permute-start(bf16[1,2,128,128]{3,2,1,0:T(8,128)(2,1)S(1)} %get-tuple-element.57), channel_id=1, source_target_pairs={{0,3},{1,2},{2,1},{3,0},{4,7},{5,6},{6,5},{7,4},{8,11},{9,10},{10,... | collective-permute-start | bytes 196616 | tf_op jit(solution)/shard_map/ppermute | solution.py:65
  23.2 0.8 %collective-permute-start.21 = (bf16[1,2,128,128]{3,2,1,0:T(8,128)(2,1)S(1)}, bf16[1,2,128,128]{3,2,1,0:T(8,128)(2,1)S(1)}, u32[]{:S(2)}, u32[]{:S(2)}) collective-permute-start(bf16[1,2,128,128]{3,2,1,0:T(8,128)(2,1)S(1)} %get-tuple-element.61), channel_id=1, source_target_pairs={{0,3},{1,2},{2,1},{3,0},{4,7},{5,6},{6,5},{7,4},{8,11},{9,10},{10,... | collective-permute-start | bytes 196616 | tf_op jit(solution)/shard_map/ppermute | solution.py:65
  24.1 1.0 %collective-permute-start.24 = (bf16[1,2,128,128]{3,2,1,0:T(8,128)(2,1)S(1)}, bf16[1,2,128,128]{3,2,1,0:T(8,128)(2,1)S(1)}, u32[]{:S(2)}, u32[]{:S(2)}) collective-permute-start(bf16[1,2,128,128]{3,2,1,0:T(8,128)(2,1)S(1)} %get-tuple-element.65), channel_id=1, source_target_pairs={{0,3},{1,2},{2,1},{3,0},{4,7},{5,6},{6,5},{7,4},{8,11},{9,10},{10,... | collective-permute-start | bytes 196616 | tf_op jit(solution)/shard_map/ppermute | solution.py:65
  25.2 0.8 %collective-permute-start.16 = (bf16[1,2,128,128]{3,2,1,0:T(8,128)(2,1)S(1)}, bf16[1,2,128,128]{3,2,1,0:T(8,128)(2,1)S(1)}, u32[]{:S(2)}, u32[]{:S(2)}) collective-permute-start(bf16[1,2,128,128]{3,2,1,0:T(8,128)(2,1)S(1)} %get-tuple-element.53), channel_id=1, source_target_pairs={{0,3},{1,2},{2,1},{3,0},{4,7},{5,6},{6,5},{7,4},{8,11},{9,10},{10,... | collective-permute-start | bytes 196616 | tf_op jit(solution)/shard_map/ppermute | solution.py:65
  26.0 0.9 %collective-permute-done.18.refs_0_ = bf16[1,2,128,128]{3,2,1,0:T(8,128)(2,1)S(1)} collective-permute-done((bf16[1,2,128,128]{3,2,1,0:T(8,128)(2,1)S(1)}, bf16[1,2,128,128]{3,2,1,0:T(8,128)(2,1)S(1)}, u32[]{:S(2)}, u32[]{:S(2)}) %collective-permute-start.18) | collective-permute-done | bytes 65568 | tf_op jit(solution)/shard_map/ppermute | solution.py:65
  27.0 1.6 %collective-permute-start.19 = (bf16[1,2,128,128]{3,2,1,0:T(8,128)(2,1)S(1)}, bf16[1,2,128,128]{3,2,1,0:T(8,128)(2,1)S(1)}, u32[]{:S(2)}, u32[]{:S(2)}) collective-permute-start(bf16[1,2,128,128]{3,2,1,0:T(8,128)(2,1)S(1)} %fold.9), channel_id=1, source_target_pairs={{0,9},{1,8},{2,11},{3,10},{4,13},{5,12},{6,15},{7,14},{8,1},{9,0},... | collective-permute-start | bytes 196616 | tf_op jit(solution)/shard_map/ppermute | solution.py:65
  28.6 2.1 %collective-permute-start.22 = (bf16[1,2,128,128]{3,2,1,0:T(8,128)(2,1)S(1)}, bf16[1,2,128,128]{3,2,1,0:T(8,128)(2,1)S(1)}, u32[]{:S(2)}, u32[]{:S(2)}) collective-permute-start(bf16[1,2,128,128]{3,2,1,0:T(8,128)(2,1)S(1)} %fold.11), channel_id=1, source_target_pairs={{0,5},{1,4},{2,7},{3,6},{4,1},{5,0},{6,3},{7,2},{8,13},{9,12},{10,... | collective-permute-start | bytes 196616 | tf_op jit(solution)/shard_map/ppermute | solution.py:65
  30.6 2.0 %collective-permute-start.25 = (bf16[1,2,128,128]{3,2,1,0:T(8,128)(2,1)S(1)}, bf16[1,2,128,128]{3,2,1,0:T(8,128)(2,1)S(1)}, u32[]{:S(2)}, u32[]{:S(2)}) collective-permute-start(bf16[1,2,128,128]{3,2,1,0:T(8,128)(2,1)S(1)} %fold.13), channel_id=1, source_target_pairs={{0,13},{1,12},{2,15},{3,14},{4,9},{5,8},{6,11},{7,10},{8,5},{9,4},... | collective-permute-start | bytes 196616 | tf_op jit(solution)/shard_map/ppermute | solution.py:65
  32.6 2.0 %last.1 = (bf16[128,3072]{1,0:T(8,128)(2,1)}, bf16[128,3072]{1,0:T(8,128)(2,1)}) custom-call(s32[8,128]{1,0:T(8,128)S(1)} %get-tuple-element.36.table, bf16[16,128,128]{2,1,0:T(8,128)(2,1)S(1)} %get-tuple-element.46.act, bf16[16,128,128]{2,1,0:T(8,128)(2,1)S(1)} %get-tuple-element.47.hgrad, bf16[2,128,128]{2,1,0:T(8,128)(2,1)S(1)} %begin.1.refs_0_.value, ...), custom_call_target="tpu_custom_call" | custom-call | flops 134217728 | bytes 9965600 | tf_op jit(solution)/shard_map/last/pallas_call | solution.py:352
  34.6 1.6 %collective-permute-done.25.refs_3_ = bf16[1,2,128,128]{3,2,1,0:T(8,128)(2,1)S(1)} collective-permute-done((bf16[1,2,128,128]{3,2,1,0:T(8,128)(2,1)S(1)}, bf16[1,2,128,128]{3,2,1,0:T(8,128)(2,1)S(1)}, u32[]{:S(2)}, u32[]{:S(2)}) %collective-permute-start.25) | collective-permute-done | bytes 65568 | tf_op jit(solution)/shard_map/ppermute | solution.py:65
  36.2 0.7 %close.1 = (f32[1,128,128]{2,1,0:T(8,128)}, f32[1,128,128]{2,1,0:T(8,128)}) custom-call(f32[1,2,128,128]{3,2,1,0:T(8,128)S(1)} %get-tuple-element.52.held, bf16[1,2,128,128]{3,2,1,0:T(8,128)(2,1)S(1)} %collective-permute-done.16.refs_0_, bf16[1,2,128,128]{3,2,1,0:T(8,128)(2,1)S(1)} %collective-permute-done.19.refs_1_, ...), custom_call_target="tpu_custom_call" | custom-call | bytes 524288 | tf_op jit(solution)/shard_map/close/pallas_call | solution.py:352
  (31 shorter events, 0.2 us)
Async XLA Ops:
  1.4 12.9 %copy-start = (bf16[128,3072]{1,0:T(8,128)(2,1)S(1)}, bf16[128,3072]{1,0:T(8,128)(2,1)}, u32[]{:S(2)}) copy-start(bf16[128,3072]{1,0:T(8,128)(2,1)} %tokens.1) | copy-start | bytes 2359300
  1.4 12.9 %copy-start.1 = (bf16[128,3072]{1,0:T(8,128)(2,1)S(1)}, bf16[128,3072]{1,0:T(8,128)(2,1)}, u32[]{:S(2)}) copy-start(bf16[128,3072]{1,0:T(8,128)(2,1)} %cot.1) | copy-start | bytes 2359300
  1.5 12.9 %copy-start.2 = (s32[16]{0:T(128)S(1)}, s32[16]{0:T(128)}, u32[]{:S(2)}) copy-start(s32[16]{0:T(128)} %r1.1) | copy-start | bytes 196
  1.5 12.9 %copy-start.3 = (s32[16]{0:T(128)S(1)}, s32[16]{0:T(128)}, u32[]{:S(2)}) copy-start(s32[16]{0:T(128)} %c1.1) | copy-start | bytes 196
  1.5 12.9 %copy-start.4 = (s32[16]{0:T(128)S(1)}, s32[16]{0:T(128)}, u32[]{:S(2)}) copy-start(s32[16]{0:T(128)} %r2.1) | copy-start | bytes 196
  1.5 12.9 %copy-start.5 = (s32[16]{0:T(128)S(1)}, s32[16]{0:T(128)}, u32[]{:S(2)}) copy-start(s32[16]{0:T(128)} %c2.1) | copy-start | bytes 196
  1.5 5.5 %collective-permute-start.2 = (bf16[2,128,128]{2,1,0:T(8,128)(2,1)S(1)}, bf16[2,128,128]{2,1,0:T(8,128)(2,1)S(1)}, u32[]{:S(2)}, u32[]{:S(2)}) collective-permute-start(bf16[2,128,128]{2,1,0:T(8,128)(2,1)S(1)} %begin.1.refs_0_.value), channel_id=1, source_target_pairs={{0,5},{1,4},{2,7},{3,6},{4,1},{5,0},{6,3},{7,2},{8,13},{9,12},{10,... | collective-permute-start | bytes 196616 | tf_op jit(solution)/shard_map/ppermute | solution.py:65
  4.3 6.1 %collective-permute-start.1 = (bf16[2,128,128]{2,1,0:T(8,128)(2,1)S(1)}, bf16[2,128,128]{2,1,0:T(8,128)(2,1)S(1)}, u32[]{:S(2)}, u32[]{:S(2)}) collective-permute-start(bf16[2,128,128]{2,1,0:T(8,128)(2,1)S(1)} %begin.1.refs_0_.value), channel_id=1, source_target_pairs={{0,9},{1,8},{2,11},{3,10},{4,13},{5,12},{6,15},{7,14},{8,1},{9,0},... | collective-permute-start | bytes 196616 | tf_op jit(solution)/shard_map/ppermute | solution.py:65
  6.3 4.2 %collective-permute-start.7 = (bf16[2,128,128]{2,1,0:T(8,128)(2,1)S(1)}, bf16[2,128,128]{2,1,0:T(8,128)(2,1)S(1)}, u32[]{:S(2)}, u32[]{:S(2)}) collective-permute-start(bf16[2,128,128]{2,1,0:T(8,128)(2,1)S(1)} %begin.1.refs_0_.value), channel_id=1, source_target_pairs={{0,1},{1,0},{2,3},{3,2},{4,5},{5,4},{6,7},{7,6},{8,9},{9,8},{10,11... | collective-permute-start | bytes 196616 | tf_op jit(solution)/shard_map/ppermute | solution.py:65
  7.0 5.6 %collective-permute-start = (bf16[2,128,128]{2,1,0:T(8,128)(2,1)S(1)}, bf16[2,128,128]{2,1,0:T(8,128)(2,1)S(1)}, u32[]{:S(2)}, u32[]{:S(2)}) collective-permute-start(bf16[2,128,128]{2,1,0:T(8,128)(2,1)S(1)} %begin.1.refs_0_.value), channel_id=1, source_target_pairs={{0,13},{1,12},{2,15},{3,14},{4,9},{5,8},{6,11},{7,10},{8,5},{9,4},... | collective-permute-start | bytes 196616 | tf_op jit(solution)/shard_map/ppermute | solution.py:65
  7.0 6.8 %collective-permute-start.9 = (bf16[2,128,128]{2,1,0:T(8,128)(2,1)S(1)}, bf16[2,128,128]{2,1,0:T(8,128)(2,1)S(1)}, u32[]{:S(2)}, u32[]{:S(2)}) collective-permute-start(bf16[2,128,128]{2,1,0:T(8,128)(2,1)S(1)} %collective-permute-done.2.refs_2_), channel_id=1, source_target_pairs={{0,1},{1,0},{2,3},{3,2},{4,5},{5,4},{6,7},{7,6},{8,9},{9,8},{10,11... | collective-permute-start | bytes 196616 | tf_op jit(solution)/shard_map/ppermute | solution.py:65
  7.0 8.7 %collective-permute-start.5 = (bf16[2,128,128]{2,1,0:T(8,128)(2,1)S(1)}, bf16[2,128,128]{2,1,0:T(8,128)(2,1)S(1)}, u32[]{:S(2)}, u32[]{:S(2)}) collective-permute-start(bf16[2,128,128]{2,1,0:T(8,128)(2,1)S(1)} %collective-permute-done.2.refs_2_), channel_id=1, source_target_pairs={{0,3},{1,2},{2,1},{3,0},{4,7},{5,6},{6,5},{7,4},{8,11},{9,10},{10,... | collective-permute-start | bytes 196616 | tf_op jit(solution)/shard_map/ppermute | solution.py:65
  10.3 5.5 %collective-permute-start.3 = (bf16[2,128,128]{2,1,0:T(8,128)(2,1)S(1)}, bf16[2,128,128]{2,1,0:T(8,128)(2,1)S(1)}, u32[]{:S(2)}, u32[]{:S(2)}) collective-permute-start(bf16[2,128,128]{2,1,0:T(8,128)(2,1)S(1)} %after.1), channel_id=1, source_target_pairs={{0,3},{1,2},{2,1},{3,0},{4,7},{5,6},{6,5},{7,4},{8,11},{9,10},{10,... | collective-permute-start | bytes 196616 | tf_op jit(solution)/shard_map/ppermute | solution.py:65
  10.5 5.9 %collective-permute-start.8 = (bf16[2,128,128]{2,1,0:T(8,128)(2,1)S(1)}, bf16[2,128,128]{2,1,0:T(8,128)(2,1)S(1)}, u32[]{:S(2)}, u32[]{:S(2)}) collective-permute-start(bf16[2,128,128]{2,1,0:T(8,128)(2,1)S(1)} %collective-permute-done.1.refs_1_.other), channel_id=1, source_target_pairs={{0,1},{1,0},{2,3},{3,2},{4,5},{5,4},{6,7},{7,6},{8,9},{9,8},{10,11... | collective-permute-start | bytes 196616 | tf_op jit(solution)/shard_map/ppermute | solution.py:65
  12.6 3.9 %collective-permute-start.4 = (bf16[2,128,128]{2,1,0:T(8,128)(2,1)S(1)}, bf16[2,128,128]{2,1,0:T(8,128)(2,1)S(1)}, u32[]{:S(2)}, u32[]{:S(2)}) collective-permute-start(bf16[2,128,128]{2,1,0:T(8,128)(2,1)S(1)} %collective-permute-done.1.refs_1_.other), channel_id=1, source_target_pairs={{0,3},{1,2},{2,1},{3,0},{4,7},{5,6},{6,5},{7,4},{8,11},{9,10},{10,... | collective-permute-start | bytes 196616 | tf_op jit(solution)/shard_map/ppermute | solution.py:65
  13.7 4.3 %collective-permute-start.6 = (bf16[2,128,128]{2,1,0:T(8,128)(2,1)S(1)}, bf16[2,128,128]{2,1,0:T(8,128)(2,1)S(1)}, u32[]{:S(2)}, u32[]{:S(2)}) collective-permute-start(bf16[2,128,128]{2,1,0:T(8,128)(2,1)S(1)} %collective-permute-done.refs_3_), channel_id=1, source_target_pairs={{0,3},{1,2},{2,1},{3,0},{4,7},{5,6},{6,5},{7,4},{8,11},{9,10},{10,... | collective-permute-start | bytes 196616 | tf_op jit(solution)/shard_map/ppermute | solution.py:65
  15.8 2.6 %collective-permute-start.10 = (bf16[2,128,128]{2,1,0:T(8,128)(2,1)S(1)}, bf16[2,128,128]{2,1,0:T(8,128)(2,1)S(1)}, u32[]{:S(2)}, u32[]{:S(2)}) collective-permute-start(bf16[2,128,128]{2,1,0:T(8,128)(2,1)S(1)} %get-tuple-element.41), channel_id=1, source_target_pairs={{0,1},{1,0},{2,3},{3,2},{4,5},{5,4},{6,7},{7,6},{8,9},{9,8},{10,11... | collective-permute-start | bytes 196616 | tf_op jit(solution)/shard_map/ppermute | solution.py:65
  15.9 2.5 %collective-permute-start.13 = (bf16[2,128,128]{2,1,0:T(8,128)(2,1)S(1)}, bf16[2,128,128]{2,1,0:T(8,128)(2,1)S(1)}, u32[]{:S(2)}, u32[]{:S(2)}) collective-permute-start(bf16[2,128,128]{2,1,0:T(8,128)(2,1)S(1)} %collective-permute-done.5.refs_2_.refs_6_), channel_id=1, source_target_pairs={{0,1},{1,0},{2,3},{3,2},{4,5},{5,4},{6,7},{7,6},{8,9},{9,8},{10,11... | collective-permute-start | bytes 196616 | tf_op jit(solution)/shard_map/ppermute | solution.py:65
  16.3 2.1 %collective-permute-start.11 = (bf16[2,128,128]{2,1,0:T(8,128)(2,1)S(1)}, bf16[2,128,128]{2,1,0:T(8,128)(2,1)S(1)}, u32[]{:S(2)}, u32[]{:S(2)}) collective-permute-start(bf16[2,128,128]{2,1,0:T(8,128)(2,1)S(1)} %collective-permute-done.3.refs_0_.refs_4_), channel_id=1, source_target_pairs={{0,1},{1,0},{2,3},{3,2},{4,5},{5,4},{6,7},{7,6},{8,9},{9,8},{10,11... | collective-permute-start | bytes 196616 | tf_op jit(solution)/shard_map/ppermute | solution.py:65
  16.4 2.0 %collective-permute-start.12 = (bf16[2,128,128]{2,1,0:T(8,128)(2,1)S(1)}, bf16[2,128,128]{2,1,0:T(8,128)(2,1)S(1)}, u32[]{:S(2)}, u32[]{:S(2)}) collective-permute-start(bf16[2,128,128]{2,1,0:T(8,128)(2,1)S(1)} %collective-permute-done.4.refs_1_.refs_5_), channel_id=1, source_target_pairs={{0,1},{1,0},{2,3},{3,2},{4,5},{5,4},{6,7},{7,6},{8,9},{9,8},{10,11... | collective-permute-start | bytes 196616 | tf_op jit(solution)/shard_map/ppermute | solution.py:65
  18.0 1.3 %collective-permute-start.14 = (bf16[2,128,128]{2,1,0:T(8,128)(2,1)S(1)}, bf16[2,128,128]{2,1,0:T(8,128)(2,1)S(1)}, u32[]{:S(2)}, u32[]{:S(2)}) collective-permute-start(bf16[2,128,128]{2,1,0:T(8,128)(2,1)S(1)} %collective-permute-done.6.refs_3_.refs_7_), channel_id=1, source_target_pairs={{0,1},{1,0},{2,3},{3,2},{4,5},{5,4},{6,7},{7,6},{8,9},{9,8},{10,11... | collective-permute-start | bytes 196616 | tf_op jit(solution)/shard_map/ppermute | solution.py:65
  20.7 1.4 %collective-permute-start.17 = (bf16[2,2,128,128]{3,2,1,0:T(8,128)(2,1)S(1)}, bf16[2,2,128,128]{3,2,1,0:T(8,128)(2,1)S(1)}, u32[]{:S(2)}, u32[]{:S(2)}) collective-permute-start(bf16[2,2,128,128]{3,2,1,0:T(8,128)(2,1)S(1)} %get-tuple-element.55), channel_id=1, source_target_pairs={{0,1},{1,0},{2,3},{3,2},{4,5},{5,4},{6,7},{7,6},{8,9},{9,8},{10,11... | collective-permute-start | bytes 393224 | tf_op jit(solution)/shard_map/ppermute | solution.py:65
  21.1 2.1 %collective-permute-start.20 = (bf16[2,2,128,128]{3,2,1,0:T(8,128)(2,1)S(1)}, bf16[2,2,128,128]{3,2,1,0:T(8,128)(2,1)S(1)}, u32[]{:S(2)}, u32[]{:S(2)}) collective-permute-start(bf16[2,2,128,128]{3,2,1,0:T(8,128)(2,1)S(1)} %get-tuple-element.59), channel_id=1, source_target_pairs={{0,1},{1,0},{2,3},{3,2},{4,5},{5,4},{6,7},{7,6},{8,9},{9,8},{10,11... | collective-permute-start | bytes 393224 | tf_op jit(solution)/shard_map/ppermute | solution.py:65
  21.3 2.8 %collective-permute-start.23 = (bf16[2,2,128,128]{3,2,1,0:T(8,128)(2,1)S(1)}, bf16[2,2,128,128]{3,2,1,0:T(8,128)(2,1)S(1)}, u32[]{:S(2)}, u32[]{:S(2)}) collective-permute-start(bf16[2,2,128,128]{3,2,1,0:T(8,128)(2,1)S(1)} %get-tuple-element.63), channel_id=1, source_target_pairs={{0,1},{1,0},{2,3},{3,2},{4,5},{5,4},{6,7},{7,6},{8,9},{9,8},{10,11... | collective-permute-start | bytes 393224 | tf_op jit(solution)/shard_map/ppermute | solution.py:65
  21.7 3.5 %collective-permute-start.15 = (bf16[2,2,128,128]{3,2,1,0:T(8,128)(2,1)S(1)}, bf16[2,2,128,128]{3,2,1,0:T(8,128)(2,1)S(1)}, u32[]{:S(2)}, u32[]{:S(2)}) collective-permute-start(bf16[2,2,128,128]{3,2,1,0:T(8,128)(2,1)S(1)} %get-tuple-element.51), channel_id=1, source_target_pairs={{0,1},{1,0},{2,3},{3,2},{4,5},{5,4},{6,7},{7,6},{8,9},{9,8},{10,11... | collective-permute-start | bytes 393224 | tf_op jit(solution)/shard_map/ppermute | solution.py:65
  22.2 4.8 %collective-permute-start.18 = (bf16[1,2,128,128]{3,2,1,0:T(8,128)(2,1)S(1)}, bf16[1,2,128,128]{3,2,1,0:T(8,128)(2,1)S(1)}, u32[]{:S(2)}, u32[]{:S(2)}) collective-permute-start(bf16[1,2,128,128]{3,2,1,0:T(8,128)(2,1)S(1)} %get-tuple-element.57), channel_id=1, source_target_pairs={{0,3},{1,2},{2,1},{3,0},{4,7},{5,6},{6,5},{7,4},{8,11},{9,10},{10,... | collective-permute-start | bytes 196616 | tf_op jit(solution)/shard_map/ppermute | solution.py:65
  23.2 5.3 %collective-permute-start.21 = (bf16[1,2,128,128]{3,2,1,0:T(8,128)(2,1)S(1)}, bf16[1,2,128,128]{3,2,1,0:T(8,128)(2,1)S(1)}, u32[]{:S(2)}, u32[]{:S(2)}) collective-permute-start(bf16[1,2,128,128]{3,2,1,0:T(8,128)(2,1)S(1)} %get-tuple-element.61), channel_id=1, source_target_pairs={{0,3},{1,2},{2,1},{3,0},{4,7},{5,6},{6,5},{7,4},{8,11},{9,10},{10,... | collective-permute-start | bytes 196616 | tf_op jit(solution)/shard_map/ppermute | solution.py:65
  24.1 6.5 %collective-permute-start.24 = (bf16[1,2,128,128]{3,2,1,0:T(8,128)(2,1)S(1)}, bf16[1,2,128,128]{3,2,1,0:T(8,128)(2,1)S(1)}, u32[]{:S(2)}, u32[]{:S(2)}) collective-permute-start(bf16[1,2,128,128]{3,2,1,0:T(8,128)(2,1)S(1)} %get-tuple-element.65), channel_id=1, source_target_pairs={{0,3},{1,2},{2,1},{3,0},{4,7},{5,6},{6,5},{7,4},{8,11},{9,10},{10,... | collective-permute-start | bytes 196616 | tf_op jit(solution)/shard_map/ppermute | solution.py:65
  25.2 9.4 %collective-permute-start.16 = (bf16[1,2,128,128]{3,2,1,0:T(8,128)(2,1)S(1)}, bf16[1,2,128,128]{3,2,1,0:T(8,128)(2,1)S(1)}, u32[]{:S(2)}, u32[]{:S(2)}) collective-permute-start(bf16[1,2,128,128]{3,2,1,0:T(8,128)(2,1)S(1)} %get-tuple-element.53), channel_id=1, source_target_pairs={{0,3},{1,2},{2,1},{3,0},{4,7},{5,6},{6,5},{7,4},{8,11},{9,10},{10,... | collective-permute-start | bytes 196616 | tf_op jit(solution)/shard_map/ppermute | solution.py:65
  27.0 7.6 %collective-permute-start.19 = (bf16[1,2,128,128]{3,2,1,0:T(8,128)(2,1)S(1)}, bf16[1,2,128,128]{3,2,1,0:T(8,128)(2,1)S(1)}, u32[]{:S(2)}, u32[]{:S(2)}) collective-permute-start(bf16[1,2,128,128]{3,2,1,0:T(8,128)(2,1)S(1)} %fold.9), channel_id=1, source_target_pairs={{0,9},{1,8},{2,11},{3,10},{4,13},{5,12},{6,15},{7,14},{8,1},{9,0},... | collective-permute-start | bytes 196616 | tf_op jit(solution)/shard_map/ppermute | solution.py:65
  28.6 6.1 %collective-permute-start.22 = (bf16[1,2,128,128]{3,2,1,0:T(8,128)(2,1)S(1)}, bf16[1,2,128,128]{3,2,1,0:T(8,128)(2,1)S(1)}, u32[]{:S(2)}, u32[]{:S(2)}) collective-permute-start(bf16[1,2,128,128]{3,2,1,0:T(8,128)(2,1)S(1)} %fold.11), channel_id=1, source_target_pairs={{0,5},{1,4},{2,7},{3,6},{4,1},{5,0},{6,3},{7,2},{8,13},{9,12},{10,... | collective-permute-start | bytes 196616 | tf_op jit(solution)/shard_map/ppermute | solution.py:65
  30.6 5.6 %collective-permute-start.25 = (bf16[1,2,128,128]{3,2,1,0:T(8,128)(2,1)S(1)}, bf16[1,2,128,128]{3,2,1,0:T(8,128)(2,1)S(1)}, u32[]{:S(2)}, u32[]{:S(2)}) collective-permute-start(bf16[1,2,128,128]{3,2,1,0:T(8,128)(2,1)S(1)} %fold.13), channel_id=1, source_target_pairs={{0,13},{1,12},{2,15},{3,14},{4,9},{5,8},{6,11},{7,10},{8,5},{9,4},... | collective-permute-start | bytes 196616 | tf_op jit(solution)/shard_map/ppermute | solution.py:65

commit v5 on v4

--- a/solution.py
+++ b/solution.py
@@ -9,14 +9,10 @@
 from jax.sharding import PartitionSpec as P
 
 FB = 96
-BEGIN_FLOPS = 10**10
+AHEAD = 10**10
 CHUNK = 6
-PRE_SLOT = 3
-TIE = 1
 EARLY = 4
-TAIL = 1
 GROUPS = ((1,), (2,), (3,), (0,))
-SPLIT = 0
 ROOT = math.sqrt(2.0 / math.pi)
 CUBE = 0.044715
 F32 = jnp.float32
@@ -24,10 +20,7 @@
 VMEM = pl.BlockSpec(memory_space=pltpu.VMEM)
 ANY = pl.BlockSpec(memory_space=pl.ANY)
 SMEM = pl.BlockSpec(memory_space=pltpu.SMEM)
-
-
-GATHER = [[9, 5, 13], [3], [1]]
-EXCHANGE = [[9, 5, 13], [3], [1]]
+ROUNDS = [[9, 5, 13], [3], [1]]
 
 
 def bits(n):
@@ -35,14 +28,14 @@
 
 
 def gather_rounds(n):
-    if GATHER and n == 16:
-        return GATHER
+    if n == 16:
+        return ROUNDS
     return [[b] for b in bits(n)] + [[1]]
 
 
 def exchange_rounds(n):
-    if EXCHANGE and n == 16:
-        return EXCHANGE
+    if n == 16:
+        return ROUNDS
     far, rounds = bits(n), []
     while far:
         a, far = far[0], far[1:]
@@ -276,7 +269,7 @@
                         send[at, which] = value.astype(BF16)
 
 
-def core(nb, parts, place, late, pieces, table, hidden_in, agrad_in, tok, tok_t, ct, ct_t, *refs):
+def core(nb, parts, place, late, groups, table, hidden_in, agrad_in, tok, tok_t, ct, ct_t, *refs):
     weights, (hidden, agrad, act, hgrad, *out, prod, prod_t) = refs[:len(late)], refs[len(late):]
     del hidden_in, agrad_in
     add_products(late, table, tok, ct, weights, hidden, agrad, prod, prod_t)
@@ -284,12 +277,7 @@
         act[s] = twice_gelu(hidden[table[1, s]]).astype(BF16)
         c = table[0, s]
         hgrad[s] = (agrad[c] * twice_gelu_slope(hidden[c])).astype(BF16)
-    grads_of(pieces, parts, place, tok_t, ct_t, act, hgrad, out)
-
-
-def rest(parts, place, pieces, arrived, tok_t, ct_t, act, hgrad, *out):
-    del arrived
-    grads_of(pieces, parts, place, tok_t, ct_t, act, hgrad, out)
+    grads_of(groups, parts, place, tok_t, ct_t, act, hgrad, out)
 
 
 def last(nb, nw, me, order, r1, c1, r2, c2, act, hgrad, *refs):
@@ -342,24 +330,24 @@
 
 
 def after(value, other):
-    return call(copy_after, [jax.ShapeDtypeStruct(value.shape, value.dtype)], (), [value, other], (), BEGIN_FLOPS, "after")[0]
-
-
-def call(kernel, outs, smem, args, scratch=(), flops=0, name=None, hbm_args=(), any_args=(), aliases=(), hbm_outs=False):
+    return call(copy_after, [jax.ShapeDtypeStruct(value.shape, value.dtype)], (), [value, other], (), AHEAD, "after")[0]
+
+
+def call(kernel, outs, smem, args, scratch=(), flops=0, name=None, hbm_args=(), aliases=(), hbm_outs=False):
     size = sum(math.prod(a.shape) * a.dtype.itemsize for a in (*args, *outs))
     size += sum(math.prod(s.shape) * 4 for s in scratch)
-    first = len(smem) + len(hbm_args) + len(any_args)
+    first = len(smem) + len(hbm_args)
     return pl.pallas_call(
         kernel,
         out_shape=outs,
-        in_specs=[SMEM] * len(smem) + [ANY] * (len(hbm_args) + len(any_args)) + [VMEM] * len(args),
+        in_specs=[SMEM] * len(smem) + [ANY] * len(hbm_args) + [VMEM] * len(args),
         out_specs=[ANY if hbm_outs else VMEM] * len(outs),
         scratch_shapes=list(scratch),
         input_output_aliases={first + i: o for i, o in aliases},
         compiler_params=pltpu.CompilerParams(vmem_limit_bytes=min(size + (4 << 20), 60 << 20)),
         cost_estimate=pl.CostEstimate(flops=flops, bytes_accessed=size, transcendentals=0),
         name=name,
-    )(*smem, *[pltpu.with_memory_space_constraint(a, pltpu.HBM) for a in hbm_args], *any_args, *args)
+    )(*smem, *[pltpu.with_memory_space_constraint(a, pltpu.HBM) for a in hbm_args], *args)
 
 
 def body(tokens, cotangent, w1_blocks, w1_rows, w1_cols, w2_blocks, w2_rows, w2_cols):
@@ -382,29 +370,28 @@
         "begin",
         (w1_blocks, w2_blocks),
     )
-    fast = n <= 16
+    fast = n == 16
     panels = jax.ShapeDtypeStruct((nb, width, size), BF16)
     units = jax.ShapeDtypeStruct((FB, width, size), F32)
     pieces = [own]
     for masks in gather_rounds(n)[:-1]:
         moving = list(pieces)
-        if fast and TIE and len(pieces) > 1:
-            moving[0] = after(pieces[0], pieces[TIE])
+        if fast and len(pieces) > 1:
+            moving[0] = after(pieces[0], pieces[1])
         pieces = pieces + [swap(p, m, n) for m in masks for p in moving]
     moved = list(pieces)
     if fast:
-        moved[PRE_SLOT], hidden, agrad, tok, tok_t, ct, ct_t, table = call(
+        moved[3], hidden, agrad, tok, tok_t, ct, ct_t, table = call(
             functools.partial(ready, nb, order),
             [jax.ShapeDtypeStruct(own.shape, BF16), units, units, panels, panels, panels, panels, jax.ShapeDtypeStruct((8, 128), jnp.int32)],
             (me, w1_rows, w1_cols, w2_rows, w2_cols),
-            [tokens, cotangent, pieces[PRE_SLOT], *pieces[:EARLY]],
+            [tokens, cotangent, pieces[3], *pieces[:EARLY]],
             name="ready",
             aliases=((2, 0),),
         )
     pieces = pieces + [swap(p, 1, n) for p in moved]
-    late = list(range(EARLY, nb))
-    if fast and TAIL:
-        soon, late = late[:-TAIL], late[-TAIL:]
+    if fast:
+        soon, late = list(range(EARLY, nb - 1)), [nb - 1]
         hidden, agrad = call(
             functools.partial(more, soon),
             [units, units],
@@ -414,9 +401,9 @@
             name="more",
             aliases=((1, 0), (2, 1)),
         )
-    weights = pieces if n <= 16 else [jnp.stack(pieces)]
+    weights = pieces if fast else [jnp.stack(pieces)]
     nw = len(weights)
-    if n <= 16:
+    if fast:
         lists = (me, w1_rows, w1_cols, w2_rows, w2_cols)
 
         def bind(kernel, *given):
@@ -437,10 +424,9 @@
     outs = [panels, panels] + [blocks(half, BF16)] * parts + [blocks(half, F32)] * parts
     if fast:
         count = [half * len(g) for g in GROUPS]
-        mine = GROUPS[:SPLIT] if SPLIT else GROUPS
         _, _, act, hgrad, *out = call(
-            functools.partial(core, nb, parts, place, late, mine),
-            [units, units, panels, panels] + [blocks(c, BF16) for c in count[:len(mine)]] + [blocks(c, F32) for c in count[:len(mine)]],
+            functools.partial(core, nb, parts, place, late, GROUPS),
+            [units, units, panels, panels] + [blocks(c, BF16) for c in count] + [blocks(c, F32) for c in count],
             (),
             [table, hidden, agrad, tok, tok_t, ct, ct_t, *[pieces[s] for s in late]],
             [pltpu.VMEM((len(late), width, size), F32)] * 2,
@@ -476,19 +462,8 @@
         output, input_grad = call(bind(last, nb, nw), [model, model], lists, [act, hgrad, *weights], [total, total], 2 * work, "last")
 
     if fast:
-        sends, keeps = out[:len(mine)], out[len(mine):]
+        sends, keeps = out[:len(GROUPS)], out[len(GROUPS):]
         arrived = [swap(v, 1, n) for v in sends]
-        if SPLIT:
-            others = count[SPLIT:]
-            made = call(
-                functools.partial(rest, parts, place, GROUPS[SPLIT:]),
-                [blocks(c, BF16) for c in others] + [blocks(c, F32) for c in others],
-                (),
-                [arrived[0], tok_t, ct_t, act, hgrad],
-                name="rest",
-            )
-            keeps = [*keeps, *made[len(others):]]
-            arrived = [*arrived, *[swap(v, 1, n) for v in made[:len(others)]]]
 
         def sums(held, arrived, shapes):
             return call(functools.partial(fold, len(shapes)), shapes, (), [held, *arrived], name="fold")

time: 37.1 us -> 37.1 us (level)
  no operation moved by 1% of the time
where the time goes in v5:
time: 37.1 us; the launch traced here: 36.9 us
  starting transfers between devices  22.4 us (60%)
  Pallas kernels  6.98 us (19%)
  waiting for transfers between devices  6.69 us (18%)
  between operations  0.84 us (2%)
    ppermute x26, starting transfers between devices, swap(): return lax.ppermute(value, 'row', [(i, i ^ mask) for i in range(n)])  22.4 us
    pallas_call x14, Pallas kernels, call(): pl.pallas_call(kernel, out_shape=outs, in_specs=[SMEM] * len(smem) + [ANY...  6.98 us
    ppermute x26, waiting for transfers between devices, swap(): return lax.ppermute(value, 'row', [(i, i ^ mask) for i in range(n)])  6.69 us
  transfers between devices with their start and end apart: 26, of which 7 were waited for; matrix products, arithmetic and copies ran while one was open for 0% of the time, Pallas kernels for 11%

profile of v5, /device:TPU:1, one launch (start us, length us, event | category | flops | bytes accessed | tf_op | source)
XLA Modules:
  0.0 36.9 jit_solution(1926824964079632570)
XLA Ops:
  0.6 0.8 %begin.1.refs_0_.value = bf16[2,128,128]{2,1,0:T(8,128)(2,1)S(1)} custom-call(bf16[1,128,128]{2,1,0:T(8,128)(2,1)} %w1.1, bf16[1,128,128]{2,1,0:T(8,128)(2,1)} %w2.1), custom_call_target="tpu_custom_call" | custom-call | bytes 65544 | tf_op jit(solution)/shard_map/begin/pallas_call | solution.py:340
  1.4 0.0 copy-start
  1.4 0.0 copy-start.1
  1.5 0.0 copy-start.2
  1.5 0.0 copy-start.3
  1.5 0.0 copy-start.4
  1.5 0.0 copy-start.5
  1.5 2.8 %collective-permute-start.2 = (bf16[2,128,128]{2,1,0:T(8,128)(2,1)S(1)}, bf16[2,128,128]{2,1,0:T(8,128)(2,1)S(1)}, u32[]{:S(2)}, u32[]{:S(2)}) collective-permute-start(bf16[2,128,128]{2,1,0:T(8,128)(2,1)S(1)} %begin.1.refs_0_.value), channel_id=1, source_target_pairs={{0,5},{1,4},{2,7},{3,6},{4,1},{5,0},{6,3},{7,2},{8,13},{9,12},{10,... | collective-permute-start | bytes 196616 | tf_op jit(solution)/shard_map/ppermute | solution.py:58
  4.3 2.0 %collective-permute-start.1 = (bf16[2,128,128]{2,1,0:T(8,128)(2,1)S(1)}, bf16[2,128,128]{2,1,0:T(8,128)(2,1)S(1)}, u32[]{:S(2)}, u32[]{:S(2)}) collective-permute-start(bf16[2,128,128]{2,1,0:T(8,128)(2,1)S(1)} %begin.1.refs_0_.value), channel_id=1, source_target_pairs={{0,9},{1,8},{2,11},{3,10},{4,13},{5,12},{6,15},{7,14},{8,1},{9,0},... | collective-permute-start | bytes 196616 | tf_op jit(solution)/shard_map/ppermute | solution.py:58
  6.3 0.7 %collective-permute-start.7 = (bf16[2,128,128]{2,1,0:T(8,128)(2,1)S(1)}, bf16[2,128,128]{2,1,0:T(8,128)(2,1)S(1)}, u32[]{:S(2)}, u32[]{:S(2)}) collective-permute-start(bf16[2,128,128]{2,1,0:T(8,128)(2,1)S(1)} %begin.1.refs_0_.value), channel_id=1, source_target_pairs={{0,1},{1,0},{2,3},{3,2},{4,5},{5,4},{6,7},{7,6},{8,9},{9,8},{10,11... | collective-permute-start | bytes 196616 | tf_op jit(solution)/shard_map/ppermute | solution.py:58
  7.0 0.0 collective-permute-start
  7.0 0.1 collective-permute-start.9
  7.0 1.6 %collective-permute-start.5 = (bf16[2,128,128]{2,1,0:T(8,128)(2,1)S(1)}, bf16[2,128,128]{2,1,0:T(8,128)(2,1)S(1)}, u32[]{:S(2)}, u32[]{:S(2)}) collective-permute-start(bf16[2,128,128]{2,1,0:T(8,128)(2,1)S(1)} %collective-permute-done.2.refs_2_), channel_id=1, source_target_pairs={{0,3},{1,2},{2,1},{3,0},{4,7},{5,6},{6,5},{7,4},{8,11},{9,10},{10,... | collective-permute-start | bytes 196616 | tf_op jit(solution)/shard_map/ppermute | solution.py:58
  8.6 1.7 %collective-permute-done.1.refs_1_.other = bf16[2,128,128]{2,1,0:T(8,128)(2,1)S(1)} collective-permute-done((bf16[2,128,128]{2,1,0:T(8,128)(2,1)S(1)}, bf16[2,128,128]{2,1,0:T(8,128)(2,1)S(1)}, u32[]{:S(2)}, u32[]{:S(2)}) %collective-permute-start.1) | collective-permute-done | bytes 65568 | tf_op jit(solution)/shard_map/ppermute | solution.py:58
  10.3 0.1 collective-permute-start.3
  10.5 0.0 collective-permute-done.7.refs_4_.refs_8_
  10.5 1.5 %collective-permute-start.8 = (bf16[2,128,128]{2,1,0:T(8,128)(2,1)S(1)}, bf16[2,128,128]{2,1,0:T(8,128)(2,1)S(1)}, u32[]{:S(2)}, u32[]{:S(2)}) collective-permute-start(bf16[2,128,128]{2,1,0:T(8,128)(2,1)S(1)} %collective-permute-done.1.refs_1_.other), channel_id=1, source_target_pairs={{0,1},{1,0},{2,3},{3,2},{4,5},{5,4},{6,7},{7,6},{8,9},{9,8},{10,11... | collective-permute-start | bytes 196616 | tf_op jit(solution)/shard_map/ppermute | solution.py:58
  12.0 0.6 %collective-permute-done.refs_3_ = bf16[2,128,128]{2,1,0:T(8,128)(2,1)S(1)} collective-permute-done((bf16[2,128,128]{2,1,0:T(8,128)(2,1)S(1)}, bf16[2,128,128]{2,1,0:T(8,128)(2,1)S(1)}, u32[]{:S(2)}, u32[]{:S(2)}) %collective-permute-start) | collective-permute-done | bytes 65568 | tf_op jit(solution)/shard_map/ppermute | solution.py:58
  12.6 1.2 %collective-permute-start.4 = (bf16[2,128,128]{2,1,0:T(8,128)(2,1)S(1)}, bf16[2,128,128]{2,1,0:T(8,128)(2,1)S(1)}, u32[]{:S(2)}, u32[]{:S(2)}) collective-permute-start(bf16[2,128,128]{2,1,0:T(8,128)(2,1)S(1)} %collective-permute-done.1.refs_1_.other), channel_id=1, source_target_pairs={{0,3},{1,2},{2,1},{3,0},{4,7},{5,6},{6,5},{7,4},{8,11},{9,10},{10,... | collective-permute-start | bytes 196616 | tf_op jit(solution)/shard_map/ppermute | solution.py:58
  13.7 0.0 collective-permute-done.9.refs_6_.refs_10_
  13.7 0.6 %collective-permute-start.6 = (bf16[2,128,128]{2,1,0:T(8,128)(2,1)S(1)}, bf16[2,128,128]{2,1,0:T(8,128)(2,1)S(1)}, u32[]{:S(2)}, u32[]{:S(2)}) collective-permute-start(bf16[2,128,128]{2,1,0:T(8,128)(2,1)S(1)} %collective-permute-done.refs_3_), channel_id=1, source_target_pairs={{0,3},{1,2},{2,1},{3,0},{4,7},{5,6},{6,5},{7,4},{8,11},{9,10},{10,... | collective-permute-start | bytes 196616 | tf_op jit(solution)/shard_map/ppermute | solution.py:58
  14.4 1.4 %ready.1 = (bf16[2,128,128]{2,1,0:T(8,128)(2,1)S(1)}, f32[96,128,128]{2,1,0:T(8,128)S(1)}, f32[96,128,128]{2,1,0:T(8,128)S(1)}, bf16[16,128,128]{2,1,0:T(8,128)(...) custom-call(s32[1]{0:T(128)} %bitcast.me, ...), custom_call_target="tpu_custom_call", output_to_operand_aliasing={{0}: (7, {})} | custom-call | bytes 16650240 | tf_op jit(solution)/shard_map/ready/pallas_call | solution.py:340
  15.8 0.1 collective-permute-start.10
  15.9 0.0 collective-permute-done.3.refs_0_.refs_4_
  15.9 0.5 %collective-permute-start.13 = (bf16[2,128,128]{2,1,0:T(8,128)(2,1)S(1)}, bf16[2,128,128]{2,1,0:T(8,128)(2,1)S(1)}, u32[]{:S(2)}, u32[]{:S(2)}) collective-permute-start(bf16[2,128,128]{2,1,0:T(8,128)(2,1)S(1)} %collective-permute-done.5.refs_2_.refs_6_), channel_id=1, source_target_pairs={{0,1},{1,0},{2,3},{3,2},{4,5},{5,4},{6,7},{7,6},{8,9},{9,8},{10,11... | collective-permute-start | bytes 196616 | tf_op jit(solution)/shard_map/ppermute | solution.py:58
  16.3 0.1 collective-permute-start.11
  16.4 0.4 %collective-permute-start.12 = (bf16[2,128,128]{2,1,0:T(8,128)(2,1)S(1)}, bf16[2,128,128]{2,1,0:T(8,128)(2,1)S(1)}, u32[]{:S(2)}, u32[]{:S(2)}) collective-permute-start(bf16[2,128,128]{2,1,0:T(8,128)(2,1)S(1)} %collective-permute-done.4.refs_1_.refs_5_), channel_id=1, source_target_pairs={{0,1},{1,0},{2,3},{3,2},{4,5},{5,4},{6,7},{7,6},{8,9},{9,8},{10,11... | collective-permute-start | bytes 196616 | tf_op jit(solution)/shard_map/ppermute | solution.py:58
  16.9 1.1 %collective-permute-done.6.refs_3_.refs_7_ = bf16[2,128,128]{2,1,0:T(8,128)(2,1)S(1)} collective-permute-done((bf16[2,128,128]{2,1,0:T(8,128)(2,1)S(1)}, bf16[2,128,128]{2,1,0:T(8,128)(2,1)S(1)}, u32[]{:S(2)}, u32[]{:S(2)}) %collective-permute-start.6) | collective-permute-done | bytes 65568 | tf_op jit(solution)/shard_map/ppermute | solution.py:58
  18.0 0.4 %collective-permute-start.14 = (bf16[2,128,128]{2,1,0:T(8,128)(2,1)S(1)}, bf16[2,128,128]{2,1,0:T(8,128)(2,1)S(1)}, u32[]{:S(2)}, u32[]{:S(2)}) collective-permute-start(bf16[2,128,128]{2,1,0:T(8,128)(2,1)S(1)} %collective-permute-done.6.refs_3_.refs_7_), channel_id=1, source_target_pairs={{0,1},{1,0},{2,3},{3,2},{4,5},{5,4},{6,7},{7,6},{8,9},{9,8},{10,11... | collective-permute-start | bytes 196616 | tf_op jit(solution)/shard_map/ppermute | solution.py:58
  18.4 0.5 %more.1 = (f32[96,128,128]{2,1,0:T(8,128)S(1)}, f32[96,128,128]{2,1,0:T(8,128)S(1)}) custom-call(s32[8,128]{1,0:T(8,128)S(1)} %get-tuple-element.36.table, f32[96,128,128]{2,1,0:T(8,128)S(1)} %get-tuple-element.37.hidden_in, f32[96,128,128]{2,1,0:T(8,128)S(1)} %get-tuple-element.38.agrad_in, ...), custom_call_target="tpu_custom_call", output_to_operand_aliasing={{0}: (1, {}), {1}: (2, {})} | custom-call | bytes 28381184 | tf_op jit(solution)/shard_map/more/pallas_call | solution.py:340
  18.9 0.4 %collective-permute-done.14.refs_0_.refs_15_ = bf16[2,128,128]{2,1,0:T(8,128)(2,1)S(1)} collective-permute-done((bf16[2,128,128]{2,1,0:T(8,128)(2,1)S(1)}, bf16[2,128,128]{2,1,0:T(8,128)(2,1)S(1)}, u32[]{:S(2)}, u32[]{:S(2)}) %collective-permute-start.14) | collective-permute-done | bytes 65568 | tf_op jit(solution)/shard_map/ppermute | solution.py:58
  19.3 1.4 %middle.1 = (f32[96,128,128]{2,1,0:T(8,128)S(1)}, f32[96,128,128]{2,1,0:T(8,128)S(1)}, bf16[16,128,128]{2,1,0:T(8,128)(2,1)S(1)}, bf16[16,128,128]{2,1,0:T(8,128...) custom-call(s32[8,128]{1,0:T(8,128)S(1)} %get-tuple-element.36.table, ...), custom_call_target="tpu_custom_call", output_to_operand_aliasing={{0}: (1, {}), {1}: (2, {})} | custom-call | flops 268435456 | bytes 30085120 | tf_op jit(solution)/shard_map/middle/pallas_call | solution.py:340
  20.7 0.4 %collective-permute-start.17 = (bf16[2,2,128,128]{3,2,1,0:T(8,128)(2,1)S(1)}, bf16[2,2,128,128]{3,2,1,0:T(8,128)(2,1)S(1)}, u32[]{:S(2)}, u32[]{:S(2)}) collective-permute-start(bf16[2,2,128,128]{3,2,1,0:T(8,128)(2,1)S(1)} %get-tuple-element.55), channel_id=1, source_target_pairs={{0,1},{1,0},{2,3},{3,2},{4,5},{5,4},{6,7},{7,6},{8,9},{9,8},{10,11... | collective-permute-start | bytes 393224 | tf_op jit(solution)/shard_map/ppermute | solution.py:58
  21.1 0.2 collective-permute-start.20
  21.3 0.4 collective-permute-start.23
  21.7 0.2 collective-permute-start.15
  21.8 0.3 collective-permute-done.17.refs_0_
  22.2 1.0 %collective-permute-start.18 = (bf16[1,2,128,128]{3,2,1,0:T(8,128)(2,1)S(1)}, bf16[1,2,128,128]{3,2,1,0:T(8,128)(2,1)S(1)}, u32[]{:S(2)}, u32[]{:S(2)}) collective-permute-start(bf16[1,2,128,128]{3,2,1,0:T(8,128)(2,1)S(1)} %get-tuple-element.57), channel_id=1, source_target_pairs={{0,3},{1,2},{2,1},{3,0},{4,7},{5,6},{6,5},{7,4},{8,11},{9,10},{10,... | collective-permute-start | bytes 196616 | tf_op jit(solution)/shard_map/ppermute | solution.py:58
  23.2 0.8 %collective-permute-start.21 = (bf16[1,2,128,128]{3,2,1,0:T(8,128)(2,1)S(1)}, bf16[1,2,128,128]{3,2,1,0:T(8,128)(2,1)S(1)}, u32[]{:S(2)}, u32[]{:S(2)}) collective-permute-start(bf16[1,2,128,128]{3,2,1,0:T(8,128)(2,1)S(1)} %get-tuple-element.61), channel_id=1, source_target_pairs={{0,3},{1,2},{2,1},{3,0},{4,7},{5,6},{6,5},{7,4},{8,11},{9,10},{10,... | collective-permute-start | bytes 196616 | tf_op jit(solution)/shard_map/ppermute | solution.py:58
  24.1 1.0 %collective-permute-start.24 = (bf16[1,2,128,128]{3,2,1,0:T(8,128)(2,1)S(1)}, bf16[1,2,128,128]{3,2,1,0:T(8,128)(2,1)S(1)}, u32[]{:S(2)}, u32[]{:S(2)}) collective-permute-start(bf16[1,2,128,128]{3,2,1,0:T(8,128)(2,1)S(1)} %get-tuple-element.65), channel_id=1, source_target_pairs={{0,3},{1,2},{2,1},{3,0},{4,7},{5,6},{6,5},{7,4},{8,11},{9,10},{10,... | collective-permute-start | bytes 196616 | tf_op jit(solution)/shard_map/ppermute | solution.py:58
  25.2 0.8 %collective-permute-start.16 = (bf16[1,2,128,128]{3,2,1,0:T(8,128)(2,1)S(1)}, bf16[1,2,128,128]{3,2,1,0:T(8,128)(2,1)S(1)}, u32[]{:S(2)}, u32[]{:S(2)}) collective-permute-start(bf16[1,2,128,128]{3,2,1,0:T(8,128)(2,1)S(1)} %get-tuple-element.53), channel_id=1, source_target_pairs={{0,3},{1,2},{2,1},{3,0},{4,7},{5,6},{6,5},{7,4},{8,11},{9,10},{10,... | collective-permute-start | bytes 196616 | tf_op jit(solution)/shard_map/ppermute | solution.py:58
  26.0 0.9 %collective-permute-done.18.refs_0_ = bf16[1,2,128,128]{3,2,1,0:T(8,128)(2,1)S(1)} collective-permute-done((bf16[1,2,128,128]{3,2,1,0:T(8,128)(2,1)S(1)}, bf16[1,2,128,128]{3,2,1,0:T(8,128)(2,1)S(1)}, u32[]{:S(2)}, u32[]{:S(2)}) %collective-permute-start.18) | collective-permute-done | bytes 65568 | tf_op jit(solution)/shard_map/ppermute | solution.py:58
  27.0 1.6 %collective-permute-start.19 = (bf16[1,2,128,128]{3,2,1,0:T(8,128)(2,1)S(1)}, bf16[1,2,128,128]{3,2,1,0:T(8,128)(2,1)S(1)}, u32[]{:S(2)}, u32[]{:S(2)}) collective-permute-start(bf16[1,2,128,128]{3,2,1,0:T(8,128)(2,1)S(1)} %fold.9), channel_id=1, source_target_pairs={{0,9},{1,8},{2,11},{3,10},{4,13},{5,12},{6,15},{7,14},{8,1},{9,0},... | collective-permute-start | bytes 196616 | tf_op jit(solution)/shard_map/ppermute | solution.py:58
  28.6 2.1 %collective-permute-start.22 = (bf16[1,2,128,128]{3,2,1,0:T(8,128)(2,1)S(1)}, bf16[1,2,128,128]{3,2,1,0:T(8,128)(2,1)S(1)}, u32[]{:S(2)}, u32[]{:S(2)}) collective-permute-start(bf16[1,2,128,128]{3,2,1,0:T(8,128)(2,1)S(1)} %fold.11), channel_id=1, source_target_pairs={{0,5},{1,4},{2,7},{3,6},{4,1},{5,0},{6,3},{7,2},{8,13},{9,12},{10,... | collective-permute-start | bytes 196616 | tf_op jit(solution)/shard_map/ppermute | solution.py:58
  30.6 2.0 %collective-permute-start.25 = (bf16[1,2,128,128]{3,2,1,0:T(8,128)(2,1)S(1)}, bf16[1,2,128,128]{3,2,1,0:T(8,128)(2,1)S(1)}, u32[]{:S(2)}, u32[]{:S(2)}) collective-permute-start(bf16[1,2,128,128]{3,2,1,0:T(8,128)(2,1)S(1)} %fold.13), channel_id=1, source_target_pairs={{0,13},{1,12},{2,15},{3,14},{4,9},{5,8},{6,11},{7,10},{8,5},{9,4},... | collective-permute-start | bytes 196616 | tf_op jit(solution)/shard_map/ppermute | solution.py:58
  32.6 2.0 %last.1 = (bf16[128,3072]{1,0:T(8,128)(2,1)}, bf16[128,3072]{1,0:T(8,128)(2,1)}) custom-call(s32[8,128]{1,0:T(8,128)S(1)} %get-tuple-element.36.table, bf16[16,128,128]{2,1,0:T(8,128)(2,1)S(1)} %get-tuple-element.46.act, bf16[16,128,128]{2,1,0:T(8,128)(2,1)S(1)} %get-tuple-element.47.hgrad, bf16[2,128,128]{2,1,0:T(8,128)(2,1)S(1)} %begin.1.refs_0_.value, ...), custom_call_target="tpu_custom_call" | custom-call | flops 134217728 | bytes 9965600 | tf_op jit(solution)/shard_map/last/pallas_call | solution.py:340
  34.6 1.6 %collective-permute-done.25.refs_3_ = bf16[1,2,128,128]{3,2,1,0:T(8,128)(2,1)S(1)} collective-permute-done((bf16[1,2,128,128]{3,2,1,0:T(8,128)(2,1)S(1)}, bf16[1,2,128,128]{3,2,1,0:T(8,128)(2,1)S(1)}, u32[]{:S(2)}, u32[]{:S(2)}) %collective-permute-start.25) | collective-permute-done | bytes 65568 | tf_op jit(solution)/shard_map/ppermute | solution.py:58
  36.2 0.7 %close.1 = (f32[1,128,128]{2,1,0:T(8,128)}, f32[1,128,128]{2,1,0:T(8,128)}) custom-call(f32[1,2,128,128]{3,2,1,0:T(8,128)S(1)} %get-tuple-element.52.held, bf16[1,2,128,128]{3,2,1,0:T(8,128)(2,1)S(1)} %collective-permute-done.16.refs_0_, bf16[1,2,128,128]{3,2,1,0:T(8,128)(2,1)S(1)} %collective-permute-done.19.refs_1_, ...), custom_call_target="tpu_custom_call" | custom-call | bytes 524288 | tf_op jit(solution)/shard_map/close/pallas_call | solution.py:340
  (31 shorter events, 0.2 us)
Async XLA Ops:
  1.4 12.9 %copy-start = (bf16[128,3072]{1,0:T(8,128)(2,1)S(1)}, bf16[128,3072]{1,0:T(8,128)(2,1)}, u32[]{:S(2)}) copy-start(bf16[128,3072]{1,0:T(8,128)(2,1)} %tokens.1) | copy-start | bytes 2359300
  1.4 12.9 %copy-start.1 = (bf16[128,3072]{1,0:T(8,128)(2,1)S(1)}, bf16[128,3072]{1,0:T(8,128)(2,1)}, u32[]{:S(2)}) copy-start(bf16[128,3072]{1,0:T(8,128)(2,1)} %cot.1) | copy-start | bytes 2359300
  1.5 12.9 %copy-start.2 = (s32[16]{0:T(128)S(1)}, s32[16]{0:T(128)}, u32[]{:S(2)}) copy-start(s32[16]{0:T(128)} %r1.1) | copy-start | bytes 196
  1.5 12.9 %copy-start.3 = (s32[16]{0:T(128)S(1)}, s32[16]{0:T(128)}, u32[]{:S(2)}) copy-start(s32[16]{0:T(128)} %c1.1) | copy-start | bytes 196
  1.5 12.9 %copy-start.4 = (s32[16]{0:T(128)S(1)}, s32[16]{0:T(128)}, u32[]{:S(2)}) copy-start(s32[16]{0:T(128)} %r2.1) | copy-start | bytes 196
  1.5 12.9 %copy-start.5 = (s32[16]{0:T(128)S(1)}, s32[16]{0:T(128)}, u32[]{:S(2)}) copy-start(s32[16]{0:T(128)} %c2.1) | copy-start | bytes 196
  1.5 5.5 %collective-permute-start.2 = (bf16[2,128,128]{2,1,0:T(8,128)(2,1)S(1)}, bf16[2,128,128]{2,1,0:T(8,128)(2,1)S(1)}, u32[]{:S(2)}, u32[]{:S(2)}) collective-permute-start(bf16[2,128,128]{2,1,0:T(8,128)(2,1)S(1)} %begin.1.refs_0_.value), channel_id=1, source_target_pairs={{0,5},{1,4},{2,7},{3,6},{4,1},{5,0},{6,3},{7,2},{8,13},{9,12},{10,... | collective-permute-start | bytes 196616 | tf_op jit(solution)/shard_map/ppermute | solution.py:58
  4.3 6.1 %collective-permute-start.1 = (bf16[2,128,128]{2,1,0:T(8,128)(2,1)S(1)}, bf16[2,128,128]{2,1,0:T(8,128)(2,1)S(1)}, u32[]{:S(2)}, u32[]{:S(2)}) collective-permute-start(bf16[2,128,128]{2,1,0:T(8,128)(2,1)S(1)} %begin.1.refs_0_.value), channel_id=1, source_target_pairs={{0,9},{1,8},{2,11},{3,10},{4,13},{5,12},{6,15},{7,14},{8,1},{9,0},... | collective-permute-start | bytes 196616 | tf_op jit(solution)/shard_map/ppermute | solution.py:58
  6.3 4.2 %collective-permute-start.7 = (bf16[2,128,128]{2,1,0:T(8,128)(2,1)S(1)}, bf16[2,128,128]{2,1,0:T(8,128)(2,1)S(1)}, u32[]{:S(2)}, u32[]{:S(2)}) collective-permute-start(bf16[2,128,128]{2,1,0:T(8,128)(2,1)S(1)} %begin.1.refs_0_.value), channel_id=1, source_target_pairs={{0,1},{1,0},{2,3},{3,2},{4,5},{5,4},{6,7},{7,6},{8,9},{9,8},{10,11... | collective-permute-start | bytes 196616 | tf_op jit(solution)/shard_map/ppermute | solution.py:58
  7.0 5.6 %collective-permute-start = (bf16[2,128,128]{2,1,0:T(8,128)(2,1)S(1)}, bf16[2,128,128]{2,1,0:T(8,128)(2,1)S(1)}, u32[]{:S(2)}, u32[]{:S(2)}) collective-permute-start(bf16[2,128,128]{2,1,0:T(8,128)(2,1)S(1)} %begin.1.refs_0_.value), channel_id=1, source_target_pairs={{0,13},{1,12},{2,15},{3,14},{4,9},{5,8},{6,11},{7,10},{8,5},{9,4},... | collective-permute-start | bytes 196616 | tf_op jit(solution)/shard_map/ppermute | solution.py:58
  7.0 6.8 %collective-permute-start.9 = (bf16[2,128,128]{2,1,0:T(8,128)(2,1)S(1)}, bf16[2,128,128]{2,1,0:T(8,128)(2,1)S(1)}, u32[]{:S(2)}, u32[]{:S(2)}) collective-permute-start(bf16[2,128,128]{2,1,0:T(8,128)(2,1)S(1)} %collective-permute-done.2.refs_2_), channel_id=1, source_target_pairs={{0,1},{1,0},{2,3},{3,2},{4,5},{5,4},{6,7},{7,6},{8,9},{9,8},{10,11... | collective-permute-start | bytes 196616 | tf_op jit(solution)/shard_map/ppermute | solution.py:58
  7.0 8.7 %collective-permute-start.5 = (bf16[2,128,128]{2,1,0:T(8,128)(2,1)S(1)}, bf16[2,128,128]{2,1,0:T(8,128)(2,1)S(1)}, u32[]{:S(2)}, u32[]{:S(2)}) collective-permute-start(bf16[2,128,128]{2,1,0:T(8,128)(2,1)S(1)} %collective-permute-done.2.refs_2_), channel_id=1, source_target_pairs={{0,3},{1,2},{2,1},{3,0},{4,7},{5,6},{6,5},{7,4},{8,11},{9,10},{10,... | collective-permute-start | bytes 196616 | tf_op jit(solution)/shard_map/ppermute | solution.py:58
  10.3 5.5 %collective-permute-start.3 = (bf16[2,128,128]{2,1,0:T(8,128)(2,1)S(1)}, bf16[2,128,128]{2,1,0:T(8,128)(2,1)S(1)}, u32[]{:S(2)}, u32[]{:S(2)}) collective-permute-start(bf16[2,128,128]{2,1,0:T(8,128)(2,1)S(1)} %after.1), channel_id=1, source_target_pairs={{0,3},{1,2},{2,1},{3,0},{4,7},{5,6},{6,5},{7,4},{8,11},{9,10},{10,... | collective-permute-start | bytes 196616 | tf_op jit(solution)/shard_map/ppermute | solution.py:58
  10.5 5.9 %collective-permute-start.8 = (bf16[2,128,128]{2,1,0:T(8,128)(2,1)S(1)}, bf16[2,128,128]{2,1,0:T(8,128)(2,1)S(1)}, u32[]{:S(2)}, u32[]{:S(2)}) collective-permute-start(bf16[2,128,128]{2,1,0:T(8,128)(2,1)S(1)} %collective-permute-done.1.refs_1_.other), channel_id=1, source_target_pairs={{0,1},{1,0},{2,3},{3,2},{4,5},{5,4},{6,7},{7,6},{8,9},{9,8},{10,11... | collective-permute-start | bytes 196616 | tf_op jit(solution)/shard_map/ppermute | solution.py:58
  12.6 3.9 %collective-permute-start.4 = (bf16[2,128,128]{2,1,0:T(8,128)(2,1)S(1)}, bf16[2,128,128]{2,1,0:T(8,128)(2,1)S(1)}, u32[]{:S(2)}, u32[]{:S(2)}) collective-permute-start(bf16[2,128,128]{2,1,0:T(8,128)(2,1)S(1)} %collective-permute-done.1.refs_1_.other), channel_id=1, source_target_pairs={{0,3},{1,2},{2,1},{3,0},{4,7},{5,6},{6,5},{7,4},{8,11},{9,10},{10,... | collective-permute-start | bytes 196616 | tf_op jit(solution)/shard_map/ppermute | solution.py:58
  13.7 4.3 %collective-permute-start.6 = (bf16[2,128,128]{2,1,0:T(8,128)(2,1)S(1)}, bf16[2,128,128]{2,1,0:T(8,128)(2,1)S(1)}, u32[]{:S(2)}, u32[]{:S(2)}) collective-permute-start(bf16[2,128,128]{2,1,0:T(8,128)(2,1)S(1)} %collective-permute-done.refs_3_), channel_id=1, source_target_pairs={{0,3},{1,2},{2,1},{3,0},{4,7},{5,6},{6,5},{7,4},{8,11},{9,10},{10,... | collective-permute-start | bytes 196616 | tf_op jit(solution)/shard_map/ppermute | solution.py:58
  15.8 2.6 %collective-permute-start.10 = (bf16[2,128,128]{2,1,0:T(8,128)(2,1)S(1)}, bf16[2,128,128]{2,1,0:T(8,128)(2,1)S(1)}, u32[]{:S(2)}, u32[]{:S(2)}) collective-permute-start(bf16[2,128,128]{2,1,0:T(8,128)(2,1)S(1)} %get-tuple-element.41), channel_id=1, source_target_pairs={{0,1},{1,0},{2,3},{3,2},{4,5},{5,4},{6,7},{7,6},{8,9},{9,8},{10,11... | collective-permute-start | bytes 196616 | tf_op jit(solution)/shard_map/ppermute | solution.py:58
  15.9 2.5 %collective-permute-start.13 = (bf16[2,128,128]{2,1,0:T(8,128)(2,1)S(1)}, bf16[2,128,128]{2,1,0:T(8,128)(2,1)S(1)}, u32[]{:S(2)}, u32[]{:S(2)}) collective-permute-start(bf16[2,128,128]{2,1,0:T(8,128)(2,1)S(1)} %collective-permute-done.5.refs_2_.refs_6_), channel_id=1, source_target_pairs={{0,1},{1,0},{2,3},{3,2},{4,5},{5,4},{6,7},{7,6},{8,9},{9,8},{10,11... | collective-permute-start | bytes 196616 | tf_op jit(solution)/shard_map/ppermute | solution.py:58
  16.3 2.1 %collective-permute-start.11 = (bf16[2,128,128]{2,1,0:T(8,128)(2,1)S(1)}, bf16[2,128,128]{2,1,0:T(8,128)(2,1)S(1)}, u32[]{:S(2)}, u32[]{:S(2)}) collective-permute-start(bf16[2,128,128]{2,1,0:T(8,128)(2,1)S(1)} %collective-permute-done.3.refs_0_.refs_4_), channel_id=1, source_target_pairs={{0,1},{1,0},{2,3},{3,2},{4,5},{5,4},{6,7},{7,6},{8,9},{9,8},{10,11... | collective-permute-start | bytes 196616 | tf_op jit(solution)/shard_map/ppermute | solution.py:58
  16.4 2.0 %collective-permute-start.12 = (bf16[2,128,128]{2,1,0:T(8,128)(2,1)S(1)}, bf16[2,128,128]{2,1,0:T(8,128)(2,1)S(1)}, u32[]{:S(2)}, u32[]{:S(2)}) collective-permute-start(bf16[2,128,128]{2,1,0:T(8,128)(2,1)S(1)} %collective-permute-done.4.refs_1_.refs_5_), channel_id=1, source_target_pairs={{0,1},{1,0},{2,3},{3,2},{4,5},{5,4},{6,7},{7,6},{8,9},{9,8},{10,11... | collective-permute-start | bytes 196616 | tf_op jit(solution)/shard_map/ppermute | solution.py:58
  18.0 1.3 %collective-permute-start.14 = (bf16[2,128,128]{2,1,0:T(8,128)(2,1)S(1)}, bf16[2,128,128]{2,1,0:T(8,128)(2,1)S(1)}, u32[]{:S(2)}, u32[]{:S(2)}) collective-permute-start(bf16[2,128,128]{2,1,0:T(8,128)(2,1)S(1)} %collective-permute-done.6.refs_3_.refs_7_), channel_id=1, source_target_pairs={{0,1},{1,0},{2,3},{3,2},{4,5},{5,4},{6,7},{7,6},{8,9},{9,8},{10,11... | collective-permute-start | bytes 196616 | tf_op jit(solution)/shard_map/ppermute | solution.py:58
  20.7 1.4 %collective-permute-start.17 = (bf16[2,2,128,128]{3,2,1,0:T(8,128)(2,1)S(1)}, bf16[2,2,128,128]{3,2,1,0:T(8,128)(2,1)S(1)}, u32[]{:S(2)}, u32[]{:S(2)}) collective-permute-start(bf16[2,2,128,128]{3,2,1,0:T(8,128)(2,1)S(1)} %get-tuple-element.55), channel_id=1, source_target_pairs={{0,1},{1,0},{2,3},{3,2},{4,5},{5,4},{6,7},{7,6},{8,9},{9,8},{10,11... | collective-permute-start | bytes 393224 | tf_op jit(solution)/shard_map/ppermute | solution.py:58
  21.1 2.1 %collective-permute-start.20 = (bf16[2,2,128,128]{3,2,1,0:T(8,128)(2,1)S(1)}, bf16[2,2,128,128]{3,2,1,0:T(8,128)(2,1)S(1)}, u32[]{:S(2)}, u32[]{:S(2)}) collective-permute-start(bf16[2,2,128,128]{3,2,1,0:T(8,128)(2,1)S(1)} %get-tuple-element.59), channel_id=1, source_target_pairs={{0,1},{1,0},{2,3},{3,2},{4,5},{5,4},{6,7},{7,6},{8,9},{9,8},{10,11... | collective-permute-start | bytes 393224 | tf_op jit(solution)/shard_map/ppermute | solution.py:58
  21.3 2.8 %collective-permute-start.23 = (bf16[2,2,128,128]{3,2,1,0:T(8,128)(2,1)S(1)}, bf16[2,2,128,128]{3,2,1,0:T(8,128)(2,1)S(1)}, u32[]{:S(2)}, u32[]{:S(2)}) collective-permute-start(bf16[2,2,128,128]{3,2,1,0:T(8,128)(2,1)S(1)} %get-tuple-element.63), channel_id=1, source_target_pairs={{0,1},{1,0},{2,3},{3,2},{4,5},{5,4},{6,7},{7,6},{8,9},{9,8},{10,11... | collective-permute-start | bytes 393224 | tf_op jit(solution)/shard_map/ppermute | solution.py:58
  21.7 3.5 %collective-permute-start.15 = (bf16[2,2,128,128]{3,2,1,0:T(8,128)(2,1)S(1)}, bf16[2,2,128,128]{3,2,1,0:T(8,128)(2,1)S(1)}, u32[]{:S(2)}, u32[]{:S(2)}) collective-permute-start(bf16[2,2,128,128]{3,2,1,0:T(8,128)(2,1)S(1)} %get-tuple-element.51), channel_id=1, source_target_pairs={{0,1},{1,0},{2,3},{3,2},{4,5},{5,4},{6,7},{7,6},{8,9},{9,8},{10,11... | collective-permute-start | bytes 393224 | tf_op jit(solution)/shard_map/ppermute | solution.py:58
  22.2 4.8 %collective-permute-start.18 = (bf16[1,2,128,128]{3,2,1,0:T(8,128)(2,1)S(1)}, bf16[1,2,128,128]{3,2,1,0:T(8,128)(2,1)S(1)}, u32[]{:S(2)}, u32[]{:S(2)}) collective-permute-start(bf16[1,2,128,128]{3,2,1,0:T(8,128)(2,1)S(1)} %get-tuple-element.57), channel_id=1, source_target_pairs={{0,3},{1,2},{2,1},{3,0},{4,7},{5,6},{6,5},{7,4},{8,11},{9,10},{10,... | collective-permute-start | bytes 196616 | tf_op jit(solution)/shard_map/ppermute | solution.py:58
  23.2 5.3 %collective-permute-start.21 = (bf16[1,2,128,128]{3,2,1,0:T(8,128)(2,1)S(1)}, bf16[1,2,128,128]{3,2,1,0:T(8,128)(2,1)S(1)}, u32[]{:S(2)}, u32[]{:S(2)}) collective-permute-start(bf16[1,2,128,128]{3,2,1,0:T(8,128)(2,1)S(1)} %get-tuple-element.61), channel_id=1, source_target_pairs={{0,3},{1,2},{2,1},{3,0},{4,7},{5,6},{6,5},{7,4},{8,11},{9,10},{10,... | collective-permute-start | bytes 196616 | tf_op jit(solution)/shard_map/ppermute | solution.py:58
  24.1 6.5 %collective-permute-start.24 = (bf16[1,2,128,128]{3,2,1,0:T(8,128)(2,1)S(1)}, bf16[1,2,128,128]{3,2,1,0:T(8,128)(2,1)S(1)}, u32[]{:S(2)}, u32[]{:S(2)}) collective-permute-start(bf16[1,2,128,128]{3,2,1,0:T(8,128)(2,1)S(1)} %get-tuple-element.65), channel_id=1, source_target_pairs={{0,3},{1,2},{2,1},{3,0},{4,7},{5,6},{6,5},{7,4},{8,11},{9,10},{10,... | collective-permute-start | bytes 196616 | tf_op jit(solution)/shard_map/ppermute | solution.py:58
  25.2 9.4 %collective-permute-start.16 = (bf16[1,2,128,128]{3,2,1,0:T(8,128)(2,1)S(1)}, bf16[1,2,128,128]{3,2,1,0:T(8,128)(2,1)S(1)}, u32[]{:S(2)}, u32[]{:S(2)}) collective-permute-start(bf16[1,2,128,128]{3,2,1,0:T(8,128)(2,1)S(1)} %get-tuple-element.53), channel_id=1, source_target_pairs={{0,3},{1,2},{2,1},{3,0},{4,7},{5,6},{6,5},{7,4},{8,11},{9,10},{10,... | collective-permute-start | bytes 196616 | tf_op jit(solution)/shard_map/ppermute | solution.py:58
  27.0 7.6 %collective-permute-start.19 = (bf16[1,2,128,128]{3,2,1,0:T(8,128)(2,1)S(1)}, bf16[1,2,128,128]{3,2,1,0:T(8,128)(2,1)S(1)}, u32[]{:S(2)}, u32[]{:S(2)}) collective-permute-start(bf16[1,2,128,128]{3,2,1,0:T(8,128)(2,1)S(1)} %fold.9), channel_id=1, source_target_pairs={{0,9},{1,8},{2,11},{3,10},{4,13},{5,12},{6,15},{7,14},{8,1},{9,0},... | collective-permute-start | bytes 196616 | tf_op jit(solution)/shard_map/ppermute | solution.py:58
  28.6 6.1 %collective-permute-start.22 = (bf16[1,2,128,128]{3,2,1,0:T(8,128)(2,1)S(1)}, bf16[1,2,128,128]{3,2,1,0:T(8,128)(2,1)S(1)}, u32[]{:S(2)}, u32[]{:S(2)}) collective-permute-start(bf16[1,2,128,128]{3,2,1,0:T(8,128)(2,1)S(1)} %fold.11), channel_id=1, source_target_pairs={{0,5},{1,4},{2,7},{3,6},{4,1},{5,0},{6,3},{7,2},{8,13},{9,12},{10,... | collective-permute-start | bytes 196616 | tf_op jit(solution)/shard_map/ppermute | solution.py:58
  30.6 5.6 %collective-permute-start.25 = (bf16[1,2,128,128]{3,2,1,0:T(8,128)(2,1)S(1)}, bf16[1,2,128,128]{3,2,1,0:T(8,128)(2,1)S(1)}, u32[]{:S(2)}, u32[]{:S(2)}) collective-permute-start(bf16[1,2,128,128]{3,2,1,0:T(8,128)(2,1)S(1)} %fold.13), channel_id=1, source_target_pairs={{0,13},{1,12},{2,15},{3,14},{4,9},{5,8},{6,11},{7,10},{8,5},{9,4},... | collective-permute-start | bytes 196616 | tf_op jit(solution)/shard_map/ppermute | solution.py:58

commit v6 on v5

--- a/solution.py
+++ b/solution.py
@@ -12,7 +12,7 @@
 AHEAD = 10**10
 CHUNK = 6
 EARLY = 4
-GROUPS = ((1,), (2,), (3,), (0,))
+GROUPS = ((1,), (2,), (0,), (3,))
 ROOT = math.sqrt(2.0 / math.pi)
 CUBE = 0.044715
 F32 = jnp.float32
@@ -207,34 +207,44 @@
         copy.wait()
 
 
-def ready(nb, order, me, r1, c1, r2, c2, tokens, cot, piece, *refs):
-    weights, (passed, hidden, agrad, tok, tok_t, ct, ct_t, table) = refs[:-8], refs[-8:]
+def ready(nb, order, r1, c1, r2, c2, tokens, cot, piece, *refs):
+    weights, (passed, hidden, agrad, tok, tok_t, ct, ct_t, table, lists) = refs[:-9], refs[-9:]
     del piece, passed
-    at = Lists(me, order, r1, c1, r2, c2)
+    me = lax.axis_index("row")
+    for k, ref in enumerate((c1, r2, r1, c2)):
+        lists[k:k + 1, :nb] = ref[...]
+    lane = lax.broadcasted_iota(jnp.int32, lists.shape, 1)
+    value, bit = lists[...], 1
+    while bit < nb:
+        other = jnp.where(lane & bit == 0, pltpu.roll(value, 128 - bit, 1), pltpu.roll(value, bit, 1))
+        value = jnp.where(me & bit == 0, value, other)
+        bit *= 2
+    lists[...] = value
+    c1, r2, r1, c2 = ([lists[k, o] for o in order] for k in range(4))
     size = tok.shape[-1]
     zero = jnp.zeros(hidden.shape[1:], F32)
     for s in range(nb):
-        hidden[at.c1(s)] = zero
-        hidden[at.r2(s)] = zero
-        agrad[at.c1(s)] = zero
-        agrad[at.r2(s)] = zero
+        hidden[c1[s]] = zero
+        hidden[r2[s]] = zero
+        agrad[c1[s]] = zero
+        agrad[r2[s]] = zero
     lane = lax.broadcasted_iota(jnp.int32, table.shape, 1)
     row = lax.broadcasted_iota(jnp.int32, table.shape, 0)
     entries = jnp.zeros(table.shape, jnp.int32)
     for s in range(nb):
-        value = jnp.where(row < 2, jnp.where(row == 0, at.c1(s), at.r2(s)), jnp.where(row == 2, at.r1(s), at.c2(s)))
+        value = jnp.where(row < 2, jnp.where(row == 0, c1[s], r2[s]), jnp.where(row == 2, r1[s], c2[s]))
         entries = jnp.where(lane == s, value, entries)
     table[...] = entries
     for s in range(nb):
-        value = panel(tokens, at.r1(s), size)
+        value = panel(tokens, r1[s], size)
         tok[s] = value
         tok_t[s] = value.T
-        value = panel(cot, at.c2(s), size)
+        value = panel(cot, c2[s], size)
         ct[s] = value
         ct_t[s] = value.T
     for s, w in enumerate(weights):
-        hidden[at.c1(s)] += dot(tok[s], w[0], ((1,), (0,)))
-        agrad[at.r2(s)] += dot(ct[s], w[1], ((1,), (1,)))
+        hidden[c1[s]] += dot(tok[s], w[0], ((1,), (0,)))
+        agrad[r2[s]] += dot(ct[s], w[1], ((1,), (1,)))
 
 
 def add_products(late, table, tok, ct, refs, hidden, agrad, prod, prod_t):
@@ -384,10 +394,11 @@
         moved[3], hidden, agrad, tok, tok_t, ct, ct_t, table = call(
             functools.partial(ready, nb, order),
             [jax.ShapeDtypeStruct(own.shape, BF16), units, units, panels, panels, panels, panels, jax.ShapeDtypeStruct((8, 128), jnp.int32)],
-            (me, w1_rows, w1_cols, w2_rows, w2_cols),
-            [tokens, cotangent, pieces[3], *pieces[:EARLY]],
+            (),
+            [*[v.reshape(1, nb) for v in (w1_rows, w1_cols, w2_rows, w2_cols)], tokens, cotangent, pieces[3], *pieces[:EARLY]],
+            [pltpu.VMEM((8, 128), jnp.int32)],
             name="ready",
-            aliases=((2, 0),),
+            aliases=((6, 0),),
         )
     pieces = pieces + [swap(p, 1, n) for p in moved]
     if fast:

time: 37.1 us -> 37.1 us (level)
  no operation moved by 1% of the time
where the time goes in v6:
time: 37.1 us; the launch traced here: 36.9 us
  starting transfers between devices  22.4 us (60%)
  Pallas kernels  6.86 us (18%)
  waiting for transfers between devices  6.79 us (18%)
  between operations  0.84 us (2%)
    ppermute x26, starting transfers between devices, swap(): return lax.ppermute(value, 'row', [(i, i ^ mask) for i in range(n)])  22.4 us
    pallas_call x14, Pallas kernels, call(): pl.pallas_call(kernel, out_shape=outs, in_specs=[SMEM] * len(smem) + [ANY...  6.86 us
    ppermute x26, waiting for transfers between devices, swap(): return lax.ppermute(value, 'row', [(i, i ^ mask) for i in range(n)])  6.79 us
  transfers between devices with their start and end apart: 26, of which 7 were waited for; matrix products, arithmetic and copies ran while one was open for 0% of the time, Pallas kernels for 11%

profile of v6, /device:TPU:1, one launch (start us, length us, event | category | flops | bytes accessed | tf_op | source)
XLA Modules:
  0.0 36.9 jit_solution(7109289087770198625)
XLA Ops:
  0.6 0.8 %begin.1.refs_0_.value = bf16[2,128,128]{2,1,0:T(8,128)(2,1)S(1)} custom-call(bf16[1,128,128]{2,1,0:T(8,128)(2,1)} %w1.1, bf16[1,128,128]{2,1,0:T(8,128)(2,1)} %w2.1), custom_call_target="tpu_custom_call" | custom-call | bytes 65544 | tf_op jit(solution)/shard_map/begin/pallas_call | solution.py:350
  1.4 0.0 copy-start
  1.4 0.0 copy-start.1
  1.5 0.0 copy-start.2
  1.5 0.0 copy-start.3
  1.5 0.0 copy-start.4
  1.5 0.0 copy-start.5
  1.5 2.8 %collective-permute-start.2 = (bf16[2,128,128]{2,1,0:T(8,128)(2,1)S(1)}, bf16[2,128,128]{2,1,0:T(8,128)(2,1)S(1)}, u32[]{:S(2)}, u32[]{:S(2)}) collective-permute-start(bf16[2,128,128]{2,1,0:T(8,128)(2,1)S(1)} %begin.1.refs_0_.value), channel_id=1, source_target_pairs={{0,5},{1,4},{2,7},{3,6},{4,1},{5,0},{6,3},{7,2},{8,13},{9,12},{10,... | collective-permute-start | bytes 196616 | tf_op jit(solution)/shard_map/ppermute | solution.py:58
  4.3 2.0 %collective-permute-start.1 = (bf16[2,128,128]{2,1,0:T(8,128)(2,1)S(1)}, bf16[2,128,128]{2,1,0:T(8,128)(2,1)S(1)}, u32[]{:S(2)}, u32[]{:S(2)}) collective-permute-start(bf16[2,128,128]{2,1,0:T(8,128)(2,1)S(1)} %begin.1.refs_0_.value), channel_id=1, source_target_pairs={{0,9},{1,8},{2,11},{3,10},{4,13},{5,12},{6,15},{7,14},{8,1},{9,0},... | collective-permute-start | bytes 196616 | tf_op jit(solution)/shard_map/ppermute | solution.py:58
  6.3 0.7 %collective-permute-start.7 = (bf16[2,128,128]{2,1,0:T(8,128)(2,1)S(1)}, bf16[2,128,128]{2,1,0:T(8,128)(2,1)S(1)}, u32[]{:S(2)}, u32[]{:S(2)}) collective-permute-start(bf16[2,128,128]{2,1,0:T(8,128)(2,1)S(1)} %begin.1.refs_0_.value), channel_id=1, source_target_pairs={{0,1},{1,0},{2,3},{3,2},{4,5},{5,4},{6,7},{7,6},{8,9},{9,8},{10,11... | collective-permute-start | bytes 196616 | tf_op jit(solution)/shard_map/ppermute | solution.py:58
  7.0 0.0 collective-permute-start
  7.0 0.0 collective-permute-done.2.refs_2_
  7.0 0.1 collective-permute-start.9
  7.0 1.6 %collective-permute-start.5 = (bf16[2,128,128]{2,1,0:T(8,128)(2,1)S(1)}, bf16[2,128,128]{2,1,0:T(8,128)(2,1)S(1)}, u32[]{:S(2)}, u32[]{:S(2)}) collective-permute-start(bf16[2,128,128]{2,1,0:T(8,128)(2,1)S(1)} %collective-permute-done.2.refs_2_), channel_id=1, source_target_pairs={{0,3},{1,2},{2,1},{3,0},{4,7},{5,6},{6,5},{7,4},{8,11},{9,10},{10,... | collective-permute-start | bytes 196616 | tf_op jit(solution)/shard_map/ppermute | solution.py:58
  8.6 1.7 %collective-permute-done.1.refs_1_.other = bf16[2,128,128]{2,1,0:T(8,128)(2,1)S(1)} collective-permute-done((bf16[2,128,128]{2,1,0:T(8,128)(2,1)S(1)}, bf16[2,128,128]{2,1,0:T(8,128)(2,1)S(1)}, u32[]{:S(2)}, u32[]{:S(2)}) %collective-permute-start.1) | collective-permute-done | bytes 65568 | tf_op jit(solution)/shard_map/ppermute | solution.py:58
  10.3 0.1 collective-permute-start.3
  10.5 1.5 %collective-permute-start.8 = (bf16[2,128,128]{2,1,0:T(8,128)(2,1)S(1)}, bf16[2,128,128]{2,1,0:T(8,128)(2,1)S(1)}, u32[]{:S(2)}, u32[]{:S(2)}) collective-permute-start(bf16[2,128,128]{2,1,0:T(8,128)(2,1)S(1)} %collective-permute-done.1.refs_1_.other), channel_id=1, source_target_pairs={{0,1},{1,0},{2,3},{3,2},{4,5},{5,4},{6,7},{7,6},{8,9},{9,8},{10,11... | collective-permute-start | bytes 196616 | tf_op jit(solution)/shard_map/ppermute | solution.py:58
  12.0 0.6 %collective-permute-done.refs_3_ = bf16[2,128,128]{2,1,0:T(8,128)(2,1)S(1)} collective-permute-done((bf16[2,128,128]{2,1,0:T(8,128)(2,1)S(1)}, bf16[2,128,128]{2,1,0:T(8,128)(2,1)S(1)}, u32[]{:S(2)}, u32[]{:S(2)}) %collective-permute-start) | collective-permute-done | bytes 65568 | tf_op jit(solution)/shard_map/ppermute | solution.py:58
  12.6 1.2 %collective-permute-start.4 = (bf16[2,128,128]{2,1,0:T(8,128)(2,1)S(1)}, bf16[2,128,128]{2,1,0:T(8,128)(2,1)S(1)}, u32[]{:S(2)}, u32[]{:S(2)}) collective-permute-start(bf16[2,128,128]{2,1,0:T(8,128)(2,1)S(1)} %collective-permute-done.1.refs_1_.other), channel_id=1, source_target_pairs={{0,3},{1,2},{2,1},{3,0},{4,7},{5,6},{6,5},{7,4},{8,11},{9,10},{10,... | collective-permute-start | bytes 196616 | tf_op jit(solution)/shard_map/ppermute | solution.py:58
  13.7 0.6 %collective-permute-start.6 = (bf16[2,128,128]{2,1,0:T(8,128)(2,1)S(1)}, bf16[2,128,128]{2,1,0:T(8,128)(2,1)S(1)}, u32[]{:S(2)}, u32[]{:S(2)}) collective-permute-start(bf16[2,128,128]{2,1,0:T(8,128)(2,1)S(1)} %collective-permute-done.refs_3_), channel_id=1, source_target_pairs={{0,3},{1,2},{2,1},{3,0},{4,7},{5,6},{6,5},{7,4},{8,11},{9,10},{10,... | collective-permute-start | bytes 196616 | tf_op jit(solution)/shard_map/ppermute | solution.py:58
  14.4 1.2 %ready.1 = (bf16[2,128,128]{2,1,0:T(8,128)(2,1)S(1)}, f32[96,128,128]{2,1,0:T(8,128)S(1)}, f32[96,128,128]{2,1,0:T(8,128)S(1)}, bf16[16,128,128]{2,1,0:T(8,128)(...) custom-call(s32[1,16]{1,0:T(1,128)S(1)} %bitcast.4, ...), custom_call_target="tpu_custom_call", output_to_operand_aliasing={{0}: (6, {})} | custom-call | bytes 16654592 | tf_op jit(solution)/shard_map/ready/pallas_call | solution.py:350
  15.6 0.1 collective-permute-start.10
  15.7 0.0 collective-permute-done.3.refs_0_.refs_4_
  15.8 0.5 %collective-permute-start.13 = (bf16[2,128,128]{2,1,0:T(8,128)(2,1)S(1)}, bf16[2,128,128]{2,1,0:T(8,128)(2,1)S(1)}, u32[]{:S(2)}, u32[]{:S(2)}) collective-permute-start(bf16[2,128,128]{2,1,0:T(8,128)(2,1)S(1)} %collective-permute-done.5.refs_2_.refs_6_), channel_id=1, source_target_pairs={{0,1},{1,0},{2,3},{3,2},{4,5},{5,4},{6,7},{7,6},{8,9},{9,8},{10,11... | collective-permute-start | bytes 196616 | tf_op jit(solution)/shard_map/ppermute | solution.py:58
  16.2 0.1 collective-permute-start.11
  16.3 0.0 collective-permute-done.4.refs_1_.refs_5_
  16.3 0.4 %collective-permute-start.12 = (bf16[2,128,128]{2,1,0:T(8,128)(2,1)S(1)}, bf16[2,128,128]{2,1,0:T(8,128)(2,1)S(1)}, u32[]{:S(2)}, u32[]{:S(2)}) collective-permute-start(bf16[2,128,128]{2,1,0:T(8,128)(2,1)S(1)} %collective-permute-done.4.refs_1_.refs_5_), channel_id=1, source_target_pairs={{0,1},{1,0},{2,3},{3,2},{4,5},{5,4},{6,7},{7,6},{8,9},{9,8},{10,11... | collective-permute-start | bytes 196616 | tf_op jit(solution)/shard_map/ppermute | solution.py:58
  16.7 1.3 %collective-permute-done.6.refs_3_.refs_7_ = bf16[2,128,128]{2,1,0:T(8,128)(2,1)S(1)} collective-permute-done((bf16[2,128,128]{2,1,0:T(8,128)(2,1)S(1)}, bf16[2,128,128]{2,1,0:T(8,128)(2,1)S(1)}, u32[]{:S(2)}, u32[]{:S(2)}) %collective-permute-start.6) | collective-permute-done | bytes 65568 | tf_op jit(solution)/shard_map/ppermute | solution.py:58
  18.0 0.4 %collective-permute-start.14 = (bf16[2,128,128]{2,1,0:T(8,128)(2,1)S(1)}, bf16[2,128,128]{2,1,0:T(8,128)(2,1)S(1)}, u32[]{:S(2)}, u32[]{:S(2)}) collective-permute-start(bf16[2,128,128]{2,1,0:T(8,128)(2,1)S(1)} %collective-permute-done.6.refs_3_.refs_7_), channel_id=1, source_target_pairs={{0,1},{1,0},{2,3},{3,2},{4,5},{5,4},{6,7},{7,6},{8,9},{9,8},{10,11... | collective-permute-start | bytes 196616 | tf_op jit(solution)/shard_map/ppermute | solution.py:58
  18.4 0.5 %more.1 = (f32[96,128,128]{2,1,0:T(8,128)S(1)}, f32[96,128,128]{2,1,0:T(8,128)S(1)}) custom-call(s32[8,128]{1,0:T(8,128)S(1)} %get-tuple-element.36.table, f32[96,128,128]{2,1,0:T(8,128)S(1)} %get-tuple-element.37.hidden_in, f32[96,128,128]{2,1,0:T(8,128)S(1)} %get-tuple-element.38.agrad_in, ...), custom_call_target="tpu_custom_call", output_to_operand_aliasing={{0}: (1, {}), {1}: (2, {})} | custom-call | bytes 28381184 | tf_op jit(solution)/shard_map/more/pallas_call | solution.py:350
  18.9 0.4 %collective-permute-done.14.refs_0_.refs_15_ = bf16[2,128,128]{2,1,0:T(8,128)(2,1)S(1)} collective-permute-done((bf16[2,128,128]{2,1,0:T(8,128)(2,1)S(1)}, bf16[2,128,128]{2,1,0:T(8,128)(2,1)S(1)}, u32[]{:S(2)}, u32[]{:S(2)}) %collective-permute-start.14) | collective-permute-done | bytes 65568 | tf_op jit(solution)/shard_map/ppermute | solution.py:58
  19.3 1.4 %middle.1 = (f32[96,128,128]{2,1,0:T(8,128)S(1)}, f32[96,128,128]{2,1,0:T(8,128)S(1)}, bf16[16,128,128]{2,1,0:T(8,128)(2,1)S(1)}, bf16[16,128,128]{2,1,0:T(8,128...) custom-call(s32[8,128]{1,0:T(8,128)S(1)} %get-tuple-element.36.table, ...), custom_call_target="tpu_custom_call", output_to_operand_aliasing={{0}: (1, {}), {1}: (2, {})} | custom-call | flops 268435456 | bytes 30085120 | tf_op jit(solution)/shard_map/middle/pallas_call | solution.py:350
  20.7 0.4 %collective-permute-start.17 = (bf16[2,2,128,128]{3,2,1,0:T(8,128)(2,1)S(1)}, bf16[2,2,128,128]{3,2,1,0:T(8,128)(2,1)S(1)}, u32[]{:S(2)}, u32[]{:S(2)}) collective-permute-start(bf16[2,2,128,128]{3,2,1,0:T(8,128)(2,1)S(1)} %get-tuple-element.55), channel_id=1, source_target_pairs={{0,1},{1,0},{2,3},{3,2},{4,5},{5,4},{6,7},{7,6},{8,9},{9,8},{10,11... | collective-permute-start | bytes 393224 | tf_op jit(solution)/shard_map/ppermute | solution.py:58
  21.1 0.2 collective-permute-start.20
  21.3 0.4 collective-permute-start.23
  21.7 0.2 collective-permute-start.15
  21.8 0.3 collective-permute-done.17.refs_0_
  22.2 1.0 %collective-permute-start.18 = (bf16[1,2,128,128]{3,2,1,0:T(8,128)(2,1)S(1)}, bf16[1,2,128,128]{3,2,1,0:T(8,128)(2,1)S(1)}, u32[]{:S(2)}, u32[]{:S(2)}) collective-permute-start(bf16[1,2,128,128]{3,2,1,0:T(8,128)(2,1)S(1)} %get-tuple-element.57), channel_id=1, source_target_pairs={{0,3},{1,2},{2,1},{3,0},{4,7},{5,6},{6,5},{7,4},{8,11},{9,10},{10,... | collective-permute-start | bytes 196616 | tf_op jit(solution)/shard_map/ppermute | solution.py:58
  23.2 0.8 %collective-permute-start.21 = (bf16[1,2,128,128]{3,2,1,0:T(8,128)(2,1)S(1)}, bf16[1,2,128,128]{3,2,1,0:T(8,128)(2,1)S(1)}, u32[]{:S(2)}, u32[]{:S(2)}) collective-permute-start(bf16[1,2,128,128]{3,2,1,0:T(8,128)(2,1)S(1)} %get-tuple-element.61), channel_id=1, source_target_pairs={{0,3},{1,2},{2,1},{3,0},{4,7},{5,6},{6,5},{7,4},{8,11},{9,10},{10,... | collective-permute-start | bytes 196616 | tf_op jit(solution)/shard_map/ppermute | solution.py:58
  24.1 1.0 %collective-permute-start.24 = (bf16[1,2,128,128]{3,2,1,0:T(8,128)(2,1)S(1)}, bf16[1,2,128,128]{3,2,1,0:T(8,128)(2,1)S(1)}, u32[]{:S(2)}, u32[]{:S(2)}) collective-permute-start(bf16[1,2,128,128]{3,2,1,0:T(8,128)(2,1)S(1)} %get-tuple-element.65), channel_id=1, source_target_pairs={{0,3},{1,2},{2,1},{3,0},{4,7},{5,6},{6,5},{7,4},{8,11},{9,10},{10,... | collective-permute-start | bytes 196616 | tf_op jit(solution)/shard_map/ppermute | solution.py:58
  25.2 0.8 %collective-permute-start.16 = (bf16[1,2,128,128]{3,2,1,0:T(8,128)(2,1)S(1)}, bf16[1,2,128,128]{3,2,1,0:T(8,128)(2,1)S(1)}, u32[]{:S(2)}, u32[]{:S(2)}) collective-permute-start(bf16[1,2,128,128]{3,2,1,0:T(8,128)(2,1)S(1)} %get-tuple-element.53), channel_id=1, source_target_pairs={{0,3},{1,2},{2,1},{3,0},{4,7},{5,6},{6,5},{7,4},{8,11},{9,10},{10,... | collective-permute-start | bytes 196616 | tf_op jit(solution)/shard_map/ppermute | solution.py:58
  26.0 0.9 %collective-permute-done.18.refs_0_ = bf16[1,2,128,128]{3,2,1,0:T(8,128)(2,1)S(1)} collective-permute-done((bf16[1,2,128,128]{3,2,1,0:T(8,128)(2,1)S(1)}, bf16[1,2,128,128]{3,2,1,0:T(8,128)(2,1)S(1)}, u32[]{:S(2)}, u32[]{:S(2)}) %collective-permute-start.18) | collective-permute-done | bytes 65568 | tf_op jit(solution)/shard_map/ppermute | solution.py:58
  27.0 1.6 %collective-permute-start.19 = (bf16[1,2,128,128]{3,2,1,0:T(8,128)(2,1)S(1)}, bf16[1,2,128,128]{3,2,1,0:T(8,128)(2,1)S(1)}, u32[]{:S(2)}, u32[]{:S(2)}) collective-permute-start(bf16[1,2,128,128]{3,2,1,0:T(8,128)(2,1)S(1)} %fold.9), channel_id=1, source_target_pairs={{0,9},{1,8},{2,11},{3,10},{4,13},{5,12},{6,15},{7,14},{8,1},{9,0},... | collective-permute-start | bytes 196616 | tf_op jit(solution)/shard_map/ppermute | solution.py:58
  28.6 2.1 %collective-permute-start.22 = (bf16[1,2,128,128]{3,2,1,0:T(8,128)(2,1)S(1)}, bf16[1,2,128,128]{3,2,1,0:T(8,128)(2,1)S(1)}, u32[]{:S(2)}, u32[]{:S(2)}) collective-permute-start(bf16[1,2,128,128]{3,2,1,0:T(8,128)(2,1)S(1)} %fold.11), channel_id=1, source_target_pairs={{0,5},{1,4},{2,7},{3,6},{4,1},{5,0},{6,3},{7,2},{8,13},{9,12},{10,... | collective-permute-start | bytes 196616 | tf_op jit(solution)/shard_map/ppermute | solution.py:58
  30.7 2.0 %collective-permute-start.25 = (bf16[1,2,128,128]{3,2,1,0:T(8,128)(2,1)S(1)}, bf16[1,2,128,128]{3,2,1,0:T(8,128)(2,1)S(1)}, u32[]{:S(2)}, u32[]{:S(2)}) collective-permute-start(bf16[1,2,128,128]{3,2,1,0:T(8,128)(2,1)S(1)} %fold.13), channel_id=1, source_target_pairs={{0,13},{1,12},{2,15},{3,14},{4,9},{5,8},{6,11},{7,10},{8,5},{9,4},... | collective-permute-start | bytes 196616 | tf_op jit(solution)/shard_map/ppermute | solution.py:58
  32.6 2.0 %last.1 = (bf16[128,3072]{1,0:T(8,128)(2,1)}, bf16[128,3072]{1,0:T(8,128)(2,1)}) custom-call(s32[8,128]{1,0:T(8,128)S(1)} %get-tuple-element.36.table, bf16[16,128,128]{2,1,0:T(8,128)(2,1)S(1)} %get-tuple-element.46.act, bf16[16,128,128]{2,1,0:T(8,128)(2,1)S(1)} %get-tuple-element.47.hgrad, bf16[2,128,128]{2,1,0:T(8,128)(2,1)S(1)} %begin.1.refs_0_.value, ...), custom_call_target="tpu_custom_call" | custom-call | flops 134217728 | bytes 9965600 | tf_op jit(solution)/shard_map/last/pallas_call | solution.py:350
  34.7 1.5 %collective-permute-done.25.refs_3_ = bf16[1,2,128,128]{3,2,1,0:T(8,128)(2,1)S(1)} collective-permute-done((bf16[1,2,128,128]{3,2,1,0:T(8,128)(2,1)S(1)}, bf16[1,2,128,128]{3,2,1,0:T(8,128)(2,1)S(1)}, u32[]{:S(2)}, u32[]{:S(2)}) %collective-permute-start.25) | collective-permute-done | bytes 65568 | tf_op jit(solution)/shard_map/ppermute | solution.py:58
  36.2 0.7 %close.1 = (f32[1,128,128]{2,1,0:T(8,128)}, f32[1,128,128]{2,1,0:T(8,128)}) custom-call(f32[1,2,128,128]{3,2,1,0:T(8,128)S(1)} %get-tuple-element.52.held, bf16[1,2,128,128]{3,2,1,0:T(8,128)(2,1)S(1)} %collective-permute-done.16.refs_0_, bf16[1,2,128,128]{3,2,1,0:T(8,128)(2,1)S(1)} %collective-permute-done.19.refs_1_, ...), custom_call_target="tpu_custom_call" | custom-call | bytes 524288 | tf_op jit(solution)/shard_map/close/pallas_call | solution.py:350
  (31 shorter events, 0.2 us)
Async XLA Ops:
  1.4 12.9 %copy-start = (bf16[128,3072]{1,0:T(8,128)(2,1)S(1)}, bf16[128,3072]{1,0:T(8,128)(2,1)}, u32[]{:S(2)}) copy-start(bf16[128,3072]{1,0:T(8,128)(2,1)} %tokens.1) | copy-start | bytes 2359300
  1.4 12.9 %copy-start.1 = (bf16[128,3072]{1,0:T(8,128)(2,1)S(1)}, bf16[128,3072]{1,0:T(8,128)(2,1)}, u32[]{:S(2)}) copy-start(bf16[128,3072]{1,0:T(8,128)(2,1)} %cot.1) | copy-start | bytes 2359300
  1.5 12.9 %copy-start.2 = (s32[16]{0:T(128)S(1)}, s32[16]{0:T(128)}, u32[]{:S(2)}) copy-start(s32[16]{0:T(128)} %param.11) | copy-start | bytes 196
  1.5 12.9 %copy-start.3 = (s32[16]{0:T(128)S(1)}, s32[16]{0:T(128)}, u32[]{:S(2)}) copy-start(s32[16]{0:T(128)} %param.12) | copy-start | bytes 196
  1.5 12.9 %copy-start.4 = (s32[16]{0:T(128)S(1)}, s32[16]{0:T(128)}, u32[]{:S(2)}) copy-start(s32[16]{0:T(128)} %param.14) | copy-start | bytes 196
  1.5 12.9 %copy-start.5 = (s32[16]{0:T(128)S(1)}, s32[16]{0:T(128)}, u32[]{:S(2)}) copy-start(s32[16]{0:T(128)} %param.15) | copy-start | bytes 196
  1.5 5.5 %collective-permute-start.2 = (bf16[2,128,128]{2,1,0:T(8,128)(2,1)S(1)}, bf16[2,128,128]{2,1,0:T(8,128)(2,1)S(1)}, u32[]{:S(2)}, u32[]{:S(2)}) collective-permute-start(bf16[2,128,128]{2,1,0:T(8,128)(2,1)S(1)} %begin.1.refs_0_.value), channel_id=1, source_target_pairs={{0,5},{1,4},{2,7},{3,6},{4,1},{5,0},{6,3},{7,2},{8,13},{9,12},{10,... | collective-permute-start | bytes 196616 | tf_op jit(solution)/shard_map/ppermute | solution.py:58
  4.3 6.1 %collective-permute-start.1 = (bf16[2,128,128]{2,1,0:T(8,128)(2,1)S(1)}, bf16[2,128,128]{2,1,0:T(8,128)(2,1)S(1)}, u32[]{:S(2)}, u32[]{:S(2)}) collective-permute-start(bf16[2,128,128]{2,1,0:T(8,128)(2,1)S(1)} %begin.1.refs_0_.value), channel_id=1, source_target_pairs={{0,9},{1,8},{2,11},{3,10},{4,13},{5,12},{6,15},{7,14},{8,1},{9,0},... | collective-permute-start | bytes 196616 | tf_op jit(solution)/shard_map/ppermute | solution.py:58
  6.3 4.2 %collective-permute-start.7 = (bf16[2,128,128]{2,1,0:T(8,128)(2,1)S(1)}, bf16[2,128,128]{2,1,0:T(8,128)(2,1)S(1)}, u32[]{:S(2)}, u32[]{:S(2)}) collective-permute-start(bf16[2,128,128]{2,1,0:T(8,128)(2,1)S(1)} %begin.1.refs_0_.value), channel_id=1, source_target_pairs={{0,1},{1,0},{2,3},{3,2},{4,5},{5,4},{6,7},{7,6},{8,9},{9,8},{10,11... | collective-permute-start | bytes 196616 | tf_op jit(solution)/shard_map/ppermute | solution.py:58
  7.0 5.6 %collective-permute-start = (bf16[2,128,128]{2,1,0:T(8,128)(2,1)S(1)}, bf16[2,128,128]{2,1,0:T(8,128)(2,1)S(1)}, u32[]{:S(2)}, u32[]{:S(2)}) collective-permute-start(bf16[2,128,128]{2,1,0:T(8,128)(2,1)S(1)} %begin.1.refs_0_.value), channel_id=1, source_target_pairs={{0,13},{1,12},{2,15},{3,14},{4,9},{5,8},{6,11},{7,10},{8,5},{9,4},... | collective-permute-start | bytes 196616 | tf_op jit(solution)/shard_map/ppermute | solution.py:58
  7.0 6.8 %collective-permute-start.9 = (bf16[2,128,128]{2,1,0:T(8,128)(2,1)S(1)}, bf16[2,128,128]{2,1,0:T(8,128)(2,1)S(1)}, u32[]{:S(2)}, u32[]{:S(2)}) collective-permute-start(bf16[2,128,128]{2,1,0:T(8,128)(2,1)S(1)} %collective-permute-done.2.refs_2_), channel_id=1, source_target_pairs={{0,1},{1,0},{2,3},{3,2},{4,5},{5,4},{6,7},{7,6},{8,9},{9,8},{10,11... | collective-permute-start | bytes 196616 | tf_op jit(solution)/shard_map/ppermute | solution.py:58
  7.0 8.6 %collective-permute-start.5 = (bf16[2,128,128]{2,1,0:T(8,128)(2,1)S(1)}, bf16[2,128,128]{2,1,0:T(8,128)(2,1)S(1)}, u32[]{:S(2)}, u32[]{:S(2)}) collective-permute-start(bf16[2,128,128]{2,1,0:T(8,128)(2,1)S(1)} %collective-permute-done.2.refs_2_), channel_id=1, source_target_pairs={{0,3},{1,2},{2,1},{3,0},{4,7},{5,6},{6,5},{7,4},{8,11},{9,10},{10,... | collective-permute-start | bytes 196616 | tf_op jit(solution)/shard_map/ppermute | solution.py:58
  10.3 5.4 %collective-permute-start.3 = (bf16[2,128,128]{2,1,0:T(8,128)(2,1)S(1)}, bf16[2,128,128]{2,1,0:T(8,128)(2,1)S(1)}, u32[]{:S(2)}, u32[]{:S(2)}) collective-permute-start(bf16[2,128,128]{2,1,0:T(8,128)(2,1)S(1)} %after.1), channel_id=1, source_target_pairs={{0,3},{1,2},{2,1},{3,0},{4,7},{5,6},{6,5},{7,4},{8,11},{9,10},{10,... | collective-permute-start | bytes 196616 | tf_op jit(solution)/shard_map/ppermute | solution.py:58
  10.5 5.7 %collective-permute-start.8 = (bf16[2,128,128]{2,1,0:T(8,128)(2,1)S(1)}, bf16[2,128,128]{2,1,0:T(8,128)(2,1)S(1)}, u32[]{:S(2)}, u32[]{:S(2)}) collective-permute-start(bf16[2,128,128]{2,1,0:T(8,128)(2,1)S(1)} %collective-permute-done.1.refs_1_.other), channel_id=1, source_target_pairs={{0,1},{1,0},{2,3},{3,2},{4,5},{5,4},{6,7},{7,6},{8,9},{9,8},{10,11... | collective-permute-start | bytes 196616 | tf_op jit(solution)/shard_map/ppermute | solution.py:58
  12.6 3.7 %collective-permute-start.4 = (bf16[2,128,128]{2,1,0:T(8,128)(2,1)S(1)}, bf16[2,128,128]{2,1,0:T(8,128)(2,1)S(1)}, u32[]{:S(2)}, u32[]{:S(2)}) collective-permute-start(bf16[2,128,128]{2,1,0:T(8,128)(2,1)S(1)} %collective-permute-done.1.refs_1_.other), channel_id=1, source_target_pairs={{0,3},{1,2},{2,1},{3,0},{4,7},{5,6},{6,5},{7,4},{8,11},{9,10},{10,... | collective-permute-start | bytes 196616 | tf_op jit(solution)/shard_map/ppermute | solution.py:58
  13.7 4.3 %collective-permute-start.6 = (bf16[2,128,128]{2,1,0:T(8,128)(2,1)S(1)}, bf16[2,128,128]{2,1,0:T(8,128)(2,1)S(1)}, u32[]{:S(2)}, u32[]{:S(2)}) collective-permute-start(bf16[2,128,128]{2,1,0:T(8,128)(2,1)S(1)} %collective-permute-done.refs_3_), channel_id=1, source_target_pairs={{0,3},{1,2},{2,1},{3,0},{4,7},{5,6},{6,5},{7,4},{8,11},{9,10},{10,... | collective-permute-start | bytes 196616 | tf_op jit(solution)/shard_map/ppermute | solution.py:58
  15.6 2.7 %collective-permute-start.10 = (bf16[2,128,128]{2,1,0:T(8,128)(2,1)S(1)}, bf16[2,128,128]{2,1,0:T(8,128)(2,1)S(1)}, u32[]{:S(2)}, u32[]{:S(2)}) collective-permute-start(bf16[2,128,128]{2,1,0:T(8,128)(2,1)S(1)} %get-tuple-element.41), channel_id=1, source_target_pairs={{0,1},{1,0},{2,3},{3,2},{4,5},{5,4},{6,7},{7,6},{8,9},{9,8},{10,11... | collective-permute-start | bytes 196616 | tf_op jit(solution)/shard_map/ppermute | solution.py:58
  15.8 2.6 %collective-permute-start.13 = (bf16[2,128,128]{2,1,0:T(8,128)(2,1)S(1)}, bf16[2,128,128]{2,1,0:T(8,128)(2,1)S(1)}, u32[]{:S(2)}, u32[]{:S(2)}) collective-permute-start(bf16[2,128,128]{2,1,0:T(8,128)(2,1)S(1)} %collective-permute-done.5.refs_2_.refs_6_), channel_id=1, source_target_pairs={{0,1},{1,0},{2,3},{3,2},{4,5},{5,4},{6,7},{7,6},{8,9},{9,8},{10,11... | collective-permute-start | bytes 196616 | tf_op jit(solution)/shard_map/ppermute | solution.py:58
  16.2 2.2 %collective-permute-start.11 = (bf16[2,128,128]{2,1,0:T(8,128)(2,1)S(1)}, bf16[2,128,128]{2,1,0:T(8,128)(2,1)S(1)}, u32[]{:S(2)}, u32[]{:S(2)}) collective-permute-start(bf16[2,128,128]{2,1,0:T(8,128)(2,1)S(1)} %collective-permute-done.3.refs_0_.refs_4_), channel_id=1, source_target_pairs={{0,1},{1,0},{2,3},{3,2},{4,5},{5,4},{6,7},{7,6},{8,9},{9,8},{10,11... | collective-permute-start | bytes 196616 | tf_op jit(solution)/shard_map/ppermute | solution.py:58
  16.3 2.1 %collective-permute-start.12 = (bf16[2,128,128]{2,1,0:T(8,128)(2,1)S(1)}, bf16[2,128,128]{2,1,0:T(8,128)(2,1)S(1)}, u32[]{:S(2)}, u32[]{:S(2)}) collective-permute-start(bf16[2,128,128]{2,1,0:T(8,128)(2,1)S(1)} %collective-permute-done.4.refs_1_.refs_5_), channel_id=1, source_target_pairs={{0,1},{1,0},{2,3},{3,2},{4,5},{5,4},{6,7},{7,6},{8,9},{9,8},{10,11... | collective-permute-start | bytes 196616 | tf_op jit(solution)/shard_map/ppermute | solution.py:58
  18.0 1.3 %collective-permute-start.14 = (bf16[2,128,128]{2,1,0:T(8,128)(2,1)S(1)}, bf16[2,128,128]{2,1,0:T(8,128)(2,1)S(1)}, u32[]{:S(2)}, u32[]{:S(2)}) collective-permute-start(bf16[2,128,128]{2,1,0:T(8,128)(2,1)S(1)} %collective-permute-done.6.refs_3_.refs_7_), channel_id=1, source_target_pairs={{0,1},{1,0},{2,3},{3,2},{4,5},{5,4},{6,7},{7,6},{8,9},{9,8},{10,11... | collective-permute-start | bytes 196616 | tf_op jit(solution)/shard_map/ppermute | solution.py:58
  20.7 1.4 %collective-permute-start.17 = (bf16[2,2,128,128]{3,2,1,0:T(8,128)(2,1)S(1)}, bf16[2,2,128,128]{3,2,1,0:T(8,128)(2,1)S(1)}, u32[]{:S(2)}, u32[]{:S(2)}) collective-permute-start(bf16[2,2,128,128]{3,2,1,0:T(8,128)(2,1)S(1)} %get-tuple-element.55), channel_id=1, source_target_pairs={{0,1},{1,0},{2,3},{3,2},{4,5},{5,4},{6,7},{7,6},{8,9},{9,8},{10,11... | collective-permute-start | bytes 393224 | tf_op jit(solution)/shard_map/ppermute | solution.py:58
  21.1 2.1 %collective-permute-start.20 = (bf16[2,2,128,128]{3,2,1,0:T(8,128)(2,1)S(1)}, bf16[2,2,128,128]{3,2,1,0:T(8,128)(2,1)S(1)}, u32[]{:S(2)}, u32[]{:S(2)}) collective-permute-start(bf16[2,2,128,128]{3,2,1,0:T(8,128)(2,1)S(1)} %get-tuple-element.59), channel_id=1, source_target_pairs={{0,1},{1,0},{2,3},{3,2},{4,5},{5,4},{6,7},{7,6},{8,9},{9,8},{10,11... | collective-permute-start | bytes 393224 | tf_op jit(solution)/shard_map/ppermute | solution.py:58
  21.3 2.8 %collective-permute-start.23 = (bf16[2,2,128,128]{3,2,1,0:T(8,128)(2,1)S(1)}, bf16[2,2,128,128]{3,2,1,0:T(8,128)(2,1)S(1)}, u32[]{:S(2)}, u32[]{:S(2)}) collective-permute-start(bf16[2,2,128,128]{3,2,1,0:T(8,128)(2,1)S(1)} %get-tuple-element.63), channel_id=1, source_target_pairs={{0,1},{1,0},{2,3},{3,2},{4,5},{5,4},{6,7},{7,6},{8,9},{9,8},{10,11... | collective-permute-start | bytes 393224 | tf_op jit(solution)/shard_map/ppermute | solution.py:58
  21.7 3.5 %collective-permute-start.15 = (bf16[2,2,128,128]{3,2,1,0:T(8,128)(2,1)S(1)}, bf16[2,2,128,128]{3,2,1,0:T(8,128)(2,1)S(1)}, u32[]{:S(2)}, u32[]{:S(2)}) collective-permute-start(bf16[2,2,128,128]{3,2,1,0:T(8,128)(2,1)S(1)} %get-tuple-element.51), channel_id=1, source_target_pairs={{0,1},{1,0},{2,3},{3,2},{4,5},{5,4},{6,7},{7,6},{8,9},{9,8},{10,11... | collective-permute-start | bytes 393224 | tf_op jit(solution)/shard_map/ppermute | solution.py:58
  22.2 4.8 %collective-permute-start.18 = (bf16[1,2,128,128]{3,2,1,0:T(8,128)(2,1)S(1)}, bf16[1,2,128,128]{3,2,1,0:T(8,128)(2,1)S(1)}, u32[]{:S(2)}, u32[]{:S(2)}) collective-permute-start(bf16[1,2,128,128]{3,2,1,0:T(8,128)(2,1)S(1)} %get-tuple-element.57), channel_id=1, source_target_pairs={{0,3},{1,2},{2,1},{3,0},{4,7},{5,6},{6,5},{7,4},{8,11},{9,10},{10,... | collective-permute-start | bytes 196616 | tf_op jit(solution)/shard_map/ppermute | solution.py:58
  23.2 5.3 %collective-permute-start.21 = (bf16[1,2,128,128]{3,2,1,0:T(8,128)(2,1)S(1)}, bf16[1,2,128,128]{3,2,1,0:T(8,128)(2,1)S(1)}, u32[]{:S(2)}, u32[]{:S(2)}) collective-permute-start(bf16[1,2,128,128]{3,2,1,0:T(8,128)(2,1)S(1)} %get-tuple-element.61), channel_id=1, source_target_pairs={{0,3},{1,2},{2,1},{3,0},{4,7},{5,6},{6,5},{7,4},{8,11},{9,10},{10,... | collective-permute-start | bytes 196616 | tf_op jit(solution)/shard_map/ppermute | solution.py:58
  24.1 6.5 %collective-permute-start.24 = (bf16[1,2,128,128]{3,2,1,0:T(8,128)(2,1)S(1)}, bf16[1,2,128,128]{3,2,1,0:T(8,128)(2,1)S(1)}, u32[]{:S(2)}, u32[]{:S(2)}) collective-permute-start(bf16[1,2,128,128]{3,2,1,0:T(8,128)(2,1)S(1)} %get-tuple-element.65), channel_id=1, source_target_pairs={{0,3},{1,2},{2,1},{3,0},{4,7},{5,6},{6,5},{7,4},{8,11},{9,10},{10,... | collective-permute-start | bytes 196616 | tf_op jit(solution)/shard_map/ppermute | solution.py:58
  25.2 9.4 %collective-permute-start.16 = (bf16[1,2,128,128]{3,2,1,0:T(8,128)(2,1)S(1)}, bf16[1,2,128,128]{3,2,1,0:T(8,128)(2,1)S(1)}, u32[]{:S(2)}, u32[]{:S(2)}) collective-permute-start(bf16[1,2,128,128]{3,2,1,0:T(8,128)(2,1)S(1)} %get-tuple-element.53), channel_id=1, source_target_pairs={{0,3},{1,2},{2,1},{3,0},{4,7},{5,6},{6,5},{7,4},{8,11},{9,10},{10,... | collective-permute-start | bytes 196616 | tf_op jit(solution)/shard_map/ppermute | solution.py:58
  27.0 7.7 %collective-permute-start.19 = (bf16[1,2,128,128]{3,2,1,0:T(8,128)(2,1)S(1)}, bf16[1,2,128,128]{3,2,1,0:T(8,128)(2,1)S(1)}, u32[]{:S(2)}, u32[]{:S(2)}) collective-permute-start(bf16[1,2,128,128]{3,2,1,0:T(8,128)(2,1)S(1)} %fold.9), channel_id=1, source_target_pairs={{0,9},{1,8},{2,11},{3,10},{4,13},{5,12},{6,15},{7,14},{8,1},{9,0},... | collective-permute-start | bytes 196616 | tf_op jit(solution)/shard_map/ppermute | solution.py:58
  28.6 6.1 %collective-permute-start.22 = (bf16[1,2,128,128]{3,2,1,0:T(8,128)(2,1)S(1)}, bf16[1,2,128,128]{3,2,1,0:T(8,128)(2,1)S(1)}, u32[]{:S(2)}, u32[]{:S(2)}) collective-permute-start(bf16[1,2,128,128]{3,2,1,0:T(8,128)(2,1)S(1)} %fold.11), channel_id=1, source_target_pairs={{0,5},{1,4},{2,7},{3,6},{4,1},{5,0},{6,3},{7,2},{8,13},{9,12},{10,... | collective-permute-start | bytes 196616 | tf_op jit(solution)/shard_map/ppermute | solution.py:58
  30.7 5.6 %collective-permute-start.25 = (bf16[1,2,128,128]{3,2,1,0:T(8,128)(2,1)S(1)}, bf16[1,2,128,128]{3,2,1,0:T(8,128)(2,1)S(1)}, u32[]{:S(2)}, u32[]{:S(2)}) collective-permute-start(bf16[1,2,128,128]{3,2,1,0:T(8,128)(2,1)S(1)} %fold.13), channel_id=1, source_target_pairs={{0,13},{1,12},{2,15},{3,14},{4,9},{5,8},{6,11},{7,10},{8,5},{9,4},... | collective-permute-start | bytes 196616 | tf_op jit(solution)/shard_map/ppermute | solution.py:58
